TPU v7x, 1024 devices: a whole 4x8x16 slice. The times are simulated.
1024 devices in a mesh: seq: 64 (over z, x_hi, core), exp: 16 (over y, x_lo).
Axes of the slice: x: 4 (x_hi: 2, x_lo: 2; x = x_hi * 2 + x_lo), y: 8, z: 16, core: 2. Of those that a mesh axis runs over, the one named last changes fastest.
Arguments:
- tokens: bfloat16 [32768, 2048], P('seq'), as said below
- phi: bfloat16 [2048, 1024], P('seq', 'exp'), as said below
- expert_out: bfloat16 [1024, 2048], P('exp'), may hold values from -6 to 6
- slot_in_grad: bfloat16 [1024, 2048], P('exp'), may hold values from -6 to 6
- out_grad: bfloat16 [32768, 2048], P('seq'), may hold values from -6 to 6
Outputs:
- token_grad: bfloat16 [32768, 2048], P('seq', 'exp')
- phi_grad: float32 [2048, 1024], P('seq', 'exp')
- slot_grad: bfloat16 [1024, 2048], P('exp', 'seq')
Inputs may be any that keep to these rules, and one draw needn't show every extreme that they name: `tokens`: finite token features. `phi`: entries of order 2048 ** -0.5.
All inputs are finite; a program needn't handle non-finite values.
Results may differ from a plain program's by a relative error of at most 0.02.
Values may be sent and summed in bfloat16 or wider, within the bound.
No kernel may reach another device: no remote copies, remote signals or barrier semaphores. Data moves between devices by JAX's collectives and lax.ppermute only.
A program may use at most 32 MiB of HBM per device.

v0:
```python
import jax
import jax.numpy as jnp
from jax import lax
from jax.sharding import PartitionSpec as P


def per_device(tokens, phi, expert_out, slot_in_grad, out_grad):
    phi_full = lax.all_gather(phi, "seq", axis=0, tiled=True)
    logits = jnp.dot(tokens, phi_full, preferred_element_type=jnp.float32)
    local_col = jnp.max(logits, axis=0)
    local_row = jnp.max(logits, axis=1)
    col_peak = lax.pmax(local_col, "seq")
    row_peak = lax.pmax(local_row, "exp")
    dexp = jnp.exp(logits - col_peak[None, :])
    cexp = jnp.exp(logits - row_peak[:, None])
    col_total = lax.psum(jnp.sum(dexp, axis=0), "seq")
    row_total = lax.psum(jnp.sum(cexp, axis=1), "exp")
    dispatch = dexp / col_total[None, :]
    combine = cexp / row_total[:, None]
    dispatch_b = dispatch.astype(jnp.bfloat16)
    combine_b = combine.astype(jnp.bfloat16)
    slot_term = lax.dot_general(
        combine_b, out_grad, (((0,), (0,)), ((), ())), preferred_element_type=jnp.float32
    )
    slot_grad = lax.psum_scatter(slot_term, "seq", scatter_dimension=1, tiled=True).astype(
        jnp.bfloat16
    )
    comb_grad = lax.dot_general(
        out_grad, expert_out, (((1,), (1,)), ((), ())), preferred_element_type=jnp.float32
    )
    row_dot = lax.psum(jnp.sum(combine * comb_grad, axis=1), "exp")
    disp_grad = lax.dot_general(
        tokens, slot_in_grad, (((1,), (1,)), ((), ())), preferred_element_type=jnp.float32
    )
    col_dot = lax.psum(jnp.sum(dispatch * disp_grad, axis=0), "seq")
    logit_grad = (
        combine * (comb_grad - row_dot[:, None]) + dispatch * (disp_grad - col_dot[None, :])
    ).astype(jnp.bfloat16)
    phi_grad = lax.psum_scatter(
        lax.dot_general(
            tokens, logit_grad, (((0,), (0,)), ((), ())), preferred_element_type=jnp.float32
        ),
        "seq",
        scatter_dimension=0,
        tiled=True,
    )
    partial_sum = jnp.dot(dispatch_b, slot_in_grad, preferred_element_type=jnp.float32)
    partial_sum = partial_sum + lax.dot_general(
        logit_grad, phi_full, (((1,), (1,)), ((), ())), preferred_element_type=jnp.float32
    )
    token_grad = lax.psum_scatter(
        partial_sum.astype(jnp.bfloat16), "exp", scatter_dimension=1, tiled=True
    )
    return (token_grad, phi_grad, slot_grad)


def solution(mesh):
    return jax.shard_map(
        per_device,
        mesh=mesh,
        in_specs=(P("seq", None), P("seq", "exp"), P("exp", None), P("exp", None), P("seq", None)),
        out_specs=(P("seq", "exp"), P("seq", "exp"), P("exp", "seq")),
        check_vma=False,
    )
```

profile of v0, /device:TPU:1, one launch (start us, length us, event | category | flops | bytes accessed | tf_op | source)
XLA Modules:
  0.0 891.7 jit_solution(18249879928579774905)
XLA Ops:
  7.2 0.0 copy-start
  7.2 0.0 reduce-scatter.8.cloned.1.call-start
  7.2 93.2 %all_gather.3 = bf16[2048,64]{1,0:T(8,128)(2,1)S(1)} all-gather(bf16[32,64]{1,0:T(8,128)(2,1)} %param.6), channel_id=1, replica_groups=mesh['seq'=64,'exp'=16] {'seq'}, dimensions={0}, use_global_device_ids=true | all-gather | bytes 266240 | tf_op jit(solution)/shard_map/all_gather | solution.py:8
  100.5 0.0 copy-done
  100.5 0.9 fusion.9
  101.3 27.0 %pmax.15 = f32[512]{0:T(512)S(1)} all-reduce(f32[512]{0:T(512)S(1)} %get-tuple-element.13), channel_id=1, replica_groups=mesh['seq'=64,'exp'=16] {'exp'}, use_global_device_ids=true, to_apply=%region_5.0 | all-reduce | flops 512 | bytes 4096 | tf_op jit(solution)/shard_map/pmax | solution.py:13
  128.3 135.3 %pmax.14 = f32[64]{0:T(128)S(1)} all-reduce(f32[64]{0:T(128)S(1)} %get-tuple-element.14), channel_id=1, replica_groups=mesh['seq'=64,'exp'=16] {'seq'}, use_global_device_ids=true, to_apply=%region_1.0 | all-reduce | flops 64 | bytes 512 | tf_op jit(solution)/shard_map/pmax | solution.py:12
  263.6 0.2 fusion.3
  263.8 23.7 %psum.29 = f32[512]{0:T(512)S(1)} all-reduce(f32[512]{0:T(512)S(1)} %get-tuple-element.11), channel_id=1, replica_groups=mesh['seq'=64,'exp'=16] {'exp'}, use_global_device_ids=true, to_apply=%region_7.0 | all-reduce | flops 512 | bytes 4096 | tf_op jit(solution)/shard_map/psum | solution.py:17
  287.5 0.0 copy-start.1
  287.5 3.5 fusion.4
  291.0 0.0 reduce-scatter.8.cloned.1.call-update
  291.1 0.0 reduce-scatter.10.cloned.1.call-start
  291.1 0.0 copy-done.1
  291.1 0.8 fusion.11
  291.9 135.7 %psum.28 = f32[64]{0:T(128)S(1)} all-reduce(f32[64]{0:T(128)S(1)} %get-tuple-element.12), channel_id=1, replica_groups=mesh['seq'=64,'exp'=16] {'seq'}, use_global_device_ids=true, to_apply=%region_3.0 | all-reduce | flops 64 | bytes 512 | tf_op jit(solution)/shard_map/psum | solution.py:16
  427.6 2.5 multiply_reduce_fusion.1
  430.1 128.8 %psum.31 = f32[64]{0:T(128)S(1)} all-reduce(f32[64]{0:T(128)S(1)} %get-tuple-element.10), channel_id=1, replica_groups=mesh['seq'=64,'exp'=16] {'seq'}, use_global_device_ids=true, to_apply=%region_11.0 | all-reduce | flops 64 | bytes 512 | tf_op jit(solution)/shard_map/psum | solution.py:35
  558.9 25.6 %psum.30 = f32[512]{0:T(512)S(1)} all-reduce(f32[512]{0:T(512)S(1)} %get-tuple-element.9), channel_id=1, replica_groups=mesh['seq'=64,'exp'=16] {'exp'}, use_global_device_ids=true, to_apply=%region_9.0 | all-reduce | flops 512 | bytes 4096 | tf_op jit(solution)/shard_map/psum | solution.py:31
  584.5 0.9 fusion.10
  585.4 2.1 add_convert_fusion
  587.5 3.9 copy.10
  591.4 0.0 reduce-scatter.10.cloned.1.call-update
  591.4 0.0 reduce-scatter.12.cloned.1.call-start
  591.5 0.5 convolution_bitcast_fusion
  592.0 1.3 copy.12
  593.3 0.0 reduce-scatter.12.cloned.1.call-update
  593.4 0.0 reduce-scatter.8.cloned.1.call-done
  593.4 1.3 convert_element_type.19
  594.7 63.6 %reduce-scatter.10.cloned.1.call-done = bf16[128,512]{1,0:T(8,128)(2,1)} async-done(((bf16[2048,512]{1,0:T(8,128)(2,1)}), bf16[128,512]{1,0:T(8,128)(2,1)}) %reduce-scatter.10.cloned.1.call-update) | async-done | bytes 131088
  658.3 1.7 copy.11
  660.0 225.2 %reduce-scatter.12.cloned.1.call-done = f32[32,64]{1,0:T(8,128)} async-done(((f32[2048,64]{1,0:T(8,128)}), f32[32,64]{1,0:T(8,128)}) %reduce-scatter.12.cloned.1.call-update) | async-done | bytes 8208
Async XLA Ops:
  7.2 93.3 %copy-start = (bf16[512,2048]{1,0:T(8,128)(2,1)S(1)}, bf16[512,2048]{1,0:T(8,128)(2,1)}, u32[]{:S(2)}) copy-start(bf16[512,2048]{1,0:T(8,128)(2,1)} %param.5) | copy-start | bytes 6291460
  7.2 586.2 %reduce-scatter.8.cloned.1.call-start = ((), (), s32[]{:S(2)}) async-start(), calls=%async_computation.3 | async-start | bytes 1064960 | tf_op jit(solution)/shard_map/reduce_scatter | solution.py:25
  287.5 3.6 copy-start.1
  291.1 367.2 %reduce-scatter.10.cloned.1.call-start = ((), (), s32[]{:S(2)}) async-start(), calls=%async_computation.4 | async-start | bytes 2228224
  591.4 293.7 %reduce-scatter.12.cloned.1.call-start = ((), (), s32[]{:S(2)}) async-start(), calls=%async_computation.5 | async-start | bytes 1064960
Sparse Core Ops, SparseCore 0:
  291.2 205.6 reduce-scatter.7
  591.5 66.7 reduce-scatter.9
  665.6 219.4 reduce-scatter.11
where the time goes:
time: 903 us; the launch traced here: 892 us
  blocking collectives  569 us (63%)
  waiting for transfers between devices  289 us (32%)
  between operations  13.8 us (2%)
  matrix products  11.2 us (1%)
    unnamed x5, waiting for transfers between devices  289 us
    psum x1, blocking collectives, per_device(): col_total = lax.psum(jnp.sum(dexp, axis=0), 'seq')  136 us
    pmax x1, blocking collectives, per_device(): col_peak = lax.pmax(local_col, 'seq')  135 us
    psum x1, blocking collectives, per_device(): col_dot = lax.psum(jnp.sum(dispatch * disp_grad, axis=0), 'seq')  129 us
    all_gather x1, blocking collectives, per_device(): phi_full = lax.all_gather(phi, 'seq', axis=0, tiled=True)  93.2 us
    pmax x1, blocking collectives, per_device(): row_peak = lax.pmax(local_row, 'exp')  27 us
    psum x1, blocking collectives, per_device(): row_dot = lax.psum(jnp.sum(combine * comb_grad, axis=1), 'exp')  25.6 us
    psum x1, blocking collectives, per_device(): row_total = lax.psum(jnp.sum(cexp, axis=1), 'exp')  23.7 us
  transfers between devices with their start and end apart: 3, of which 2 were waited for; matrix products, arithmetic and copies ran while one was open for 2% of the time, Pallas kernels for 0%

commit v1 on v0

v1 whole, which is shorter than its diff:
```python
import jax
import jax.numpy as jnp
from jax import lax
from jax.sharding import PartitionSpec as P

BF = jnp.bfloat16
F32 = jnp.float32


def gather_blocks(block, axis, n):
    spread = jnp.broadcast_to(block[None], (n,) + block.shape)
    return lax.all_to_all(spread, axis, 0, 0, tiled=True)


def merge_stats(got, axis):
    peak, total, dot = got[:, 0], got[:, 1], got[:, 2]
    top = jnp.max(peak, axis=0)
    scale = jnp.exp(peak - top[None, :])
    total = jnp.sum(total * scale, axis=0)
    dot = jnp.sum(dot * scale, axis=0)
    return top, total, dot / total


def make_per_device(n_seq, n_exp):
    def per_device(tokens, phi, expert_out, slot_in_grad, out_grad):
        rows, width = tokens.shape
        slots = expert_out.shape[0]
        phi_full = gather_blocks(phi, "seq", n_seq).reshape(width, slots)

        logits = jnp.dot(tokens, phi_full, preferred_element_type=F32)
        disp_grad = lax.dot_general(
            tokens, slot_in_grad, (((1,), (1,)), ((), ())), preferred_element_type=F32
        )
        comb_grad = lax.dot_general(
            out_grad, expert_out, (((1,), (1,)), ((), ())), preferred_element_type=F32
        )

        row_top = jnp.max(logits, axis=1)
        row_exp = jnp.exp(logits - row_top[:, None])
        row_stats = jnp.stack(
            [row_top, jnp.sum(row_exp, axis=1), jnp.sum(row_exp * comb_grad, axis=1)]
        )
        col_top = jnp.max(logits, axis=0)
        col_exp = jnp.exp(logits - col_top[None, :])
        col_stats = jnp.stack(
            [col_top, jnp.sum(col_exp, axis=0), jnp.sum(col_exp * disp_grad, axis=0)]
        )

        row_got = gather_blocks(row_stats, "exp", n_exp)
        row_peak, row_total, row_dot = merge_stats(row_got, "exp")
        col_got = gather_blocks(col_stats, "seq", n_seq)
        col_peak, col_total, col_dot = merge_stats(col_got, "seq")

        combine = jnp.exp(logits - row_peak[:, None]) / row_total[:, None]
        dispatch = jnp.exp(logits - col_peak[None, :]) / col_total[None, :]
        dispatch_b = dispatch.astype(BF)
        combine_b = combine.astype(BF)
        logit_grad = (
            combine * (comb_grad - row_dot[:, None]) + dispatch * (disp_grad - col_dot[None, :])
        ).astype(BF)

        partial = jnp.dot(dispatch_b, slot_in_grad, preferred_element_type=F32)
        partial = partial + lax.dot_general(
            logit_grad, phi_full, (((1,), (1,)), ((), ())), preferred_element_type=F32
        )
        token_grad = lax.psum_scatter(
            partial.astype(BF), "exp", scatter_dimension=1, tiled=True
        )

        slot_term = lax.dot_general(
            out_grad, combine_b, (((0,), (0,)), ((), ())), preferred_element_type=F32
        ).astype(BF)
        phi_term = lax.dot_general(
            tokens, logit_grad, (((0,), (0,)), ((), ())), preferred_element_type=F32
        ).astype(BF)
        both = jnp.stack(
            [slot_term.reshape(n_seq, -1, slots), phi_term.reshape(n_seq, -1, slots)], axis=1
        )
        got = lax.all_to_all(both, "seq", 0, 0, tiled=True)
        total = jnp.sum(got.astype(F32), axis=0)
        slot_grad = total[0].T.astype(BF)
        phi_grad = total[1]
        return (token_grad, phi_grad, slot_grad)

    return per_device


def solution(mesh):
    return jax.shard_map(
        make_per_device(mesh.shape["seq"], mesh.shape["exp"]),
        mesh=mesh,
        in_specs=(P("seq", None), P("seq", "exp"), P("exp", None), P("exp", None), P("seq", None)),
        out_specs=(P("seq", "exp"), P("seq", "exp"), P("exp", "seq")),
        check_vma=False,
    )
```

time: 903 us -> 183 us (0.20)
  the two profiles are of different devices: /device:TPU:1 before, /device:TPU:64 now
where the time goes in v1:
time: 183 us; the launch traced here: 182 us
  waiting for transfers between devices  67.9 us (37%)
  blocking collectives  38.7 us (21%)
  starting transfers between devices  34 us (19%)
  local copies, waits for them, and re-layouts  16.5 us (9%)
  between operations  14.2 us (8%)
  matrix products  8.95 us (5%)
    all_to_all x3, waiting for transfers between devices, gather_blocks(): return lax.all_to_all(spread, axis, 0, 0, tiled=True)  45.5 us
    all_to_all x1, blocking collectives, per_device(): got = lax.all_to_all(both, 'seq', 0, 0, tiled=True)  38.7 us
    all_to_all x3, starting transfers between devices, gather_blocks(): return lax.all_to_all(spread, axis, 0, 0, tiled=True)  34 us
    unnamed x2, waiting for transfers between devices  22.4 us
    unnamed x16, local copies, waits for them, and re-layouts  12.4 us
  transfers between devices with their start and end apart: 4, of which 4 were waited for; matrix products, arithmetic and copies ran while one was open for 6% of the time, Pallas kernels for 0%

profile of v1, /device:TPU:64, one launch (start us, length us, event | category | flops | bytes accessed | tf_op | source)
XLA Modules:
  0.0 181.9 jit_solution(2198342097775708040)
XLA Ops:
  7.2 0.0 copy-start
  7.2 0.9 broadcast_in_dim.6
  8.1 1.0 reshape.33
  9.1 21.4 %all-to-all-start = ((bf16[64,2,1024]{2,1,0:T(2,128)(2,1)}), bf16[64,2,1024]{2,1,0:T(2,128)(2,1)S(1)}, u32[]{:S(2)}, u32[]{:S(2)}) async-start(bf16[64,2,1024]{2,1,0:T(2,128)(2,1)} %reshape.33), calls=%async_computation | async-start | bytes 524288 | tf_op jit(solution)/shard_map/all_to_all | solution.py:12
  30.5 0.0 copy-done
  30.5 1.7 fusion.16
  32.3 0.0 copy-start.3
  32.3 21.1 %all-to-all-done = bf16[64,2,1024]{2,1,0:T(2,128)(2,1)S(1)} async-done(((bf16[64,2,1024]{2,1,0:T(2,128)(2,1)}), bf16[64,2,1024]{2,1,0:T(2,128)(2,1)S(1)}, u32[]{:S(2)}, u32[]{:S(2)}) %all-to-all-start) | async-done | bytes 262176 | tf_op jit(solution)/shard_map/all_to_all | solution.py:12
  53.4 0.3 reshape.34
  53.7 0.0 copy-start.1
  53.8 0.9 fusion.12
  54.6 0.0 copy-done.3
  54.6 0.7 copy-done.1
  55.3 0.8 fusion.3
  56.2 0.7 broadcast_in_dim.8
  56.8 7.2 %all-to-all-start.2 = ((f32[16,3,512]{2,1,0:T(4,128)}), f32[16,3,512]{2,1,0:T(4,128)S(1)}, u32[]{:S(2)}, u32[]{:S(2)}) async-start(f32[16,3,512]{2,1,0:T(4,128)} %broadcast_in_dim.8), calls=%async_computation.2 | async-start | bytes 262144 | tf_op jit(solution)/shard_map/all_to_all | solution.py:12
  64.1 0.7 reshape.35
  64.9 9.2 %all-to-all-done.2 = f32[16,3,512]{2,1,0:T(4,128)S(1)} async-done(((f32[16,3,512]{2,1,0:T(4,128)}), f32[16,3,512]{2,1,0:T(4,128)S(1)}, u32[]{:S(2)}, u32[]{:S(2)}) %all-to-all-start.2) | async-done | bytes 98336 | tf_op jit(solution)/shard_map/all_to_all | solution.py:12
  74.1 5.3 %all-to-all-start.1 = ((f32[64,1,192]{2,1,0:T(1,128)}), f32[64,1,192]{2,1,0:T(1,128)S(1)}, u32[]{:S(2)}, u32[]{:S(2)}) async-start(f32[64,1,192]{2,1,0:T(1,128)} %reshape.35), calls=%async_computation.1 | async-start | bytes 131072 | tf_op jit(solution)/shard_map/all_to_all | solution.py:12
  79.4 0.0 reduce-scatter.4.cloned.1.call-start
  79.5 0.1 fusion.13
  79.6 15.1 %all-to-all-done.1 = f32[64,1,192]{2,1,0:T(1,128)S(1)} async-done(((f32[64,1,192]{2,1,0:T(1,128)}), f32[64,1,192]{2,1,0:T(1,128)S(1)}, u32[]{:S(2)}, u32[]{:S(2)}) %all-to-all-start.1) | async-done | bytes 49184 | tf_op jit(solution)/shard_map/all_to_all | solution.py:12
  94.7 0.5 broadcast.10
  95.2 0.8 reduce.2
  96.0 0.1 reshape.36
  96.1 0.1 fusion.14
  96.3 0.0 copy-start.2
  96.3 0.9 fusion.15
  97.2 0.1 copy-done.2
  97.2 2.1 %add_convert_fusion = bf16[512,2048]{1,0:T(8,128)(2,1)} fusion(f32[512,2048]{1,0:T(8,128)S(1)} %fusion.15, bf16[64,2048]{1,0:T(8,128)(2,1)S(1)} %copy-done.2, f32[512,64]{0,1:T(8,128)S(1)} %get-tuple-element.22, f32[64]{0:T(128)S(1)} %get-tuple-element.13, f32[64]{0:T(128)S(1)} %reduce_max.37), kind=kOutput, calls=%fused_computation | convolution fusion | flops 136413184 | bytes 6685184 | tf_op jit(solution)/shard_map/dot_general | solution.py:62
  99.4 3.9 %copy.35 = bf16[512,2048]{0,1:T(8,128)(2,1)} copy(bf16[512,2048]{1,0:T(8,128)(2,1)} %add_convert_fusion) | data formatting | bytes 4194304
  103.3 0.0 reduce-scatter.4.cloned.1.call-update
  103.3 2.1 %fusion = bf16[2048,64]{0,1:T(8,128)(2,1)S(1)} fusion(bf16[512,2048]{1,0:T(8,128)(2,1)} %param.9, f32[512,64]{0,1:T(8,128)S(1)} %get-tuple-element.22, f32[512]{0:T(512)S(1)} %get-tuple-element.11, f32[512]{0:T(512)S(1)} %get-tuple-element.16), kind=kOutput, calls=%fused_computation.3 | convolution fusion | flops 134447104 | bytes 2494464 | tf_op jit(solution)/shard_map/dot_general | solution.py:70
  105.4 0.3 copy.32
  105.7 0.5 fusion.1
  106.2 0.3 copy.33
  106.5 0.2 pad_maximum_fusion
  106.8 0.1 copy.34
  106.9 1.6 reshape.37
  108.5 38.7 %all_to_all.20 = bf16[64,2,2048]{2,1,0:T(2,128)(2,1)} all-to-all(bf16[64,2,2048]{2,1,0:T(2,128)(2,1)} %reshape.37), channel_id=1, replica_groups=mesh['seq'=64,'exp'=16] {'seq'}, dimensions={0} | all-to-all | bytes 1048576 | tf_op jit(solution)/shard_map/all_to_all | solution.py:79
  147.2 2.3 %reshape.38 = bf16[64,2,32,64]{3,2,1,0:T(8,128)(2,1)S(1)} reshape(bf16[64,2,2048]{2,1,0:T(2,128)(2,1)} %all_to_all.20) | data formatting | bytes 1048576
  149.5 0.2 convert_reduce_fusion
  149.7 0.6 fusion.11
  150.3 0.6 slice_bitcast_fusion
  150.9 22.4 %reduce-scatter.4.cloned.1.call-done = bf16[128,512]{1,0:T(8,128)(2,1)} async-done(((bf16[2048,512]{1,0:T(8,128)(2,1)}), bf16[128,512]{1,0:T(8,128)(2,1)}) %reduce-scatter.4.cloned.1.call-update) | async-done | bytes 131088
  173.4 1.7 copy.36
  (8 shorter events, 0.1 us)
Async XLA Ops:
  7.2 23.4 %copy-start = (bf16[512,2048]{1,0:T(8,128)(2,1)S(1)}, bf16[512,2048]{1,0:T(8,128)(2,1)}, u32[]{:S(2)}) copy-start(bf16[512,2048]{1,0:T(8,128)(2,1)} %param.5) | copy-start | bytes 6291460
  9.1 44.3 %all-to-all-start = ((bf16[64,2,1024]{2,1,0:T(2,128)(2,1)}), bf16[64,2,1024]{2,1,0:T(2,128)(2,1)S(1)}, u32[]{:S(2)}, u32[]{:S(2)}) async-start(bf16[64,2,1024]{2,1,0:T(2,128)(2,1)} %reshape.33), calls=%async_computation | async-start | bytes 524288 | tf_op jit(solution)/shard_map/all_to_all | solution.py:12
  32.3 22.4 %copy-start.3 = (bf16[64,2048]{1,0:T(8,128)(2,1)S(1)}, bf16[64,2048]{1,0:T(8,128)(2,1)}, u32[]{:S(2)}) copy-start(bf16[64,2048]{1,0:T(8,128)(2,1)} %param.7) | copy-start | bytes 786436
  53.7 1.6 copy-start.1
  56.8 17.2 %all-to-all-start.2 = ((f32[16,3,512]{2,1,0:T(4,128)}), f32[16,3,512]{2,1,0:T(4,128)S(1)}, u32[]{:S(2)}, u32[]{:S(2)}) async-start(f32[16,3,512]{2,1,0:T(4,128)} %broadcast_in_dim.8), calls=%async_computation.2 | async-start | bytes 262144 | tf_op jit(solution)/shard_map/all_to_all | solution.py:12
  74.1 20.6 %all-to-all-start.1 = ((f32[64,1,192]{2,1,0:T(1,128)}), f32[64,1,192]{2,1,0:T(1,128)S(1)}, u32[]{:S(2)}, u32[]{:S(2)}) async-start(f32[64,1,192]{2,1,0:T(1,128)} %reshape.35), calls=%async_computation.1 | async-start | bytes 131072 | tf_op jit(solution)/shard_map/all_to_all | solution.py:12
  79.4 93.9 %reduce-scatter.4.cloned.1.call-start = ((), (), s32[]{:S(2)}) async-start(), calls=%async_computation.5 | async-start | bytes 2228224
  96.3 1.0 copy-start.2
Sparse Core Ops, SparseCore 0:
  103.4 69.8 reduce-scatter.3

commit v2 on v1

v2 whole, which is shorter than its diff:
```python
import jax
import jax.numpy as jnp
from jax import lax
from jax.experimental import pallas as pl
from jax.experimental.pallas import tpu as pltpu
from jax.sharding import Mesh
from jax.sharding import PartitionSpec as P

BF = jnp.bfloat16
F32 = jnp.float32
EXP = ("y", "xl")
SWAP = [(0, 1), (1, 0)]


def gather_blocks(block, axis, n):
    spread = jnp.broadcast_to(block[None], (n,) + block.shape)
    return lax.all_to_all(spread, axis, 0, 0, tiled=True)


def merge_stats(got):
    peak, total, dot = got[:, 0], got[:, 1], got[:, 2]
    top = jnp.max(peak, axis=0)
    scale = jnp.exp(peak - top[None, :])
    total = jnp.sum(total * scale, axis=0)
    dot = jnp.sum(dot * scale, axis=0)
    return top, total, dot / total


def weights_kernel(place_ref, sig_ref, phi_ref, own_ref, lent_ref):
    wide = own_ref.shape[1]
    slots = sig_ref.shape[0]
    first = place_ref[0] == 0
    for top, part in ((0, sig_ref[...]), (slots, phi_ref[...].T)):
        even, odd = part[:, :wide], part[:, wide:]
        own_ref[top : top + slots] = jnp.where(first, even, odd)
        lent_ref[top : top + slots] = jnp.where(first, odd, even)


def split_weights(place, sig, phi_full, n, wide):
    slots, width = sig.shape
    out = jax.ShapeDtypeStruct((2 * slots, n * wide), BF)
    spec = pl.BlockSpec((2 * slots, wide), lambda i: (0, i))
    return pl.pallas_call(
        weights_kernel,
        grid=(n,),
        in_specs=[
            pl.BlockSpec(memory_space=pltpu.SMEM),
            pl.BlockSpec((slots, 2 * wide), lambda i: (0, i)),
            pl.BlockSpec((2 * wide, slots), lambda i: (i, 0)),
        ],
        out_specs=[spec, spec],
        out_shape=[out, out],
        cost_estimate=pl.CostEstimate(
            flops=4 * slots * width, bytes_accessed=8 * slots * width, transcendentals=0
        ),
        compiler_params=pltpu.CompilerParams(vmem_limit_bytes=32 * 1024 * 1024),
    )(place[None], sig, phi_full)


def blocks_kernel(own_ref, far_ref, own_w_ref, far_w_ref, out_ref):
    acc = jnp.dot(own_ref[...], own_w_ref[...], preferred_element_type=F32)
    acc = acc + jnp.dot(far_ref[...], far_w_ref[...], preferred_element_type=F32)
    out_ref[0] = acc.astype(BF)


def column_blocks(own, far, own_w, far_w, n, wide):
    rows, depth = own.shape
    whole = pl.BlockSpec((rows, depth), lambda i: (0, 0))
    part = pl.BlockSpec((depth, wide), lambda i: (0, i))
    return pl.pallas_call(
        blocks_kernel,
        grid=(n,),
        in_specs=[whole, whole, part, part],
        out_specs=pl.BlockSpec((1, rows, wide), lambda i: (i, 0, 0)),
        out_shape=jax.ShapeDtypeStruct((n, rows, wide), BF),
        cost_estimate=pl.CostEstimate(
            flops=4 * n * rows * depth * wide,
            bytes_accessed=2 * (2 * rows * depth + 2 * n * depth * wide + n * rows * wide),
            transcendentals=0,
        ),
        compiler_params=pltpu.CompilerParams(vmem_limit_bytes=32 * 1024 * 1024),
    )(own, far, own_w, far_w)


def make_per_device(n_seq, n_y):
    def per_device(tokens, phi, expert_out, slot_in_grad, out_grad):
        rows, width = tokens.shape
        slots = expert_out.shape[0]
        wide = width // (2 * n_y)
        half = phi.shape[0] // 2
        packed = jnp.concatenate([phi[:half], phi[half:]], axis=1)
        got_phi = gather_blocks(packed, "seq", n_seq)
        phi_full = jnp.concatenate([got_phi[:, :, :slots], got_phi[:, :, slots:]], axis=1)
        phi_full = phi_full.reshape(width, slots)

        logits = jnp.dot(tokens, phi_full, preferred_element_type=F32)
        disp_grad = lax.dot_general(
            tokens, slot_in_grad, (((1,), (1,)), ((), ())), preferred_element_type=F32
        )
        comb_grad = lax.dot_general(
            out_grad, expert_out, (((1,), (1,)), ((), ())), preferred_element_type=F32
        )

        place = lax.axis_index("xl").astype(jnp.int32)
        own_w, lent_w = split_weights(place, slot_in_grad, phi_full, n_y, wide)
        far_w = lax.ppermute(lent_w, "xl", SWAP)

        row_top = jnp.max(logits, axis=1)
        row_exp = jnp.exp(logits - row_top[:, None])
        row_stats = jnp.stack(
            [row_top, jnp.sum(row_exp, axis=1), jnp.sum(row_exp * comb_grad, axis=1)]
        )
        col_top = jnp.max(logits, axis=0)
        col_exp = jnp.exp(logits - col_top[None, :])
        col_stats = jnp.stack(
            [col_top, jnp.sum(col_exp, axis=0), jnp.sum(col_exp * disp_grad, axis=0)]
        )

        row_got = gather_blocks(row_stats, EXP, 2 * n_y)
        row_got, far_w = lax.optimization_barrier((row_got, far_w))
        row_peak, row_total, row_dot = merge_stats(row_got)
        col_got = gather_blocks(col_stats, "seq", n_seq)
        col_peak, col_total, col_dot = merge_stats(col_got)

        combine = jnp.exp(logits - row_peak[:, None]) / row_total[:, None]
        dispatch = jnp.exp(logits - col_peak[None, :]) / col_total[None, :]
        combine_b = combine.astype(BF)
        logit_grad = (
            combine * (comb_grad - row_dot[:, None]) + dispatch * (disp_grad - col_dot[None, :])
        ).astype(BF)

        own = jnp.concatenate([dispatch.astype(BF), logit_grad], axis=1)
        own, logit_grad, combine_b = lax.optimization_barrier((own, logit_grad, combine_b))
        far = lax.ppermute(own, "xl", SWAP)
        slot_term = lax.dot_general(
            out_grad, combine_b, (((0,), (0,)), ((), ())), preferred_element_type=F32
        ).astype(BF)

        partial = column_blocks(own, far, own_w, far_w, n_y, wide)
        partial, logit_grad, slot_term = lax.optimization_barrier((partial, logit_grad, slot_term))
        token_grad = lax.psum_scatter(
            partial.reshape(n_y * rows, wide), "y", scatter_dimension=0, tiled=True
        )
        phi_term = lax.dot_general(
            tokens, logit_grad, (((0,), (0,)), ((), ())), preferred_element_type=F32
        ).astype(BF)
        both = jnp.concatenate([phi_term, slot_term], axis=1)
        got = lax.all_to_all(both.reshape(n_seq, -1, 2 * slots), "seq", 0, 0, tiled=True)
        total = jnp.sum(got.astype(F32), axis=0)
        phi_grad = total[:, :slots]
        slot_grad = total[:, slots:].T.astype(BF)
        return (token_grad, phi_grad, slot_grad)

    return per_device


def solution(mesh):
    n_seq, n_exp = mesh.devices.shape
    n_y = n_exp // 2
    fine = Mesh(mesh.devices.reshape(n_seq, n_y, 2), ("seq", "y", "xl"))
    return jax.shard_map(
        make_per_device(n_seq, n_y),
        mesh=fine,
        in_specs=(P("seq", None), P("seq", EXP), P(EXP, None), P(EXP, None), P("seq", None)),
        out_specs=(P("seq", EXP), P("seq", EXP), P(EXP, "seq")),
        check_vma=False,
    )
```

time: 183 us -> 174 us (0.951)
  the two profiles are of different devices: /device:TPU:64 before, /device:TPU:8 now
where the time goes in v2:
time: 174 us
  waiting for transfers between devices  85.8 us (49%)
  starting transfers between devices  45.9 us (26%)
  between operations  14.3 us (8%)
  local copies, waits for them, and re-layouts  11.7 us (7%)
  other arithmetic  7.08 us (4%)
  Pallas kernels  4.59 us (3%)
  matrix products  4.34 us (2%)
    all_to_all x3, starting transfers between devices, gather_blocks(): return lax.all_to_all(spread, axis, 0, 0, tiled=True)  34.7 us
    all_to_all x1, waiting for transfers between devices, per_device(): lax.all_to_all(both.reshape(n_seq, -1, 2 * slots), 'seq', 0, 0, tiled=True)  33 us
    all_to_all x3, waiting for transfers between devices, gather_blocks(): return lax.all_to_all(spread, axis, 0, 0, tiled=True)  31.8 us
    reduce_scatter x1, waiting for transfers between devices, per_device(): lax.psum_scatter(partial.reshape(n_y * rows, wide), 'y', scatter_dimensio...  16.7 us
    all_to_all x1, starting transfers between devices, per_device(): lax.all_to_all(both.reshape(n_seq, -1, 2 * slots), 'seq', 0, 0, tiled=True)  5.79 us
    pallas_call x1, Pallas kernels, column_blocks(): pl.pallas_call(blocks_kernel, grid=(n,), in_specs=[whole, whole, part, pa...  3.81 us
    ppermute x1, waiting for transfers between devices, per_device(): far = lax.ppermute(own, 'xl', SWAP)  3.63 us
  transfers between devices with their start and end apart: 7, of which 6 were waited for; matrix products, arithmetic and copies ran while one was open for 8% of the time, Pallas kernels for 0%

profile of v2, /device:TPU:8, one launch (start us, length us, event | category | flops | bytes accessed | tf_op | source)
XLA Modules:
  0.0 173.7 jit_solution(13940908659164847773)
XLA Ops:
  7.2 0.0 copy-start
  7.2 0.9 fusion.16
  8.0 0.1 pad_maximum_fusion.4
  8.1 0.7 broadcast_in_dim.8
  8.8 22.2 %all-to-all-start = ((bf16[64,16,128]{2,1,0:T(8,128)(2,1)}), bf16[64,16,128]{2,1,0:T(8,128)(2,1)S(1)}, u32[]{:S(2)}, u32[]{:S(2)}) async-start(bf16[64,16,128]{2,1,0:T(8,128)(2,1)} %broadcast_in_dim.8), calls=%async_computation | async-start | bytes 524288 | tf_op jit(solution)/shard_map/all_to_all | solution.py:17
  31.1 0.0 copy-done
  31.1 1.7 fusion.17
  32.8 21.2 %all-to-all-done = bf16[64,16,128]{2,1,0:T(8,128)(2,1)S(1)} async-done(((bf16[64,16,128]{2,1,0:T(8,128)(2,1)}), bf16[64,16,128]{2,1,0:T(8,128)(2,1)S(1)}, u32[]{:S(2)}, u32[]{:S(2)}) %all-to-all-start) | async-done | bytes 262176 | tf_op jit(solution)/shard_map/all_to_all | solution.py:17
  54.0 0.1 fusion.14
  54.1 0.0 copy-start.2
  54.1 0.0 copy-start.6
  54.1 0.1 pad_maximum_fusion
  54.2 0.9 fusion.13
  55.1 0.2 fusion.7
  55.3 0.4 copy-done.2
  55.7 0.0 copy-done.6
  55.7 0.0 copy-start.1
  55.7 0.8 fusion.4
  56.5 0.8 reshape.38
  57.3 4.9 %all-to-all-start.1 = ((f32[64,1,192]{2,1,0:T(1,128)}), f32[64,1,192]{2,1,0:T(1,128)S(1)}, u32[]{:S(2)}, u32[]{:S(2)}) async-start(f32[64,1,192]{2,1,0:T(1,128)} %reshape.38), calls=%async_computation.1 | async-start | bytes 131072 | tf_op jit(solution)/shard_map/all_to_all | solution.py:17
  62.2 0.8 copy.48
  63.0 0.8 copy.40
  63.8 0.8 copy.47
  64.7 0.0 copy-done.1
  64.7 0.8 shard_map.76
  65.5 0.0 copy-start.4
  65.5 0.0 copy-start.5
  65.5 2.6 %collective-permute-start = (bf16[128,1024]{1,0:T(8,128)(2,1)S(1)}, bf16[128,1024]{1,0:T(8,128)(2,1)S(1)}, u32[]{:S(2)}, u32[]{:S(2)}) collective-permute-start(bf16[128,1024]{1,0:T(8,128)(2,1)S(1)} %get-tuple-element.13), channel_id=1, source_target_pairs={{0,1},{1,0},{2,3},{3,2},{4,5},{5,4},{6,7},{7,6},{8,9},{9,8},{10,11... | collective-permute-start | bytes 786440 | tf_op jit(solution)/shard_map/ppermute | solution.py:106
  68.1 9.9 %all-to-all-done.1 = f32[64,1,192]{2,1,0:T(1,128)S(1)} async-done(((f32[64,1,192]{2,1,0:T(1,128)}), f32[64,1,192]{2,1,0:T(1,128)S(1)}, u32[]{:S(2)}, u32[]{:S(2)}) %all-to-all-start.1) | async-done | bytes 49184 | tf_op jit(solution)/shard_map/all_to_all | solution.py:17
  78.0 0.0 copy-start.7
  78.0 0.7 broadcast_in_dim.10
  78.7 0.0 copy-done.7
  78.7 7.6 %all-to-all-start.2 = ((f32[16,3,512]{2,1,0:T(4,128)}), f32[16,3,512]{2,1,0:T(4,128)S(1)}, u32[]{:S(2)}, u32[]{:S(2)}) async-start(f32[16,3,512]{2,1,0:T(4,128)} %broadcast_in_dim.10), calls=%async_computation.2 | async-start | bytes 262144 | tf_op jit(solution)/shard_map/all_to_all | solution.py:17
  86.3 0.5 broadcast.16
  86.8 2.3 %reduce.6 = f32[64,192]{1,0:T(8,128)} reduce(f32[64,1,192]{2,1,0:T(1,128)} %copy-done.7, f32[]{:T(128)} %broadcast.16), dimensions={1}, to_apply=%all_to_all.13.reduce_sub_computation | reduce | bytes 98308 | tf_op jit(solution)/shard_map/all_to_all | solution.py:17
  89.1 1.6 reshape.39
  90.7 1.8 %fusion.15 = (f32[64,1,64]{2,1,0:T(1,128)}, f32[64,1,64]{2,1,0:T(1,128)}, f32[64,1,64]{2,1,0:T(1,128)}) fusion(f32[64,3,64]{2,1,0:T(4,128)} %reshape.39), kind=kLoop, calls=%fused_computation.42 | loop fusion | bytes 98304 | tf_op jit(solution)/shard_map/slice | solution.py:21
  92.4 0.8 reduce_max.37
  93.2 0.8 multiply_reduce_fusion.1
  94.1 0.7 all-to-all-done.2
  94.7 0.0 copy-start.3
  94.7 0.0 collective-permute-done.far_w_ref
  94.9 1.3 bitcast_convert_fusion
  96.2 0.0 copy-done.4
  96.2 0.0 copy-done.5
  96.2 1.2 fusion.3
  97.4 0.1 pad_maximum_fusion.2.own_ref
  97.5 2.7 %collective-permute-start.1 = (bf16[512,128]{1,0:T(8,128)(2,1)S(1)}, bf16[512,128]{1,0:T(8,128)(2,1)S(1)}, u32[]{:S(2)}, u32[]{:S(2)}) collective-permute-start(bf16[512,128]{1,0:T(8,128)(2,1)S(1)} %pad_maximum_fusion.2.own_ref), channel_id=1, source_target_pairs={{0,1},{1,0},{2,3},{3,2},{4,5},{5,4},{6,7},{7,6},{8,9},{9,8},{10,11... | collective-permute-start | bytes 393224 | tf_op jit(solution)/shard_map/ppermute | solution.py:134
  100.3 0.0 copy-done.3
  100.3 0.5 fusion
  100.8 3.6 %collective-permute-done.1.far_ref = bf16[512,128]{1,0:T(8,128)(2,1)S(1)} collective-permute-done((bf16[512,128]{1,0:T(8,128)(2,1)S(1)}, bf16[512,128]{1,0:T(8,128)(2,1)S(1)}, u32[]{:S(2)}, u32[]{:S(2)}) %collective-permute-start.1) | collective-permute-done | bytes 131104 | tf_op jit(solution)/shard_map/ppermute | solution.py:134
  104.4 3.8 %shard_map.77 = bf16[8,512,128]{2,1,0:T(8,128)(2,1)} custom-call(bf16[512,128]{1,0:T(8,128)(2,1)S(1)} %pad_maximum_fusion.2.own_ref, bf16[512,128]{1,0:T(8,128)(2,1)S(1)} %collective-permute-done.1.far_ref, bf16[128,1024]{1,0:T(8,128)(2,1)S(1)} %get-tuple-element.16.own_w_ref, bf16[128,1024]{1,0:T(8,128)(2,1)S(1)} %collective-permute-done.far_w_ref), custom_call_target="tpu_custom_call" | custom-call | flops 268435456 | bytes 1835008 | tf_op jit(solution)/shard_map/pallas_call | solution.py:70
  108.2 0.5 fusion.1
  108.8 1.0 copy.49
  109.8 5.8 %all-to-all-start.3 = ((bf16[64,32,128]{2,1,0:T(8,128)(2,1)}), bf16[64,32,128]{2,1,0:T(8,128)(2,1)S(1)}, u32[]{:S(2)}, u32[]{:S(2)}) async-start(bf16[64,32,128]{2,1,0:T(8,128)(2,1)} %bitcast.20), calls=%async_computation.4 | async-start | bytes 1048576 | tf_op jit(solution)/shard_map/all_to_all | solution.py:148
  115.6 0.0 reduce-scatter.2.cloned.1.call-start
  115.6 0.7 reduce-scatter.2.cloned.1.call-update
  116.3 33.0 %all-to-all-done.3 = bf16[64,32,128]{2,1,0:T(8,128)(2,1)S(1)} async-done(((bf16[64,32,128]{2,1,0:T(8,128)(2,1)}), bf16[64,32,128]{2,1,0:T(8,128)(2,1)S(1)}, u32[]{:S(2)}, u32[]{:S(2)}) %all-to-all-start.3) | async-done | bytes 524320 | tf_op jit(solution)/shard_map/all_to_all | solution.py:148
  149.3 0.1 convert_reduce_fusion
  149.4 0.0 copy-start.8
  149.4 0.7 fusion.12
  150.1 16.7 %reduce-scatter.2.cloned.1.call-done = bf16[512,128]{1,0:T(8,128)(2,1)} async-done(((bf16[4096,128]{1,0:T(8,128)(2,1)}), bf16[512,128]{1,0:T(8,128)(2,1)}) %reduce-scatter.2.cloned.1.call-update) | async-done | bytes 131088 | tf_op jit(solution)/shard_map/reduce_scatter | solution.py:141
  166.8 0.0 copy-done.8
  (10 shorter events, 0.2 us)
Async XLA Ops:
  7.2 23.9 %copy-start = (bf16[512,2048]{1,0:T(8,128)(2,1)S(1)}, bf16[512,2048]{1,0:T(8,128)(2,1)}, u32[]{:S(2)}) copy-start(bf16[512,2048]{1,0:T(8,128)(2,1)} %param.5) | copy-start | bytes 6291460
  8.8 45.1 %all-to-all-start = ((bf16[64,16,128]{2,1,0:T(8,128)(2,1)}), bf16[64,16,128]{2,1,0:T(8,128)(2,1)S(1)}, u32[]{:S(2)}, u32[]{:S(2)}) async-start(bf16[64,16,128]{2,1,0:T(8,128)(2,1)} %broadcast_in_dim.8), calls=%async_computation | async-start | bytes 524288 | tf_op jit(solution)/shard_map/all_to_all | solution.py:17
  54.1 1.6 copy-start.2
  54.1 1.6 copy-start.6
  55.7 9.0 %copy-start.1 = (bf16[64,2048]{1,0:T(8,128)(2,1)S(1)}, bf16[64,2048]{1,0:T(8,128)(2,1)}, u32[]{:S(2)}) copy-start(bf16[64,2048]{1,0:T(8,128)(2,1)} %sig_ref.1) | copy-start | bytes 786436
  57.3 20.8 %all-to-all-start.1 = ((f32[64,1,192]{2,1,0:T(1,128)}), f32[64,1,192]{2,1,0:T(1,128)S(1)}, u32[]{:S(2)}, u32[]{:S(2)}) async-start(f32[64,1,192]{2,1,0:T(1,128)} %reshape.38), calls=%async_computation.1 | async-start | bytes 131072 | tf_op jit(solution)/shard_map/all_to_all | solution.py:17
  65.5 30.7 %copy-start.4 = (f32[64,512]{0,1:T(8,128)S(1)}, f32[64,512]{0,1:T(8,128)}, u32[]{:S(2)}) copy-start(f32[64,512]{0,1:T(8,128)} %copy.40) | copy-start | bytes 393220
  65.5 30.7 %copy-start.5 = (f32[512,64]{1,0:T(8,128)S(1)}, f32[512,64]{1,0:T(8,128)}, u32[]{:S(2)}) copy-start(f32[512,64]{1,0:T(8,128)} %copy.48) | copy-start | bytes 393220
  65.5 29.3 %collective-permute-start = (bf16[128,1024]{1,0:T(8,128)(2,1)S(1)}, bf16[128,1024]{1,0:T(8,128)(2,1)S(1)}, u32[]{:S(2)}, u32[]{:S(2)}) collective-permute-start(bf16[128,1024]{1,0:T(8,128)(2,1)S(1)} %get-tuple-element.13), channel_id=1, source_target_pairs={{0,1},{1,0},{2,3},{3,2},{4,5},{5,4},{6,7},{7,6},{8,9},{9,8},{10,11... | collective-permute-start | bytes 786440 | tf_op jit(solution)/shard_map/ppermute | solution.py:106
  78.0 0.7 copy-start.7
  78.7 16.0 %all-to-all-start.2 = ((f32[16,3,512]{2,1,0:T(4,128)}), f32[16,3,512]{2,1,0:T(4,128)S(1)}, u32[]{:S(2)}, u32[]{:S(2)}) async-start(f32[16,3,512]{2,1,0:T(4,128)} %broadcast_in_dim.10), calls=%async_computation.2 | async-start | bytes 262144 | tf_op jit(solution)/shard_map/all_to_all | solution.py:17
  94.7 5.5 %copy-start.3 = (bf16[512,2048]{1,0:T(8,128)(2,1)S(1)}, bf16[512,2048]{1,0:T(8,128)(2,1)}, u32[]{:S(2)}) copy-start(bf16[512,2048]{1,0:T(8,128)(2,1)} %param.9) | copy-start | bytes 6291460
  97.5 6.9 %collective-permute-start.1 = (bf16[512,128]{1,0:T(8,128)(2,1)S(1)}, bf16[512,128]{1,0:T(8,128)(2,1)S(1)}, u32[]{:S(2)}, u32[]{:S(2)}) collective-permute-start(bf16[512,128]{1,0:T(8,128)(2,1)S(1)} %pad_maximum_fusion.2.own_ref), channel_id=1, source_target_pairs={{0,1},{1,0},{2,3},{3,2},{4,5},{5,4},{6,7},{7,6},{8,9},{9,8},{10,11... | collective-permute-start | bytes 393224 | tf_op jit(solution)/shard_map/ppermute | solution.py:134
  109.8 39.5 %all-to-all-start.3 = ((bf16[64,32,128]{2,1,0:T(8,128)(2,1)}), bf16[64,32,128]{2,1,0:T(8,128)(2,1)S(1)}, u32[]{:S(2)}, u32[]{:S(2)}) async-start(bf16[64,32,128]{2,1,0:T(8,128)(2,1)} %bitcast.20), calls=%async_computation.4 | async-start | bytes 1048576 | tf_op jit(solution)/shard_map/all_to_all | solution.py:148
  115.6 51.2 %reduce-scatter.2.cloned.1.call-start = ((), (), s32[]{:S(2)}) async-start(), calls=%async_computation.5 | async-start | bytes 1179648 | tf_op jit(solution)/shard_map/reduce_scatter | solution.py:141
  149.4 17.4 %copy-start.8 = (f32[32,128]{1,0:T(8,128)}, f32[32,128]{1,0:T(8,128)S(1)}, u32[]{:S(2)}) copy-start(f32[32,128]{1,0:T(8,128)S(1)} %convert_reduce_fusion) | copy-start | bytes 49156
Sparse Core Ops, SparseCore 0:
  120.4 46.3 reduce-scatter.1

commit v3 on v2

--- a/solution.py
+++ b/solution.py
@@ -39,40 +39,41 @@
 def split_weights(place, sig, phi_full, n, wide):
     slots, width = sig.shape
     out = jax.ShapeDtypeStruct((2 * slots, n * wide), BF)
-    spec = pl.BlockSpec((2 * slots, wide), lambda i: (0, i))
+    spec = pl.BlockSpec((2 * slots, wide), lambda i, at: (0, i))
     return pl.pallas_call(
         weights_kernel,
-        grid=(n,),
-        in_specs=[
-            pl.BlockSpec(memory_space=pltpu.SMEM),
-            pl.BlockSpec((slots, 2 * wide), lambda i: (0, i)),
-            pl.BlockSpec((2 * wide, slots), lambda i: (i, 0)),
-        ],
-        out_specs=[spec, spec],
+        grid_spec=pltpu.PrefetchScalarGridSpec(
+            num_scalar_prefetch=1,
+            grid=(n,),
+            in_specs=[
+                pl.BlockSpec((slots, 2 * wide), lambda i, at: (0, lax.rem(i + at[1], n))),
+                pl.BlockSpec((2 * wide, slots), lambda i, at: (lax.rem(i + at[1], n), 0)),
+            ],
+            out_specs=[spec, spec],
+        ),
         out_shape=[out, out],
         cost_estimate=pl.CostEstimate(
             flops=4 * slots * width, bytes_accessed=8 * slots * width, transcendentals=0
         ),
         compiler_params=pltpu.CompilerParams(vmem_limit_bytes=32 * 1024 * 1024),
-    )(place[None], sig, phi_full)
+    )(place, sig, phi_full)
 
 
-def blocks_kernel(own_ref, far_ref, own_w_ref, far_w_ref, out_ref):
-    acc = jnp.dot(own_ref[...], own_w_ref[...], preferred_element_type=F32)
-    acc = acc + jnp.dot(far_ref[...], far_w_ref[...], preferred_element_type=F32)
-    out_ref[0] = acc.astype(BF)
+def blocks_kernel(own_ref, far_ref, own_w_ref, far_w_ref, *out_refs):
+    own, far = own_ref[...], far_ref[...]
+    for i, out_ref in enumerate(out_refs):
+        wide = out_ref.shape[1]
+        at = slice(i * wide, (i + 1) * wide)
+        acc = jnp.dot(own, own_w_ref[:, at], preferred_element_type=F32)
+        acc = acc + jnp.dot(far, far_w_ref[:, at], preferred_element_type=F32)
+        out_ref[...] = acc.astype(BF)
 
 
 def column_blocks(own, far, own_w, far_w, n, wide):
     rows, depth = own.shape
-    whole = pl.BlockSpec((rows, depth), lambda i: (0, 0))
-    part = pl.BlockSpec((depth, wide), lambda i: (0, i))
     return pl.pallas_call(
         blocks_kernel,
-        grid=(n,),
-        in_specs=[whole, whole, part, part],
-        out_specs=pl.BlockSpec((1, rows, wide), lambda i: (i, 0, 0)),
-        out_shape=jax.ShapeDtypeStruct((n, rows, wide), BF),
+        out_shape=[jax.ShapeDtypeStruct((rows, wide), BF)] * n,
         cost_estimate=pl.CostEstimate(
             flops=4 * n * rows * depth * wide,
             bytes_accessed=2 * (2 * rows * depth + 2 * n * depth * wide + n * rows * wide),
@@ -101,7 +102,7 @@
             out_grad, expert_out, (((1,), (1,)), ((), ())), preferred_element_type=F32
         )
 
-        place = lax.axis_index("xl").astype(jnp.int32)
+        place = jnp.stack([lax.axis_index("xl"), lax.axis_index("y")]).astype(jnp.int32)
         own_w, lent_w = split_weights(place, slot_in_grad, phi_full, n_y, wide)
         far_w = lax.ppermute(lent_w, "xl", SWAP)
 
@@ -136,16 +137,19 @@
             out_grad, combine_b, (((0,), (0,)), ((), ())), preferred_element_type=F32
         ).astype(BF)
 
-        partial = column_blocks(own, far, own_w, far_w, n_y, wide)
-        partial, logit_grad, slot_term = lax.optimization_barrier((partial, logit_grad, slot_term))
-        token_grad = lax.psum_scatter(
-            partial.reshape(n_y * rows, wide), "y", scatter_dimension=0, tiled=True
-        )
         phi_term = lax.dot_general(
             tokens, logit_grad, (((0,), (0,)), ((), ())), preferred_element_type=F32
         ).astype(BF)
         both = jnp.concatenate([phi_term, slot_term], axis=1)
         got = lax.all_to_all(both.reshape(n_seq, -1, 2 * slots), "seq", 0, 0, tiled=True)
+
+        blocks = column_blocks(own, far, own_w, far_w, n_y, wide)
+        token_sum = blocks[0].astype(F32)
+        for i in range(1, n_y):
+            turn = [(j, (j + i) % n_y) for j in range(n_y)]
+            token_sum = token_sum + lax.ppermute(blocks[i], "y", turn).astype(F32)
+        token_grad = token_sum.astype(BF)
+
         total = jnp.sum(got.astype(F32), axis=0)
         phi_grad = total[:, :slots]
         slot_grad = total[:, slots:].T.astype(BF)

time: 174 us -> 151 us (0.87)
  the two profiles are of different devices: /device:TPU:8 before, /device:TPU:1 now
where the time goes in v3:
time: 151 us; the launch traced here: 149 us
  starting transfers between devices  72.5 us (48%)
  waiting for transfers between devices  49.3 us (33%)
  local copies, waits for them, and re-layouts  11.8 us (8%)
  other arithmetic  8 us (5%)
  matrix products  4.35 us (3%)
  Pallas kernels  2.17 us (1%)
    all_to_all x3, starting transfers between devices, gather_blocks(): return lax.all_to_all(spread, axis, 0, 0, tiled=True)  34.4 us
    all_to_all x3, waiting for transfers between devices, gather_blocks(): return lax.all_to_all(spread, axis, 0, 0, tiled=True)  32 us
    ppermute x7, starting transfers between devices, per_device(): token_sum = token_sum + lax.ppermute(blocks[i], 'y', turn).astype(F32)  26.4 us
    ppermute x7, waiting for transfers between devices, per_device(): token_sum = token_sum + lax.ppermute(blocks[i], 'y', turn).astype(F32)  12 us
    all_to_all x1, starting transfers between devices, per_device(): lax.all_to_all(both.reshape(n_seq, -1, 2 * slots), 'seq', 0, 0, tiled=True)  7.4 us
    ppermute x1, waiting for transfers between devices, per_device(): far = lax.ppermute(own, 'xl', SWAP)  5.29 us
  transfers between devices with their start and end apart: 13, of which 7 were waited for; matrix products, arithmetic and copies ran while one was open for 9% of the time, Pallas kernels for 1%

profile of v3, /device:TPU:1, one launch (start us, length us, event | category | flops | bytes accessed | tf_op | source)
XLA Modules:
  0.0 149.1 jit_solution(12659224264057298192)
XLA Ops:
  0.6 0.0 copy-start
  0.6 0.9 fusion.16
  1.5 0.1 pad_maximum_fusion.4
  1.6 0.7 broadcast_in_dim.6
  2.3 23.3 %all-to-all-start = ((bf16[64,16,128]{2,1,0:T(8,128)(2,1)}), bf16[64,16,128]{2,1,0:T(8,128)(2,1)S(1)}, u32[]{:S(2)}, u32[]{:S(2)}) async-start(bf16[64,16,128]{2,1,0:T(8,128)(2,1)} %broadcast_in_dim.6), calls=%async_computation | async-start | bytes 524288 | tf_op jit(solution)/shard_map/all_to_all | solution.py:17
  25.6 1.7 %fusion.17 = f32[512,64]{0,1:T(8,128)S(1)} fusion(bf16[512,2048]{1,0:T(8,128)(2,1)S(1)} %copy-done, bf16[64,2048]{1,0:T(8,128)(2,1)} %sig_ref.1), kind=kOutput, calls=%fused_computation.46 | convolution fusion | flops 134217728 | bytes 2490368 | tf_op jit(solution)/shard_map/dot_general | solution.py:98
  27.3 0.8 copy.48
  28.2 21.2 %all-to-all-done = bf16[64,16,128]{2,1,0:T(8,128)(2,1)S(1)} async-done(((bf16[64,16,128]{2,1,0:T(8,128)(2,1)}), bf16[64,16,128]{2,1,0:T(8,128)(2,1)S(1)}, u32[]{:S(2)}, u32[]{:S(2)}) %all-to-all-start) | async-done | bytes 262176 | tf_op jit(solution)/shard_map/all_to_all | solution.py:17
  49.4 0.1 fusion.14
  49.5 0.0 copy-start.2
  49.6 0.0 copy-start.6
  49.6 0.1 pad_maximum_fusion
  49.7 0.9 fusion.13
  50.5 0.2 fusion.7
  50.7 0.4 copy-done.2
  51.1 0.8 fusion.4
  52.0 0.8 reshape.34
  52.7 4.2 %all-to-all-start.1 = ((f32[64,1,192]{2,1,0:T(1,128)}), f32[64,1,192]{2,1,0:T(1,128)S(1)}, u32[]{:S(2)}, u32[]{:S(2)}) async-start(f32[64,1,192]{2,1,0:T(1,128)} %reshape.34), calls=%async_computation.1 | async-start | bytes 131072 | tf_op jit(solution)/shard_map/all_to_all | solution.py:17
  56.9 0.1 pad_add_fusion.place_ref
  57.0 0.8 copy.40
  57.8 0.8 copy.47
  58.7 1.5 shard_map.76
  60.2 2.4 %collective-permute-start = (bf16[128,1024]{1,0:T(8,128)(2,1)S(1)}, bf16[128,1024]{1,0:T(8,128)(2,1)S(1)}, u32[]{:S(2)}, u32[]{:S(2)}) collective-permute-start(bf16[128,1024]{1,0:T(8,128)(2,1)S(1)} %get-tuple-element.18), channel_id=1, source_target_pairs={{0,1},{1,0},{2,3},{3,2},{4,5},{5,4},{6,7},{7,6},{8,9},{9,8},{10,11... | collective-permute-start | bytes 786440 | tf_op jit(solution)/shard_map/ppermute | solution.py:107
  62.6 10.1 %all-to-all-done.1 = f32[64,1,192]{2,1,0:T(1,128)S(1)} async-done(((f32[64,1,192]{2,1,0:T(1,128)}), f32[64,1,192]{2,1,0:T(1,128)S(1)}, u32[]{:S(2)}, u32[]{:S(2)}) %all-to-all-start.1) | async-done | bytes 49184 | tf_op jit(solution)/shard_map/all_to_all | solution.py:17
  72.6 0.7 broadcast_in_dim.8
  73.3 7.0 %all-to-all-start.2 = ((f32[16,3,512]{2,1,0:T(4,128)}), f32[16,3,512]{2,1,0:T(4,128)S(1)}, u32[]{:S(2)}, u32[]{:S(2)}) async-start(f32[16,3,512]{2,1,0:T(4,128)} %broadcast_in_dim.8), calls=%async_computation.2 | async-start | bytes 262144 | tf_op jit(solution)/shard_map/all_to_all | solution.py:17
  80.3 0.5 broadcast.16
  80.8 2.3 %reduce.6 = f32[64,192]{1,0:T(8,128)} reduce(f32[64,1,192]{2,1,0:T(1,128)} %copy-done.7, f32[]{:T(128)} %broadcast.16), dimensions={1}, to_apply=%all_to_all.13.reduce_sub_computation | reduce | bytes 98308 | tf_op jit(solution)/shard_map/all_to_all | solution.py:17
  83.0 1.6 %reshape.35 = f32[64,3,64]{2,1,0:T(4,128)} reshape(f32[64,192]{1,0:T(8,128)} %reduce.6) | data formatting | bytes 98304
  84.6 1.8 %fusion.15 = (f32[64,1,64]{2,1,0:T(1,128)}, f32[64,1,64]{2,1,0:T(1,128)}, f32[64,1,64]{2,1,0:T(1,128)}) fusion(f32[64,3,64]{2,1,0:T(4,128)} %reshape.35), kind=kLoop, calls=%fused_computation.44 | loop fusion | bytes 98304 | tf_op jit(solution)/shard_map/slice | solution.py:21
  86.4 0.8 reduce_max.37
  87.2 0.8 multiply_reduce_fusion.1
  88.0 0.7 all-to-all-done.2
  88.7 0.0 collective-permute-done.far_w_ref
  88.9 0.0 copy-start.3
  88.9 1.3 bitcast_convert_fusion
  90.2 0.0 copy-done.4
  90.2 1.2 fusion.3
  91.5 0.1 pad_maximum_fusion.2.own_ref
  91.6 0.5 fusion
  92.1 0.5 fusion.1
  92.6 1.0 copy.49
  93.6 7.4 %all-to-all-start.3 = ((bf16[64,32,128]{2,1,0:T(8,128)(2,1)}), bf16[64,32,128]{2,1,0:T(8,128)(2,1)S(1)}, u32[]{:S(2)}, u32[]{:S(2)}) async-start(bf16[64,32,128]{2,1,0:T(8,128)(2,1)} %bitcast.74), calls=%async_computation.3 | async-start | bytes 1048576 | tf_op jit(solution)/shard_map/all_to_all | solution.py:144
  101.0 1.9 %collective-permute-start.1 = (bf16[512,128]{1,0:T(8,128)(2,1)S(1)}, bf16[512,128]{1,0:T(8,128)(2,1)S(1)}, u32[]{:S(2)}, u32[]{:S(2)}) collective-permute-start(bf16[512,128]{1,0:T(8,128)(2,1)S(1)} %pad_maximum_fusion.2.own_ref), channel_id=1, source_target_pairs={{0,1},{1,0},{2,3},{3,2},{4,5},{5,4},{6,7},{7,6},{8,9},{9,8},{10,11... | collective-permute-start | bytes 393224 | tf_op jit(solution)/shard_map/ppermute | solution.py:135
  103.0 5.3 %collective-permute-done.1.far_ref = bf16[512,128]{1,0:T(8,128)(2,1)S(1)} collective-permute-done((bf16[512,128]{1,0:T(8,128)(2,1)S(1)}, bf16[512,128]{1,0:T(8,128)(2,1)S(1)}, u32[]{:S(2)}, u32[]{:S(2)}) %collective-permute-start.1) | collective-permute-done | bytes 131104 | tf_op jit(solution)/shard_map/ppermute | solution.py:135
  108.3 0.7 shard_map.77
  109.0 1.9 %collective-permute-start.2 = (bf16[512,128]{1,0:T(8,128)(2,1)S(1)}, bf16[512,128]{1,0:T(8,128)(2,1)S(1)}, u32[]{:S(2)}, u32[]{:S(2)}) collective-permute-start(bf16[512,128]{1,0:T(8,128)(2,1)S(1)} %get-tuple-element.24), channel_id=1, source_target_pairs={{0,2},{2,4},{4,6},{6,8},{8,10},{10,12},{12,14},{14,0},{1,3},{3,5},... | collective-permute-start | bytes 393224 | tf_op jit(solution)/shard_map/ppermute | solution.py:150
  110.9 3.6 %collective-permute-start.3 = (bf16[512,128]{1,0:T(8,128)(2,1)S(1)}, bf16[512,128]{1,0:T(8,128)(2,1)S(1)}, u32[]{:S(2)}, u32[]{:S(2)}) collective-permute-start(bf16[512,128]{1,0:T(8,128)(2,1)S(1)} %get-tuple-element.25), channel_id=1, source_target_pairs={{0,4},{2,6},{4,8},{6,10},{8,12},{10,14},{12,0},{14,2},{1,5},{3,7},... | collective-permute-start | bytes 393224 | tf_op jit(solution)/shard_map/ppermute | solution.py:150
  114.5 4.3 %collective-permute-start.4 = (bf16[512,128]{1,0:T(8,128)(2,1)S(1)}, bf16[512,128]{1,0:T(8,128)(2,1)S(1)}, u32[]{:S(2)}, u32[]{:S(2)}) collective-permute-start(bf16[512,128]{1,0:T(8,128)(2,1)S(1)} %get-tuple-element.26), channel_id=1, source_target_pairs={{0,6},{2,8},{4,10},{6,12},{8,14},{10,0},{12,2},{14,4},{1,7},{3,9},... | collective-permute-start | bytes 393224 | tf_op jit(solution)/shard_map/ppermute | solution.py:150
  118.8 4.0 %collective-permute-start.5 = (bf16[512,128]{1,0:T(8,128)(2,1)S(1)}, bf16[512,128]{1,0:T(8,128)(2,1)S(1)}, u32[]{:S(2)}, u32[]{:S(2)}) collective-permute-start(bf16[512,128]{1,0:T(8,128)(2,1)S(1)} %get-tuple-element.27), channel_id=1, source_target_pairs={{0,8},{2,10},{4,12},{6,14},{8,0},{10,2},{12,4},{14,6},{1,9},{3,11}... | collective-permute-start | bytes 393224 | tf_op jit(solution)/shard_map/ppermute | solution.py:150
  122.8 4.3 %collective-permute-start.6 = (bf16[512,128]{1,0:T(8,128)(2,1)S(1)}, bf16[512,128]{1,0:T(8,128)(2,1)S(1)}, u32[]{:S(2)}, u32[]{:S(2)}) collective-permute-start(bf16[512,128]{1,0:T(8,128)(2,1)S(1)} %get-tuple-element.28), channel_id=1, source_target_pairs={{0,10},{2,12},{4,14},{6,0},{8,2},{10,4},{12,6},{14,8},{1,11},{3,13... | collective-permute-start | bytes 393224 | tf_op jit(solution)/shard_map/ppermute | solution.py:150
  127.2 0.0 collective-permute-done.2
  127.2 5.2 %collective-permute-start.7 = (bf16[512,128]{1,0:T(8,128)(2,1)S(1)}, bf16[512,128]{1,0:T(8,128)(2,1)S(1)}, u32[]{:S(2)}, u32[]{:S(2)}) collective-permute-start(bf16[512,128]{1,0:T(8,128)(2,1)S(1)} %get-tuple-element.29), channel_id=1, source_target_pairs={{0,12},{2,14},{4,0},{6,2},{8,4},{10,6},{12,8},{14,10},{1,13},{3,15... | collective-permute-start | bytes 393224 | tf_op jit(solution)/shard_map/ppermute | solution.py:150
  132.4 0.0 collective-permute-done.3
  132.4 3.1 %collective-permute-start.8 = (bf16[512,128]{1,0:T(8,128)(2,1)S(1)}, bf16[512,128]{1,0:T(8,128)(2,1)S(1)}, u32[]{:S(2)}, u32[]{:S(2)}) collective-permute-start(bf16[512,128]{1,0:T(8,128)(2,1)S(1)} %get-tuple-element.30), channel_id=1, source_target_pairs={{0,14},{2,0},{4,2},{6,4},{8,6},{10,8},{12,10},{14,12},{1,15},{3,1}... | collective-permute-start | bytes 393224 | tf_op jit(solution)/shard_map/ppermute | solution.py:150
  135.5 0.0 collective-permute-done.4
  135.5 0.0 collective-permute-done.5
  135.5 5.0 %collective-permute-done.6 = bf16[512,128]{1,0:T(8,128)(2,1)S(1)} collective-permute-done((bf16[512,128]{1,0:T(8,128)(2,1)S(1)}, bf16[512,128]{1,0:T(8,128)(2,1)S(1)}, u32[]{:S(2)}, u32[]{:S(2)}) %collective-permute-start.6) | collective-permute-done | bytes 131104 | tf_op jit(solution)/shard_map/ppermute | solution.py:150
  140.5 5.9 %collective-permute-done.7 = bf16[512,128]{1,0:T(8,128)(2,1)S(1)} collective-permute-done((bf16[512,128]{1,0:T(8,128)(2,1)S(1)}, bf16[512,128]{1,0:T(8,128)(2,1)S(1)}, u32[]{:S(2)}, u32[]{:S(2)}) %collective-permute-start.7) | collective-permute-done | bytes 131104 | tf_op jit(solution)/shard_map/ppermute | solution.py:150
  146.4 1.1 collective-permute-done.8
  147.5 0.8 add_convert_fusion
  148.3 0.0 all-to-all-done.3
  148.3 0.1 convert_reduce_fusion
  148.4 0.7 fusion.12
  (22 shorter events, 0.2 us)
Async XLA Ops:
  0.6 25.0 %copy-start = (bf16[512,2048]{1,0:T(8,128)(2,1)S(1)}, bf16[512,2048]{1,0:T(8,128)(2,1)}, u32[]{:S(2)}) copy-start(bf16[512,2048]{1,0:T(8,128)(2,1)} %param.5) | copy-start | bytes 6291460
  2.3 47.1 %all-to-all-start = ((bf16[64,16,128]{2,1,0:T(8,128)(2,1)}), bf16[64,16,128]{2,1,0:T(8,128)(2,1)S(1)}, u32[]{:S(2)}, u32[]{:S(2)}) async-start(bf16[64,16,128]{2,1,0:T(8,128)(2,1)} %broadcast_in_dim.6), calls=%async_computation | async-start | bytes 524288 | tf_op jit(solution)/shard_map/all_to_all | solution.py:17
  49.5 1.6 %copy-start.2 = (bf16[512,2048]{1,0:T(8,128)(2,1)S(1)}, bf16[512,2048]{1,0:T(8,128)(2,1)}, u32[]{:S(2)}) copy-start(bf16[512,2048]{1,0:T(8,128)(2,1)} %param.9) | copy-start | bytes 6291460
  49.6 1.6 %copy-start.6 = (bf16[64,2048]{1,0:T(8,128)(2,1)S(1)}, bf16[64,2048]{1,0:T(8,128)(2,1)}, u32[]{:S(2)}) copy-start(bf16[64,2048]{1,0:T(8,128)(2,1)} %param.7) | copy-start | bytes 786436
  50.5 8.1 %copy-start.1 = (bf16[64,2048]{1,0:T(8,128)(2,1)S(1)}, bf16[64,2048]{1,0:T(8,128)(2,1)}, u32[]{:S(2)}) copy-start(bf16[64,2048]{1,0:T(8,128)(2,1)} %sig_ref.1) | copy-start | bytes 786436
  52.7 19.9 %all-to-all-start.1 = ((f32[64,1,192]{2,1,0:T(1,128)}), f32[64,1,192]{2,1,0:T(1,128)S(1)}, u32[]{:S(2)}, u32[]{:S(2)}) async-start(f32[64,1,192]{2,1,0:T(1,128)} %reshape.34), calls=%async_computation.1 | async-start | bytes 131072 | tf_op jit(solution)/shard_map/all_to_all | solution.py:17
  60.2 30.0 %copy-start.4 = (f32[64,512]{0,1:T(8,128)S(1)}, f32[64,512]{0,1:T(8,128)}, u32[]{:S(2)}) copy-start(f32[64,512]{0,1:T(8,128)} %copy.40) | copy-start | bytes 393220
  60.2 30.0 %copy-start.5 = (f32[512,64]{1,0:T(8,128)S(1)}, f32[512,64]{1,0:T(8,128)}, u32[]{:S(2)}) copy-start(f32[512,64]{1,0:T(8,128)} %copy.47) | copy-start | bytes 393220
  60.2 28.6 %collective-permute-start = (bf16[128,1024]{1,0:T(8,128)(2,1)S(1)}, bf16[128,1024]{1,0:T(8,128)(2,1)S(1)}, u32[]{:S(2)}, u32[]{:S(2)}) collective-permute-start(bf16[128,1024]{1,0:T(8,128)(2,1)S(1)} %get-tuple-element.18), channel_id=1, source_target_pairs={{0,1},{1,0},{2,3},{3,2},{4,5},{5,4},{6,7},{7,6},{8,9},{9,8},{10,11... | collective-permute-start | bytes 786440 | tf_op jit(solution)/shard_map/ppermute | solution.py:107
  72.6 0.7 copy-start.7
  73.3 15.4 %all-to-all-start.2 = ((f32[16,3,512]{2,1,0:T(4,128)}), f32[16,3,512]{2,1,0:T(4,128)S(1)}, u32[]{:S(2)}, u32[]{:S(2)}) async-start(f32[16,3,512]{2,1,0:T(4,128)} %broadcast_in_dim.8), calls=%async_computation.2 | async-start | bytes 262144 | tf_op jit(solution)/shard_map/all_to_all | solution.py:17
  88.9 3.2 %copy-start.3 = (bf16[512,2048]{1,0:T(8,128)(2,1)S(1)}, bf16[512,2048]{1,0:T(8,128)(2,1)}, u32[]{:S(2)}) copy-start(bf16[512,2048]{1,0:T(8,128)(2,1)} %param.9) | copy-start | bytes 6291460
  93.6 54.7 %all-to-all-start.3 = ((bf16[64,32,128]{2,1,0:T(8,128)(2,1)}), bf16[64,32,128]{2,1,0:T(8,128)(2,1)S(1)}, u32[]{:S(2)}, u32[]{:S(2)}) async-start(bf16[64,32,128]{2,1,0:T(8,128)(2,1)} %bitcast.74), calls=%async_computation.3 | async-start | bytes 1048576 | tf_op jit(solution)/shard_map/all_to_all | solution.py:144
  101.0 7.2 %collective-permute-start.1 = (bf16[512,128]{1,0:T(8,128)(2,1)S(1)}, bf16[512,128]{1,0:T(8,128)(2,1)S(1)}, u32[]{:S(2)}, u32[]{:S(2)}) collective-permute-start(bf16[512,128]{1,0:T(8,128)(2,1)S(1)} %pad_maximum_fusion.2.own_ref), channel_id=1, source_target_pairs={{0,1},{1,0},{2,3},{3,2},{4,5},{5,4},{6,7},{7,6},{8,9},{9,8},{10,11... | collective-permute-start | bytes 393224 | tf_op jit(solution)/shard_map/ppermute | solution.py:135
  109.0 18.2 %collective-permute-start.2 = (bf16[512,128]{1,0:T(8,128)(2,1)S(1)}, bf16[512,128]{1,0:T(8,128)(2,1)S(1)}, u32[]{:S(2)}, u32[]{:S(2)}) collective-permute-start(bf16[512,128]{1,0:T(8,128)(2,1)S(1)} %get-tuple-element.24), channel_id=1, source_target_pairs={{0,2},{2,4},{4,6},{6,8},{8,10},{10,12},{12,14},{14,0},{1,3},{3,5},... | collective-permute-start | bytes 393224 | tf_op jit(solution)/shard_map/ppermute | solution.py:150
  110.9 21.5 %collective-permute-start.3 = (bf16[512,128]{1,0:T(8,128)(2,1)S(1)}, bf16[512,128]{1,0:T(8,128)(2,1)S(1)}, u32[]{:S(2)}, u32[]{:S(2)}) collective-permute-start(bf16[512,128]{1,0:T(8,128)(2,1)S(1)} %get-tuple-element.25), channel_id=1, source_target_pairs={{0,4},{2,6},{4,8},{6,10},{8,12},{10,14},{12,0},{14,2},{1,5},{3,7},... | collective-permute-start | bytes 393224 | tf_op jit(solution)/shard_map/ppermute | solution.py:150
  114.5 20.9 %collective-permute-start.4 = (bf16[512,128]{1,0:T(8,128)(2,1)S(1)}, bf16[512,128]{1,0:T(8,128)(2,1)S(1)}, u32[]{:S(2)}, u32[]{:S(2)}) collective-permute-start(bf16[512,128]{1,0:T(8,128)(2,1)S(1)} %get-tuple-element.26), channel_id=1, source_target_pairs={{0,6},{2,8},{4,10},{6,12},{8,14},{10,0},{12,2},{14,4},{1,7},{3,9},... | collective-permute-start | bytes 393224 | tf_op jit(solution)/shard_map/ppermute | solution.py:150
  118.8 16.6 %collective-permute-start.5 = (bf16[512,128]{1,0:T(8,128)(2,1)S(1)}, bf16[512,128]{1,0:T(8,128)(2,1)S(1)}, u32[]{:S(2)}, u32[]{:S(2)}) collective-permute-start(bf16[512,128]{1,0:T(8,128)(2,1)S(1)} %get-tuple-element.27), channel_id=1, source_target_pairs={{0,8},{2,10},{4,12},{6,14},{8,0},{10,2},{12,4},{14,6},{1,9},{3,11}... | collective-permute-start | bytes 393224 | tf_op jit(solution)/shard_map/ppermute | solution.py:150
  122.8 17.6 %collective-permute-start.6 = (bf16[512,128]{1,0:T(8,128)(2,1)S(1)}, bf16[512,128]{1,0:T(8,128)(2,1)S(1)}, u32[]{:S(2)}, u32[]{:S(2)}) collective-permute-start(bf16[512,128]{1,0:T(8,128)(2,1)S(1)} %get-tuple-element.28), channel_id=1, source_target_pairs={{0,10},{2,12},{4,14},{6,0},{8,2},{10,4},{12,6},{14,8},{1,11},{3,13... | collective-permute-start | bytes 393224 | tf_op jit(solution)/shard_map/ppermute | solution.py:150
  127.2 19.2 %collective-permute-start.7 = (bf16[512,128]{1,0:T(8,128)(2,1)S(1)}, bf16[512,128]{1,0:T(8,128)(2,1)S(1)}, u32[]{:S(2)}, u32[]{:S(2)}) collective-permute-start(bf16[512,128]{1,0:T(8,128)(2,1)S(1)} %get-tuple-element.29), channel_id=1, source_target_pairs={{0,12},{2,14},{4,0},{6,2},{8,4},{10,6},{12,8},{14,10},{1,13},{3,15... | collective-permute-start | bytes 393224 | tf_op jit(solution)/shard_map/ppermute | solution.py:150
  132.4 15.1 %collective-permute-start.8 = (bf16[512,128]{1,0:T(8,128)(2,1)S(1)}, bf16[512,128]{1,0:T(8,128)(2,1)S(1)}, u32[]{:S(2)}, u32[]{:S(2)}) collective-permute-start(bf16[512,128]{1,0:T(8,128)(2,1)S(1)} %get-tuple-element.30), channel_id=1, source_target_pairs={{0,14},{2,0},{4,2},{6,4},{8,6},{10,8},{12,10},{14,12},{1,15},{3,1}... | collective-permute-start | bytes 393224 | tf_op jit(solution)/shard_map/ppermute | solution.py:150
  148.4 0.7 copy-start.8

commit v4 on v3

v4 whole, which is shorter than its diff:
```python
import jax
import jax.numpy as jnp
from jax import lax
from jax.experimental import pallas as pl
from jax.experimental.pallas import tpu as pltpu
from jax.sharding import PartitionSpec as P

BF = jnp.bfloat16
F32 = jnp.float32
GROUP = 4


def gather_blocks(block, axis, n):
    spread = jnp.broadcast_to(block[None], (n,) + block.shape)
    return lax.all_to_all(spread, axis, 0, 0, tiled=True)


def merge_stats(got):
    peak, total, dot = got[:, 0], got[:, 1], got[:, 2]
    top = jnp.max(peak, axis=0)
    scale = jnp.exp(peak - top[None, :])
    total = jnp.sum(total * scale, axis=0)
    dot = jnp.sum(dot * scale, axis=0)
    return top, total, dot / total


def weights_kernel(place_ref, sig_ref, phi_ref, *out_refs):
    slots = sig_ref.shape[0]
    wide = out_refs[0].shape[1]
    for k, out_ref in enumerate(out_refs):
        block = jnp.bitwise_xor(place_ref[0], k)
        at = pl.ds(pl.multiple_of(block * wide, wide), wide)
        out_ref[:slots] = sig_ref[:, at]
        out_ref[slots:] = phi_ref[at, :].T


def split_weights(place, sig, phi_full, n, wide):
    slots, width = sig.shape
    spec = pl.BlockSpec((2 * slots, wide), lambda i, at: (0, i))
    return pl.pallas_call(
        weights_kernel,
        grid_spec=pltpu.PrefetchScalarGridSpec(
            num_scalar_prefetch=1,
            grid=(n,),
            in_specs=[
                pl.BlockSpec((slots, GROUP * wide), lambda i, at: (0, lax.rem(i + at[1], n))),
                pl.BlockSpec((GROUP * wide, slots), lambda i, at: (lax.rem(i + at[1], n), 0)),
            ],
            out_specs=[spec] * GROUP,
        ),
        out_shape=[jax.ShapeDtypeStruct((2 * slots, n * wide), BF)] * GROUP,
        cost_estimate=pl.CostEstimate(
            flops=4 * slots * width, bytes_accessed=8 * slots * width, transcendentals=0
        ),
        compiler_params=pltpu.CompilerParams(vmem_limit_bytes=32 * 1024 * 1024),
    )(place, sig, phi_full)


def blocks_kernel(*refs):
    factors, weights, out_refs = refs[:GROUP], refs[GROUP : 2 * GROUP], refs[2 * GROUP :]
    for i, out_ref in enumerate(out_refs):
        wide = out_ref.shape[1]
        at = slice(i * wide, (i + 1) * wide)
        acc = jnp.dot(factors[0][...], weights[0][:, at], preferred_element_type=F32)
        for f, w in zip(factors[1:], weights[1:]):
            acc = acc + jnp.dot(f[...], w[:, at], preferred_element_type=F32)
        out_ref[...] = acc.astype(BF)


def column_blocks(factors, weights, n, wide):
    rows, depth = factors[0].shape
    return pl.pallas_call(
        blocks_kernel,
        out_shape=[jax.ShapeDtypeStruct((rows, wide), BF)] * n,
        cost_estimate=pl.CostEstimate(
            flops=2 * GROUP * n * rows * depth * wide,
            bytes_accessed=2 * (GROUP * depth * (rows + n * wide) + n * rows * wide),
            transcendentals=0,
        ),
        compiler_params=pltpu.CompilerParams(vmem_limit_bytes=32 * 1024 * 1024),
    )(*factors, *weights)


def make_per_device(n_seq, n_exp):
    groups = n_exp // GROUP

    def swap(x, k):
        return lax.ppermute(x, "exp", [(j, j ^ k) for j in range(n_exp)])

    def per_device(tokens, phi, expert_out, slot_in_grad, out_grad):
        rows, width = tokens.shape
        slots = expert_out.shape[0]
        wide = width // n_exp
        half = phi.shape[0] // 2
        packed = jnp.concatenate([phi[:half], phi[half:]], axis=1)
        got_phi = gather_blocks(packed, "seq", n_seq)
        phi_full = jnp.concatenate([got_phi[:, :, :slots], got_phi[:, :, slots:]], axis=1)
        phi_full = phi_full.reshape(width, slots)

        logits = jnp.dot(tokens, phi_full, preferred_element_type=F32)
        disp_grad = lax.dot_general(
            tokens, slot_in_grad, (((1,), (1,)), ((), ())), preferred_element_type=F32
        )
        comb_grad = lax.dot_general(
            out_grad, expert_out, (((1,), (1,)), ((), ())), preferred_element_type=F32
        )

        rank = lax.axis_index("exp")
        place = jnp.stack([lax.rem(rank, GROUP), lax.div(rank, GROUP)]).astype(jnp.int32)
        weights = split_weights(place, slot_in_grad, phi_full, groups, wide)
        weights = [weights[0]] + [swap(weights[k], k) for k in range(1, GROUP)]

        row_top = jnp.max(logits, axis=1)
        row_exp = jnp.exp(logits - row_top[:, None])
        row_stats = jnp.stack(
            [row_top, jnp.sum(row_exp, axis=1), jnp.sum(row_exp * comb_grad, axis=1)]
        )
        col_top = jnp.max(logits, axis=0)
        col_exp = jnp.exp(logits - col_top[None, :])
        col_stats = jnp.stack(
            [col_top, jnp.sum(col_exp, axis=0), jnp.sum(col_exp * disp_grad, axis=0)]
        )

        col_stats = jnp.pad(col_stats, ((0, 0), (0, -slots % 128)))
        col_got = gather_blocks(col_stats, "seq", n_seq)
        row_stats, col_got, weights = lax.optimization_barrier((row_stats, col_got, weights))
        row_got = gather_blocks(row_stats, "exp", n_exp)
        col_peak, col_total, col_dot = merge_stats(col_got[:, :, :slots])
        row_peak, row_total, row_dot = merge_stats(row_got)

        combine = jnp.exp(logits - row_peak[:, None]) / row_total[:, None]
        dispatch = jnp.exp(logits - col_peak[None, :]) / col_total[None, :]
        combine_b = combine.astype(BF)
        logit_grad = (
            combine * (comb_grad - row_dot[:, None]) + dispatch * (disp_grad - col_dot[None, :])
        ).astype(BF)

        own = jnp.concatenate([dispatch.astype(BF), logit_grad], axis=1)
        own, logit_grad, combine_b = lax.optimization_barrier((own, logit_grad, combine_b))
        factors = [own] + [swap(own, k) for k in range(1, GROUP)]
        slot_term = lax.dot_general(
            out_grad, combine_b, (((0,), (0,)), ((), ())), preferred_element_type=F32
        ).astype(BF)

        phi_term = lax.dot_general(
            tokens, logit_grad, (((0,), (0,)), ((), ())), preferred_element_type=F32
        ).astype(BF)
        both = jnp.concatenate([phi_term, slot_term], axis=1)
        got = lax.all_to_all(both.reshape(n_seq, -1, 2 * slots), "seq", 0, 0, tiled=True)

        blocks = column_blocks(factors, weights, groups, wide)
        token_sum = blocks[0].astype(F32)
        for i in range(1, groups):
            turn = [(j, (j + i * GROUP) % n_exp) for j in range(n_exp)]
            token_sum = token_sum + lax.ppermute(blocks[i], "exp", turn).astype(F32)
        token_grad = token_sum.astype(BF)

        total = jnp.sum(got.astype(F32), axis=0)
        phi_grad = total[:, :slots]
        slot_grad = total[:, slots:].T.astype(BF)
        return (token_grad, phi_grad, slot_grad)

    return per_device


def solution(mesh):
    return jax.shard_map(
        make_per_device(mesh.shape["seq"], mesh.shape["exp"]),
        mesh=mesh,
        in_specs=(P("seq", None), P("seq", "exp"), P("exp", None), P("exp", None), P("seq", None)),
        out_specs=(P("seq", "exp"), P("seq", "exp"), P("exp", "seq")),
        check_vma=False,
    )
```

time: 151 us -> 148 us (0.980)
  other arithmetic: 8 us -> 3.3 us
  starting transfers between devices: 72.5 us -> 75.1 us
  local copies, waits for them, and re-layouts: 11.8 us -> 10.2 us
    all_to_all x1, starting transfers between devices: 7.4 us -> 13.2 us  [per_device(): lax.all_to_all(both.reshape(n_seq, -1, 2 * slots), 'seq', 0, 0, tiled=True)]
    ppermute x9, starting transfers between devices: 30.7 us -> 26.6 us  [the longest x6 16.7 us: swap(): return lax.ppermute(x, 'exp', [(j, j ^ k) for j in range(n_exp)])]
    unnamed x20 -> x10, local copies, waits for them, and re-layouts: 2.79 us -> 0.03 us
    all_to_all x1 -> x0, other arithmetic: 2.26 us -> none  [gather_blocks(): return lax.all_to_all(spread, axis, 0, 0, tiled=True)]
    all_to_all x3, waiting for transfers between devices: 32 us -> 33.6 us  [gather_blocks(): return lax.all_to_all(spread, axis, 0, 0, tiled=True)]
    dot_general x1, matrix products: 0.78 us -> 2.35 us  [per_device(): lax.dot_general(out_grad, expert_out, (((1,), (1,)), ((), ())), preferred...]
  transfers between devices with their start and end apart: 13 -> 13, of which waited for: 7 -> 8; matrix products, arithmetic and copies ran while one was open for 9% -> 5% of each run, Pallas kernels for 1% -> 1%
where the time goes in v4:
time: 148 us
  starting transfers between devices  75.1 us (51%)
  waiting for transfers between devices  50.5 us (34%)
  local copies, waits for them, and re-layouts  10.2 us (7%)
  matrix products  5.73 us (4%)
  other arithmetic  3.3 us (2%)
  Pallas kernels  1.82 us (1%)
    all_to_all x3, starting transfers between devices, gather_blocks(): return lax.all_to_all(spread, axis, 0, 0, tiled=True)  35.2 us
    all_to_all x3, waiting for transfers between devices, gather_blocks(): return lax.all_to_all(spread, axis, 0, 0, tiled=True)  33.6 us
    ppermute x6, starting transfers between devices, swap(): return lax.ppermute(x, 'exp', [(j, j ^ k) for j in range(n_exp)])  16.7 us
    all_to_all x1, starting transfers between devices, per_device(): lax.all_to_all(both.reshape(n_seq, -1, 2 * slots), 'seq', 0, 0, tiled=True)  13.2 us
    ppermute x3, waiting for transfers between devices, per_device(): token_sum = token_sum + lax.ppermute(blocks[i], 'exp', turn).astype(F32)  11.9 us
    ppermute x3, starting transfers between devices, per_device(): token_sum = token_sum + lax.ppermute(blocks[i], 'exp', turn).astype(F32)  9.87 us
    ppermute x6, waiting for transfers between devices, swap(): return lax.ppermute(x, 'exp', [(j, j ^ k) for j in range(n_exp)])  4.99 us
  transfers between devices with their start and end apart: 13, of which 8 were waited for; matrix products, arithmetic and copies ran while one was open for 5% of the time, Pallas kernels for 1%

profile of v4, /device:TPU:1, one launch (start us, length us, event | category | flops | bytes accessed | tf_op | source)
XLA Modules:
  0.0 147.6 jit_solution(16509473417523027013)
XLA Ops:
  0.6 0.0 copy-start
  0.6 0.9 fusion.20
  1.5 0.1 pad_maximum_fusion.4
  1.6 0.7 broadcast_in_dim.6
  2.3 23.3 %all-to-all-start = ((bf16[64,16,128]{2,1,0:T(8,128)(2,1)}), bf16[64,16,128]{2,1,0:T(8,128)(2,1)S(1)}, u32[]{:S(2)}, u32[]{:S(2)}) async-start(bf16[64,16,128]{2,1,0:T(8,128)(2,1)} %broadcast_in_dim.6), calls=%async_computation | async-start | bytes 524288 | tf_op jit(solution)/shard_map/all_to_all | solution.py:15
  25.6 2.4 %fusion.21 = f32[512,64]{0,1:T(8,128)S(1)} fusion(bf16[512,2048]{1,0:T(8,128)(2,1)} %param.9, bf16[64,2048]{1,0:T(8,128)(2,1)} %param.7), kind=kOutput, calls=%fused_computation.53 | convolution fusion | flops 134217728 | bytes 2490368 | tf_op jit(solution)/shard_map/dot_general | solution.py:104
  27.9 0.0 copy-start.3
  28.0 21.4 %all-to-all-done = bf16[64,16,128]{2,1,0:T(8,128)(2,1)S(1)} async-done(((bf16[64,16,128]{2,1,0:T(8,128)(2,1)}), bf16[64,16,128]{2,1,0:T(8,128)(2,1)S(1)}, u32[]{:S(2)}, u32[]{:S(2)}) %all-to-all-start) | async-done | bytes 262176 | tf_op jit(solution)/shard_map/all_to_all | solution.py:15
  49.4 0.1 fusion.18
  49.5 0.0 copy-start.1
  49.6 0.1 pad_maximum_fusion
  49.7 0.0 copy-done
  49.7 0.9 fusion.17
  50.5 0.2 fusion.7
  50.7 0.0 copy-done.1
  50.7 1.5 %fusion.4 = (f32[64]{0:T(128)S(1)}, f32[512]{0:T(512)S(1)}, f32[512,64]{0,1:T(8,128)}) fusion(f32[64,512]{1,0:T(8,128)S(1)} %get-tuple-element.57, f32[64]{0:T(128)S(1)} %get-tuple-element.41, f32[512,64]{0,1:T(8,128)S(1)} %fusion.21, f32[512]{0:T(512)S(1)} %get-tuple-element.42, bf16[512,2048]{1,0:T(8,128)(2,1)S(1)} %copy-done, ...), kind=kOutput, calls=%fused_computation.18 | convolution fusion | flops 134413760 | bytes 2757120 | tf_op jit(solution)/shard_map/dot_general | solution.py:101
  52.3 0.7 broadcast_in_dim.7
  52.9 5.0 %all-to-all-start.1 = ((f32[64,3,128]{2,1,0:T(4,128)}), f32[64,3,128]{2,1,0:T(4,128)}, u32[]{:S(2)}, u32[]{:S(2)}) async-start(f32[64,3,128]{2,1,0:T(4,128)} %broadcast_in_dim.7), calls=%async_computation.1 | async-start | bytes 262144 | tf_op jit(solution)/shard_map/all_to_all | solution.py:15
  58.0 0.0 copy-done.3
  58.0 0.1 pad_add_fusion.place_ref
  58.0 1.1 shard_map.76
  59.2 2.2 %collective-permute-start = (bf16[128,512]{1,0:T(8,128)(2,1)S(1)}, bf16[128,512]{1,0:T(8,128)(2,1)S(1)}, u32[]{:S(2)}, u32[]{:S(2)}) collective-permute-start(bf16[128,512]{1,0:T(8,128)(2,1)S(1)} %get-tuple-element.21), channel_id=1, source_target_pairs={{0,1},{1,0},{2,3},{3,2},{4,5},{5,4},{6,7},{7,6},{8,9},{9,8},{10,11... | collective-permute-start | bytes 393224 | tf_op jit(solution)/shard_map/ppermute | solution.py:88
  61.4 3.2 %collective-permute-start.1 = (bf16[128,512]{1,0:T(8,128)(2,1)S(1)}, bf16[128,512]{1,0:T(8,128)(2,1)S(1)}, u32[]{:S(2)}, u32[]{:S(2)}) collective-permute-start(bf16[128,512]{1,0:T(8,128)(2,1)S(1)} %get-tuple-element.22), channel_id=1, source_target_pairs={{0,2},{1,3},{2,0},{3,1},{4,6},{5,7},{6,4},{7,5},{8,10},{9,11},{10,... | collective-permute-start | bytes 393224 | tf_op jit(solution)/shard_map/ppermute | solution.py:88
  64.6 2.9 %collective-permute-start.2 = (bf16[128,512]{1,0:T(8,128)(2,1)S(1)}, bf16[128,512]{1,0:T(8,128)(2,1)S(1)}, u32[]{:S(2)}, u32[]{:S(2)}) collective-permute-start(bf16[128,512]{1,0:T(8,128)(2,1)S(1)} %get-tuple-element.23), channel_id=1, source_target_pairs={{0,3},{1,2},{2,1},{3,0},{4,7},{5,6},{6,5},{7,4},{8,11},{9,10},{10,... | collective-permute-start | bytes 393224 | tf_op jit(solution)/shard_map/ppermute | solution.py:88
  67.6 1.7 %copy.47 = f32[512,64]{1,0:T(8,128)} copy(f32[512,64]{0,1:T(8,128)} %copy-done.3) | data formatting | bytes 262144 | tf_op jit(solution)/shard_map/dot_general | solution.py:104
  69.3 0.1 copy.40
  69.5 1.7 %copy.48 = f32[512,64]{1,0:T(8,128)} copy(f32[512,64]{0,1:T(8,128)} %get-tuple-element.58) | data formatting | bytes 262144 | tf_op jit(solution)/shard_map/dot_general | solution.py:101
  71.2 0.0 collective-permute-done.refs_5_
  71.2 0.0 collective-permute-done.1.refs_6_
  71.2 0.9 collective-permute-done.2.refs_7_
  72.1 3.8 %all-to-all-done.1 = f32[64,3,128]{2,1,0:T(4,128)} async-done(((f32[64,3,128]{2,1,0:T(4,128)}), f32[64,3,128]{2,1,0:T(4,128)}, u32[]{:S(2)}, u32[]{:S(2)}) %all-to-all-start.1) | async-done | bytes 98336 | tf_op jit(solution)/shard_map/all_to_all | solution.py:15
  75.9 0.9 copy.39
  76.8 0.9 slice.50
  77.7 0.7 broadcast_in_dim.8
  78.4 7.0 %all-to-all-start.2 = ((f32[16,3,512]{2,1,0:T(4,128)}), f32[16,3,512]{2,1,0:T(4,128)S(1)}, u32[]{:S(2)}, u32[]{:S(2)}) async-start(f32[16,3,512]{2,1,0:T(4,128)} %broadcast_in_dim.8), calls=%async_computation.2 | async-start | bytes 262144 | tf_op jit(solution)/shard_map/all_to_all | solution.py:15
  85.4 8.4 %all-to-all-done.2 = f32[16,3,512]{2,1,0:T(4,128)S(1)} async-done(((f32[16,3,512]{2,1,0:T(4,128)}), f32[16,3,512]{2,1,0:T(4,128)S(1)}, u32[]{:S(2)}, u32[]{:S(2)}) %all-to-all-start.2) | async-done | bytes 98336 | tf_op jit(solution)/shard_map/all_to_all | solution.py:15
  93.8 0.1 fusion.19
  94.0 0.0 copy-start.2
  94.0 0.2 bitcast_convert_fusion
  94.2 1.4 fusion.3
  95.6 0.1 pad_maximum_fusion.2.refs_0_
  95.8 0.5 fusion
  96.3 0.0 copy-done.2
  96.3 0.5 fusion.1
  96.8 1.0 copy.49
  97.8 13.2 %all-to-all-start.3 = ((bf16[64,32,128]{2,1,0:T(8,128)(2,1)}), bf16[64,32,128]{2,1,0:T(8,128)(2,1)S(1)}, u32[]{:S(2)}, u32[]{:S(2)}) async-start(bf16[64,32,128]{2,1,0:T(8,128)(2,1)} %bitcast.84), calls=%async_computation.3 | async-start | bytes 1048576 | tf_op jit(solution)/shard_map/all_to_all | solution.py:149
  111.1 1.9 %collective-permute-start.3 = (bf16[512,128]{1,0:T(8,128)(2,1)S(1)}, bf16[512,128]{1,0:T(8,128)(2,1)S(1)}, u32[]{:S(2)}, u32[]{:S(2)}) collective-permute-start(bf16[512,128]{1,0:T(8,128)(2,1)S(1)} %pad_maximum_fusion.2.refs_0_), channel_id=1, source_target_pairs={{0,1},{1,0},{2,3},{3,2},{4,5},{5,4},{6,7},{7,6},{8,9},{9,8},{10,11... | collective-permute-start | bytes 393224 | tf_op jit(solution)/shard_map/ppermute | solution.py:88
  113.0 2.0 %collective-permute-start.4 = (bf16[512,128]{1,0:T(8,128)(2,1)S(1)}, bf16[512,128]{1,0:T(8,128)(2,1)S(1)}, u32[]{:S(2)}, u32[]{:S(2)}) collective-permute-start(bf16[512,128]{1,0:T(8,128)(2,1)S(1)} %pad_maximum_fusion.2.refs_0_), channel_id=1, source_target_pairs={{0,2},{1,3},{2,0},{3,1},{4,6},{5,7},{6,4},{7,5},{8,10},{9,11},{10,... | collective-permute-start | bytes 393224 | tf_op jit(solution)/shard_map/ppermute | solution.py:88
  115.0 4.4 %collective-permute-start.5 = (bf16[512,128]{1,0:T(8,128)(2,1)S(1)}, bf16[512,128]{1,0:T(8,128)(2,1)S(1)}, u32[]{:S(2)}, u32[]{:S(2)}) collective-permute-start(bf16[512,128]{1,0:T(8,128)(2,1)S(1)} %pad_maximum_fusion.2.refs_0_), channel_id=1, source_target_pairs={{0,3},{1,2},{2,1},{3,0},{4,7},{5,6},{6,5},{7,4},{8,11},{9,10},{10,... | collective-permute-start | bytes 393224 | tf_op jit(solution)/shard_map/ppermute | solution.py:88
  119.5 0.0 collective-permute-done.3.refs_1_
  119.5 0.0 collective-permute-done.4.refs_2_
  119.5 4.1 %collective-permute-done.5.refs_3_ = bf16[512,128]{1,0:T(8,128)(2,1)S(1)} collective-permute-done((bf16[512,128]{1,0:T(8,128)(2,1)S(1)}, bf16[512,128]{1,0:T(8,128)(2,1)S(1)}, u32[]{:S(2)}, u32[]{:S(2)}) %collective-permute-start.5) | collective-permute-done | bytes 131104 | tf_op jit(solution)/shard_map/ppermute | solution.py:88
  123.6 0.7 shard_map.77
  124.3 2.7 %collective-permute-start.6 = (bf16[512,128]{1,0:T(8,128)(2,1)S(1)}, bf16[512,128]{1,0:T(8,128)(2,1)S(1)}, u32[]{:S(2)}, u32[]{:S(2)}) collective-permute-start(bf16[512,128]{1,0:T(8,128)(2,1)S(1)} %get-tuple-element.32), channel_id=1, source_target_pairs={{0,4},{1,5},{2,6},{3,7},{4,8},{5,9},{6,10},{7,11},{8,12},{9,13},{1... | collective-permute-start | bytes 393224 | tf_op jit(solution)/shard_map/ppermute | solution.py:155
  127.0 4.1 %collective-permute-start.7 = (bf16[512,128]{1,0:T(8,128)(2,1)S(1)}, bf16[512,128]{1,0:T(8,128)(2,1)S(1)}, u32[]{:S(2)}, u32[]{:S(2)}) collective-permute-start(bf16[512,128]{1,0:T(8,128)(2,1)S(1)} %get-tuple-element.33), channel_id=1, source_target_pairs={{0,8},{1,9},{2,10},{3,11},{4,12},{5,13},{6,14},{7,15},{8,0},{9,1},... | collective-permute-start | bytes 393224 | tf_op jit(solution)/shard_map/ppermute | solution.py:155
  131.1 3.1 %collective-permute-start.8 = (bf16[512,128]{1,0:T(8,128)(2,1)S(1)}, bf16[512,128]{1,0:T(8,128)(2,1)S(1)}, u32[]{:S(2)}, u32[]{:S(2)}) collective-permute-start(bf16[512,128]{1,0:T(8,128)(2,1)S(1)} %get-tuple-element.34), channel_id=1, source_target_pairs={{0,12},{1,13},{2,14},{3,15},{4,0},{5,1},{6,2},{7,3},{8,4},{9,5},{1... | collective-permute-start | bytes 393224 | tf_op jit(solution)/shard_map/ppermute | solution.py:155
  134.2 0.8 collective-permute-done.6
  135.0 3.1 %collective-permute-done.7 = bf16[512,128]{1,0:T(8,128)(2,1)S(1)} collective-permute-done((bf16[512,128]{1,0:T(8,128)(2,1)S(1)}, bf16[512,128]{1,0:T(8,128)(2,1)S(1)}, u32[]{:S(2)}, u32[]{:S(2)}) %collective-permute-start.7) | collective-permute-done | bytes 131104 | tf_op jit(solution)/shard_map/ppermute | solution.py:155
  138.1 7.9 %collective-permute-done.8 = bf16[512,128]{1,0:T(8,128)(2,1)S(1)} collective-permute-done((bf16[512,128]{1,0:T(8,128)(2,1)S(1)}, bf16[512,128]{1,0:T(8,128)(2,1)S(1)}, u32[]{:S(2)}, u32[]{:S(2)}) %collective-permute-start.8) | collective-permute-done | bytes 131104 | tf_op jit(solution)/shard_map/ppermute | solution.py:155
  146.1 0.7 add_convert_fusion
  146.8 0.0 all-to-all-done.3
  146.8 0.1 convert_reduce_fusion
  146.9 0.7 fusion.16
  147.6 0.0 copy-done.4
  (9 shorter events, 0.2 us)
Async XLA Ops:
  0.6 49.0 %copy-start = (bf16[512,2048]{1,0:T(8,128)(2,1)S(1)}, bf16[512,2048]{1,0:T(8,128)(2,1)}, u32[]{:S(2)}) copy-start(bf16[512,2048]{1,0:T(8,128)(2,1)} %param.5) | copy-start | bytes 6291460
  2.3 47.1 %all-to-all-start = ((bf16[64,16,128]{2,1,0:T(8,128)(2,1)}), bf16[64,16,128]{2,1,0:T(8,128)(2,1)S(1)}, u32[]{:S(2)}, u32[]{:S(2)}) async-start(bf16[64,16,128]{2,1,0:T(8,128)(2,1)} %broadcast_in_dim.6), calls=%async_computation | async-start | bytes 524288 | tf_op jit(solution)/shard_map/all_to_all | solution.py:15
  27.9 30.0 %copy-start.3 = (f32[512,64]{0,1:T(8,128)}, f32[512,64]{0,1:T(8,128)S(1)}, u32[]{:S(2)}) copy-start(f32[512,64]{0,1:T(8,128)S(1)} %fusion.21) | copy-start | bytes 393220
  49.5 1.2 copy-start.1
  52.9 22.9 %all-to-all-start.1 = ((f32[64,3,128]{2,1,0:T(4,128)}), f32[64,3,128]{2,1,0:T(4,128)}, u32[]{:S(2)}, u32[]{:S(2)}) async-start(f32[64,3,128]{2,1,0:T(4,128)} %broadcast_in_dim.7), calls=%async_computation.1 | async-start | bytes 262144 | tf_op jit(solution)/shard_map/all_to_all | solution.py:15
  59.2 12.0 %collective-permute-start = (bf16[128,512]{1,0:T(8,128)(2,1)S(1)}, bf16[128,512]{1,0:T(8,128)(2,1)S(1)}, u32[]{:S(2)}, u32[]{:S(2)}) collective-permute-start(bf16[128,512]{1,0:T(8,128)(2,1)S(1)} %get-tuple-element.21), channel_id=1, source_target_pairs={{0,1},{1,0},{2,3},{3,2},{4,5},{5,4},{6,7},{7,6},{8,9},{9,8},{10,11... | collective-permute-start | bytes 393224 | tf_op jit(solution)/shard_map/ppermute | solution.py:88
  61.4 9.8 %collective-permute-start.1 = (bf16[128,512]{1,0:T(8,128)(2,1)S(1)}, bf16[128,512]{1,0:T(8,128)(2,1)S(1)}, u32[]{:S(2)}, u32[]{:S(2)}) collective-permute-start(bf16[128,512]{1,0:T(8,128)(2,1)S(1)} %get-tuple-element.22), channel_id=1, source_target_pairs={{0,2},{1,3},{2,0},{3,1},{4,6},{5,7},{6,4},{7,5},{8,10},{9,11},{10,... | collective-permute-start | bytes 393224 | tf_op jit(solution)/shard_map/ppermute | solution.py:88
  64.6 7.4 %collective-permute-start.2 = (bf16[128,512]{1,0:T(8,128)(2,1)S(1)}, bf16[128,512]{1,0:T(8,128)(2,1)S(1)}, u32[]{:S(2)}, u32[]{:S(2)}) collective-permute-start(bf16[128,512]{1,0:T(8,128)(2,1)S(1)} %get-tuple-element.23), channel_id=1, source_target_pairs={{0,3},{1,2},{2,1},{3,0},{4,7},{5,6},{6,5},{7,4},{8,11},{9,10},{10,... | collective-permute-start | bytes 393224 | tf_op jit(solution)/shard_map/ppermute | solution.py:88
  78.4 15.4 %all-to-all-start.2 = ((f32[16,3,512]{2,1,0:T(4,128)}), f32[16,3,512]{2,1,0:T(4,128)S(1)}, u32[]{:S(2)}, u32[]{:S(2)}) async-start(f32[16,3,512]{2,1,0:T(4,128)} %broadcast_in_dim.8), calls=%async_computation.2 | async-start | bytes 262144 | tf_op jit(solution)/shard_map/all_to_all | solution.py:15
  94.0 2.3 %copy-start.2 = (bf16[512,2048]{1,0:T(8,128)(2,1)S(1)}, bf16[512,2048]{1,0:T(8,128)(2,1)}, u32[]{:S(2)}) copy-start(bf16[512,2048]{1,0:T(8,128)(2,1)} %param.9) | copy-start | bytes 6291460
  97.8 49.0 %all-to-all-start.3 = ((bf16[64,32,128]{2,1,0:T(8,128)(2,1)}), bf16[64,32,128]{2,1,0:T(8,128)(2,1)S(1)}, u32[]{:S(2)}, u32[]{:S(2)}) async-start(bf16[64,32,128]{2,1,0:T(8,128)(2,1)} %bitcast.84), calls=%async_computation.3 | async-start | bytes 1048576 | tf_op jit(solution)/shard_map/all_to_all | solution.py:149
  111.1 8.4 %collective-permute-start.3 = (bf16[512,128]{1,0:T(8,128)(2,1)S(1)}, bf16[512,128]{1,0:T(8,128)(2,1)S(1)}, u32[]{:S(2)}, u32[]{:S(2)}) collective-permute-start(bf16[512,128]{1,0:T(8,128)(2,1)S(1)} %pad_maximum_fusion.2.refs_0_), channel_id=1, source_target_pairs={{0,1},{1,0},{2,3},{3,2},{4,5},{5,4},{6,7},{7,6},{8,9},{9,8},{10,11... | collective-permute-start | bytes 393224 | tf_op jit(solution)/shard_map/ppermute | solution.py:88
  113.0 6.5 %collective-permute-start.4 = (bf16[512,128]{1,0:T(8,128)(2,1)S(1)}, bf16[512,128]{1,0:T(8,128)(2,1)S(1)}, u32[]{:S(2)}, u32[]{:S(2)}) collective-permute-start(bf16[512,128]{1,0:T(8,128)(2,1)S(1)} %pad_maximum_fusion.2.refs_0_), channel_id=1, source_target_pairs={{0,2},{1,3},{2,0},{3,1},{4,6},{5,7},{6,4},{7,5},{8,10},{9,11},{10,... | collective-permute-start | bytes 393224 | tf_op jit(solution)/shard_map/ppermute | solution.py:88
  115.0 8.6 %collective-permute-start.5 = (bf16[512,128]{1,0:T(8,128)(2,1)S(1)}, bf16[512,128]{1,0:T(8,128)(2,1)S(1)}, u32[]{:S(2)}, u32[]{:S(2)}) collective-permute-start(bf16[512,128]{1,0:T(8,128)(2,1)S(1)} %pad_maximum_fusion.2.refs_0_), channel_id=1, source_target_pairs={{0,3},{1,2},{2,1},{3,0},{4,7},{5,6},{6,5},{7,4},{8,11},{9,10},{10,... | collective-permute-start | bytes 393224 | tf_op jit(solution)/shard_map/ppermute | solution.py:88
  124.3 10.7 %collective-permute-start.6 = (bf16[512,128]{1,0:T(8,128)(2,1)S(1)}, bf16[512,128]{1,0:T(8,128)(2,1)S(1)}, u32[]{:S(2)}, u32[]{:S(2)}) collective-permute-start(bf16[512,128]{1,0:T(8,128)(2,1)S(1)} %get-tuple-element.32), channel_id=1, source_target_pairs={{0,4},{1,5},{2,6},{3,7},{4,8},{5,9},{6,10},{7,11},{8,12},{9,13},{1... | collective-permute-start | bytes 393224 | tf_op jit(solution)/shard_map/ppermute | solution.py:155
  127.0 11.1 %collective-permute-start.7 = (bf16[512,128]{1,0:T(8,128)(2,1)S(1)}, bf16[512,128]{1,0:T(8,128)(2,1)S(1)}, u32[]{:S(2)}, u32[]{:S(2)}) collective-permute-start(bf16[512,128]{1,0:T(8,128)(2,1)S(1)} %get-tuple-element.33), channel_id=1, source_target_pairs={{0,8},{1,9},{2,10},{3,11},{4,12},{5,13},{6,14},{7,15},{8,0},{9,1},... | collective-permute-start | bytes 393224 | tf_op jit(solution)/shard_map/ppermute | solution.py:155
  131.1 15.0 %collective-permute-start.8 = (bf16[512,128]{1,0:T(8,128)(2,1)S(1)}, bf16[512,128]{1,0:T(8,128)(2,1)S(1)}, u32[]{:S(2)}, u32[]{:S(2)}) collective-permute-start(bf16[512,128]{1,0:T(8,128)(2,1)S(1)} %get-tuple-element.34), channel_id=1, source_target_pairs={{0,12},{1,13},{2,14},{3,15},{4,0},{5,1},{6,2},{7,3},{8,4},{9,5},{1... | collective-permute-start | bytes 393224 | tf_op jit(solution)/shard_map/ppermute | solution.py:155
  146.9 0.7 copy-start.4

commit v5 on v4

--- a/solution.py
+++ b/solution.py
@@ -121,12 +121,14 @@
             [col_top, jnp.sum(col_exp, axis=0), jnp.sum(col_exp * disp_grad, axis=0)]
         )
 
+        row_got = gather_blocks(row_stats, "exp", n_exp)
         col_stats = jnp.pad(col_stats, ((0, 0), (0, -slots % 128)))
-        col_got = gather_blocks(col_stats, "seq", n_seq)
-        row_stats, col_got, weights = lax.optimization_barrier((row_stats, col_got, weights))
-        row_got = gather_blocks(row_stats, "exp", n_exp)
+        spread = jnp.broadcast_to(col_stats[None], (n_seq,) + col_stats.shape)
+        spread, row_got = lax.optimization_barrier((spread, row_got))
+        col_got = lax.all_to_all(spread, "seq", 0, 0, tiled=True)
+        col_got, weights = lax.optimization_barrier((col_got, weights))
+        row_peak, row_total, row_dot = merge_stats(row_got)
         col_peak, col_total, col_dot = merge_stats(col_got[:, :, :slots])
-        row_peak, row_total, row_dot = merge_stats(row_got)
 
         combine = jnp.exp(logits - row_peak[:, None]) / row_total[:, None]
         dispatch = jnp.exp(logits - col_peak[None, :]) / col_total[None, :]
@@ -150,7 +152,7 @@
 
         blocks = column_blocks(factors, weights, groups, wide)
         token_sum = blocks[0].astype(F32)
-        for i in range(1, groups):
+        for i in sorted(range(1, groups), key=lambda i: abs(2 * i - groups)):
             turn = [(j, (j + i * GROUP) % n_exp) for j in range(n_exp)]
             token_sum = token_sum + lax.ppermute(blocks[i], "exp", turn).astype(F32)
         token_grad = token_sum.astype(BF)

time: 148 us -> 148 us (level)
  waiting for transfers between devices: 50.5 us -> 48.5 us
    ppermute x3, waiting for transfers between devices: 11.9 us -> 6.02 us  [per_device(): token_sum = token_sum + lax.ppermute(blocks[i], 'exp', turn).astype(F32)]
    all_to_all x0 -> x1, starting transfers between devices: none -> 5.43 us  [per_device(): col_got = lax.all_to_all(spread, 'seq', 0, 0, tiled=True)]
    all_to_all x3 -> x2, starting transfers between devices: 35.2 us -> 30.2 us  [gather_blocks(): return lax.all_to_all(spread, axis, 0, 0, tiled=True)]
    all_to_all x0 -> x1, waiting for transfers between devices: none -> 3.33 us  [per_device(): col_got = lax.all_to_all(spread, 'seq', 0, 0, tiled=True)]
    all_to_all x1, waiting for transfers between devices: 0.01 us -> 3.12 us  [per_device(): lax.all_to_all(both.reshape(n_seq, -1, 2 * slots), 'seq', 0, 0, tiled=True)]
    all_to_all x3 -> x2, waiting for transfers between devices: 33.6 us -> 31.3 us  [gather_blocks(): return lax.all_to_all(spread, axis, 0, 0, tiled=True)]
    ppermute x3, starting transfers between devices: 9.87 us -> 11.4 us  [per_device(): token_sum = token_sum + lax.ppermute(blocks[i], 'exp', turn).astype(F32)]
where the time goes in v5:
time: 148 us; the launch traced here: 147 us
  starting transfers between devices  76.5 us (52%)
  waiting for transfers between devices  48.5 us (33%)
  local copies, waits for them, and re-layouts  9.81 us (7%)
  matrix products  5.09 us (3%)
  other arithmetic  4.2 us (3%)
  Pallas kernels  1.82 us (1%)
    all_to_all x2, waiting for transfers between devices, gather_blocks(): return lax.all_to_all(spread, axis, 0, 0, tiled=True)  31.3 us
    all_to_all x2, starting transfers between devices, gather_blocks(): return lax.all_to_all(spread, axis, 0, 0, tiled=True)  30.2 us
    ppermute x6, starting transfers between devices, swap(): return lax.ppermute(x, 'exp', [(j, j ^ k) for j in range(n_exp)])  16.7 us
    all_to_all x1, starting transfers between devices, per_device(): lax.all_to_all(both.reshape(n_seq, -1, 2 * slots), 'seq', 0, 0, tiled=True)  12.8 us
    ppermute x3, starting transfers between devices, per_device(): token_sum = token_sum + lax.ppermute(blocks[i], 'exp', turn).astype(F32)  11.4 us
    ppermute x3, waiting for transfers between devices, per_device(): token_sum = token_sum + lax.ppermute(blocks[i], 'exp', turn).astype(F32)  6.02 us
    all_to_all x1, starting transfers between devices, per_device(): col_got = lax.all_to_all(spread, 'seq', 0, 0, tiled=True)  5.43 us
    ppermute x6, waiting for transfers between devices, swap(): return lax.ppermute(x, 'exp', [(j, j ^ k) for j in range(n_exp)])  4.69 us
  transfers between devices with their start and end apart: 13, of which 8 were waited for; matrix products, arithmetic and copies ran while one was open for 5% of the time, Pallas kernels for 1%

profile of v5, /device:TPU:1, one launch (start us, length us, event | category | flops | bytes accessed | tf_op | source)
XLA Modules:
  0.0 146.9 jit_solution(6268092644416533590)
XLA Ops:
  0.6 0.0 copy-start
  0.6 0.9 fusion.18
  1.5 0.1 pad_maximum_fusion.4
  1.6 0.7 broadcast_in_dim.6
  2.3 23.3 %all-to-all-start = ((bf16[64,16,128]{2,1,0:T(8,128)(2,1)}), bf16[64,16,128]{2,1,0:T(8,128)(2,1)S(1)}, u32[]{:S(2)}, u32[]{:S(2)}) async-start(bf16[64,16,128]{2,1,0:T(8,128)(2,1)} %broadcast_in_dim.6), calls=%async_computation | async-start | bytes 524288 | tf_op jit(solution)/shard_map/all_to_all | solution.py:15
  25.6 0.0 copy-done
  25.6 1.7 %fusion.19 = f32[512,64]{0,1:T(8,128)S(1)} fusion(bf16[512,2048]{1,0:T(8,128)(2,1)S(1)} %copy-done, bf16[64,2048]{1,0:T(8,128)(2,1)} %sig_ref.1), kind=kOutput, calls=%fused_computation.51 | convolution fusion | flops 134217728 | bytes 2490368 | tf_op jit(solution)/shard_map/dot_general | solution.py:101
  27.3 22.1 %all-to-all-done = bf16[64,16,128]{2,1,0:T(8,128)(2,1)S(1)} async-done(((bf16[64,16,128]{2,1,0:T(8,128)(2,1)}), bf16[64,16,128]{2,1,0:T(8,128)(2,1)S(1)}, u32[]{:S(2)}, u32[]{:S(2)}) %all-to-all-start) | async-done | bytes 262176 | tf_op jit(solution)/shard_map/all_to_all | solution.py:15
  49.4 0.1 fusion.17
  49.5 0.0 copy-start.2
  49.6 0.0 copy-start.5
  49.6 0.1 pad_maximum_fusion
  49.7 0.9 fusion.16
  50.5 0.2 fusion.7
  50.7 0.4 copy-done.2
  51.1 0.0 copy-done.5
  51.1 1.5 %fusion.4 = (f32[512]{0:T(512)S(1)}, f32[64]{0:T(128)S(1)}, f32[512,64]{0,1:T(8,128)}) fusion(f32[64,512]{1,0:T(8,128)S(1)} %get-tuple-element.55, f32[512]{0:T(512)S(1)} %get-tuple-element.43, f32[512,64]{0,1:T(8,128)S(1)} %fusion.19, f32[64]{0:T(128)S(1)} %get-tuple-element.44, bf16[512,2048]{1,0:T(8,128)(2,1)S(1)} %copy-done.2, ...), kind=kOutput, calls=%fused_computation.18 | convolution fusion | flops 134413760 | bytes 2757120 | tf_op jit(solution)/shard_map/dot_general | solution.py:104
  52.7 0.7 broadcast_in_dim.8
  53.3 7.0 %all-to-all-start.1 = ((f32[16,3,512]{2,1,0:T(4,128)}), f32[16,3,512]{2,1,0:T(4,128)S(1)}, u32[]{:S(2)}, u32[]{:S(2)}) async-start(f32[16,3,512]{2,1,0:T(4,128)} %broadcast_in_dim.8), calls=%async_computation.1 | async-start | bytes 262144 | tf_op jit(solution)/shard_map/all_to_all | solution.py:15
  60.3 9.2 %all-to-all-done.1 = f32[16,3,512]{2,1,0:T(4,128)S(1)} async-done(((f32[16,3,512]{2,1,0:T(4,128)}), f32[16,3,512]{2,1,0:T(4,128)S(1)}, u32[]{:S(2)}, u32[]{:S(2)}) %all-to-all-start.1) | async-done | bytes 98336 | tf_op jit(solution)/shard_map/all_to_all | solution.py:15
  69.5 0.7 broadcast_in_dim.7
  70.2 5.4 %all-to-all-start.2 = ((f32[64,3,128]{2,1,0:T(4,128)}), f32[64,3,128]{2,1,0:T(4,128)S(1)}, u32[]{:S(2)}, u32[]{:S(2)}) async-start(f32[64,3,128]{2,1,0:T(4,128)} %broadcast_in_dim.7), calls=%async_computation.2 | async-start | bytes 262144 | tf_op jit(solution)/shard_map/all_to_all | solution.py:128
  75.7 0.8 copy.48
  76.5 0.1 pad_add_fusion.place_ref
  76.6 0.0 copy-done.4
  76.6 0.8 copy.40
  77.4 0.0 copy-done.1
  77.4 1.1 shard_map.76
  78.6 2.2 %collective-permute-start = (bf16[128,512]{1,0:T(8,128)(2,1)S(1)}, bf16[128,512]{1,0:T(8,128)(2,1)S(1)}, u32[]{:S(2)}, u32[]{:S(2)}) collective-permute-start(bf16[128,512]{1,0:T(8,128)(2,1)S(1)} %get-tuple-element.23), channel_id=1, source_target_pairs={{0,1},{1,0},{2,3},{3,2},{4,5},{5,4},{6,7},{7,6},{8,9},{9,8},{10,11... | collective-permute-start | bytes 393224 | tf_op jit(solution)/shard_map/ppermute | solution.py:88
  80.8 2.0 %collective-permute-start.1 = (bf16[128,512]{1,0:T(8,128)(2,1)S(1)}, bf16[128,512]{1,0:T(8,128)(2,1)S(1)}, u32[]{:S(2)}, u32[]{:S(2)}) collective-permute-start(bf16[128,512]{1,0:T(8,128)(2,1)S(1)} %get-tuple-element.24), channel_id=1, source_target_pairs={{0,2},{1,3},{2,0},{3,1},{4,6},{5,7},{6,4},{7,5},{8,10},{9,11},{10,... | collective-permute-start | bytes 393224 | tf_op jit(solution)/shard_map/ppermute | solution.py:88
  82.8 4.2 %collective-permute-start.2 = (bf16[128,512]{1,0:T(8,128)(2,1)S(1)}, bf16[128,512]{1,0:T(8,128)(2,1)S(1)}, u32[]{:S(2)}, u32[]{:S(2)}) collective-permute-start(bf16[128,512]{1,0:T(8,128)(2,1)S(1)} %get-tuple-element.25), channel_id=1, source_target_pairs={{0,3},{1,2},{2,1},{3,0},{4,7},{5,6},{6,5},{7,4},{8,11},{9,10},{10,... | collective-permute-start | bytes 393224 | tf_op jit(solution)/shard_map/ppermute | solution.py:88
  87.0 1.0 copy.47
  88.0 0.9 copy.43
  89.0 0.9 slice.49
  90.0 0.0 collective-permute-done.refs_5_
  90.0 0.0 collective-permute-done.1.refs_6_
  90.0 1.1 collective-permute-done.2.refs_7_
  91.0 3.3 %all-to-all-done.2 = f32[64,3,128]{2,1,0:T(4,128)S(1)} async-done(((f32[64,3,128]{2,1,0:T(4,128)}), f32[64,3,128]{2,1,0:T(4,128)S(1)}, u32[]{:S(2)}, u32[]{:S(2)}) %all-to-all-start.2) | async-done | bytes 98336 | tf_op jit(solution)/shard_map/all_to_all | solution.py:128
  94.5 1.3 bitcast_convert_fusion
  95.8 1.3 fusion.3
  97.1 0.1 pad_maximum_fusion.2.refs_0_
  97.3 0.5 fusion
  97.8 0.0 copy-done.3
  97.8 0.5 fusion.1
  98.3 1.0 copy.49
  99.3 12.8 %all-to-all-start.3 = ((bf16[64,32,128]{2,1,0:T(8,128)(2,1)}), bf16[64,32,128]{2,1,0:T(8,128)(2,1)S(1)}, u32[]{:S(2)}, u32[]{:S(2)}) async-start(bf16[64,32,128]{2,1,0:T(8,128)(2,1)} %bitcast.82), calls=%async_computation.3 | async-start | bytes 1048576 | tf_op jit(solution)/shard_map/all_to_all | solution.py:151
  112.1 2.2 %collective-permute-start.3 = (bf16[512,128]{1,0:T(8,128)(2,1)S(1)}, bf16[512,128]{1,0:T(8,128)(2,1)S(1)}, u32[]{:S(2)}, u32[]{:S(2)}) collective-permute-start(bf16[512,128]{1,0:T(8,128)(2,1)S(1)} %pad_maximum_fusion.2.refs_0_), channel_id=1, source_target_pairs={{0,1},{1,0},{2,3},{3,2},{4,5},{5,4},{6,7},{7,6},{8,9},{9,8},{10,11... | collective-permute-start | bytes 393224 | tf_op jit(solution)/shard_map/ppermute | solution.py:88
  114.3 2.8 %collective-permute-start.4 = (bf16[512,128]{1,0:T(8,128)(2,1)S(1)}, bf16[512,128]{1,0:T(8,128)(2,1)S(1)}, u32[]{:S(2)}, u32[]{:S(2)}) collective-permute-start(bf16[512,128]{1,0:T(8,128)(2,1)S(1)} %pad_maximum_fusion.2.refs_0_), channel_id=1, source_target_pairs={{0,2},{1,3},{2,0},{3,1},{4,6},{5,7},{6,4},{7,5},{8,10},{9,11},{10,... | collective-permute-start | bytes 393224 | tf_op jit(solution)/shard_map/ppermute | solution.py:88
  117.1 3.3 %collective-permute-start.5 = (bf16[512,128]{1,0:T(8,128)(2,1)S(1)}, bf16[512,128]{1,0:T(8,128)(2,1)S(1)}, u32[]{:S(2)}, u32[]{:S(2)}) collective-permute-start(bf16[512,128]{1,0:T(8,128)(2,1)S(1)} %pad_maximum_fusion.2.refs_0_), channel_id=1, source_target_pairs={{0,3},{1,2},{2,1},{3,0},{4,7},{5,6},{6,5},{7,4},{8,11},{9,10},{10,... | collective-permute-start | bytes 393224 | tf_op jit(solution)/shard_map/ppermute | solution.py:88
  120.5 0.0 collective-permute-done.3.refs_1_
  120.5 0.0 collective-permute-done.4.refs_2_
  120.5 3.6 %collective-permute-done.5.refs_3_ = bf16[512,128]{1,0:T(8,128)(2,1)S(1)} collective-permute-done((bf16[512,128]{1,0:T(8,128)(2,1)S(1)}, bf16[512,128]{1,0:T(8,128)(2,1)S(1)}, u32[]{:S(2)}, u32[]{:S(2)}) %collective-permute-start.5) | collective-permute-done | bytes 131104 | tf_op jit(solution)/shard_map/ppermute | solution.py:88
  124.1 0.7 shard_map.77
  124.8 4.0 %collective-permute-start.6 = (bf16[512,128]{1,0:T(8,128)(2,1)S(1)}, bf16[512,128]{1,0:T(8,128)(2,1)S(1)}, u32[]{:S(2)}, u32[]{:S(2)}) collective-permute-start(bf16[512,128]{1,0:T(8,128)(2,1)S(1)} %get-tuple-element.34), channel_id=1, source_target_pairs={{0,8},{1,9},{2,10},{3,11},{4,12},{5,13},{6,14},{7,15},{8,0},{9,1},... | collective-permute-start | bytes 393224 | tf_op jit(solution)/shard_map/ppermute | solution.py:157
  128.8 2.7 %collective-permute-start.7 = (bf16[512,128]{1,0:T(8,128)(2,1)S(1)}, bf16[512,128]{1,0:T(8,128)(2,1)S(1)}, u32[]{:S(2)}, u32[]{:S(2)}) collective-permute-start(bf16[512,128]{1,0:T(8,128)(2,1)S(1)} %get-tuple-element.35), channel_id=1, source_target_pairs={{0,4},{1,5},{2,6},{3,7},{4,8},{5,9},{6,10},{7,11},{8,12},{9,13},{1... | collective-permute-start | bytes 393224 | tf_op jit(solution)/shard_map/ppermute | solution.py:157
  131.5 4.7 %collective-permute-start.8 = (bf16[512,128]{1,0:T(8,128)(2,1)S(1)}, bf16[512,128]{1,0:T(8,128)(2,1)S(1)}, u32[]{:S(2)}, u32[]{:S(2)}) collective-permute-start(bf16[512,128]{1,0:T(8,128)(2,1)S(1)} %get-tuple-element.36), channel_id=1, source_target_pairs={{0,12},{1,13},{2,14},{3,15},{4,0},{5,1},{6,2},{7,3},{8,4},{9,5},{1... | collective-permute-start | bytes 393224 | tf_op jit(solution)/shard_map/ppermute | solution.py:157
  136.2 0.0 collective-permute-done.6
  136.2 5.0 %collective-permute-done.7 = bf16[512,128]{1,0:T(8,128)(2,1)S(1)} collective-permute-done((bf16[512,128]{1,0:T(8,128)(2,1)S(1)}, bf16[512,128]{1,0:T(8,128)(2,1)S(1)}, u32[]{:S(2)}, u32[]{:S(2)}) %collective-permute-start.7) | collective-permute-done | bytes 131104 | tf_op jit(solution)/shard_map/ppermute | solution.py:157
  141.3 1.0 collective-permute-done.8
  142.2 0.7 add_convert_fusion
  143.0 3.1 %all-to-all-done.3 = bf16[64,32,128]{2,1,0:T(8,128)(2,1)S(1)} async-done(((bf16[64,32,128]{2,1,0:T(8,128)(2,1)}), bf16[64,32,128]{2,1,0:T(8,128)(2,1)S(1)}, u32[]{:S(2)}, u32[]{:S(2)}) %all-to-all-start.3) | async-done | bytes 524320 | tf_op jit(solution)/shard_map/all_to_all | solution.py:151
  146.1 0.1 convert_reduce_fusion
  146.2 0.7 fusion.15
  146.9 0.0 copy-done.6
  (15 shorter events, 0.2 us)
Async XLA Ops:
  0.6 25.0 %copy-start = (bf16[512,2048]{1,0:T(8,128)(2,1)S(1)}, bf16[512,2048]{1,0:T(8,128)(2,1)}, u32[]{:S(2)}) copy-start(bf16[512,2048]{1,0:T(8,128)(2,1)} %param.5) | copy-start | bytes 6291460
  2.3 47.1 %all-to-all-start = ((bf16[64,16,128]{2,1,0:T(8,128)(2,1)}), bf16[64,16,128]{2,1,0:T(8,128)(2,1)S(1)}, u32[]{:S(2)}, u32[]{:S(2)}) async-start(bf16[64,16,128]{2,1,0:T(8,128)(2,1)} %broadcast_in_dim.6), calls=%async_computation | async-start | bytes 524288 | tf_op jit(solution)/shard_map/all_to_all | solution.py:15
  49.5 1.6 %copy-start.2 = (bf16[512,2048]{1,0:T(8,128)(2,1)S(1)}, bf16[512,2048]{1,0:T(8,128)(2,1)}, u32[]{:S(2)}) copy-start(bf16[512,2048]{1,0:T(8,128)(2,1)} %param.9) | copy-start | bytes 6291460
  49.6 1.6 %copy-start.5 = (bf16[64,2048]{1,0:T(8,128)(2,1)S(1)}, bf16[64,2048]{1,0:T(8,128)(2,1)}, u32[]{:S(2)}) copy-start(bf16[64,2048]{1,0:T(8,128)(2,1)} %param.7) | copy-start | bytes 786436
  51.1 26.3 %copy-start.1 = (bf16[64,2048]{1,0:T(8,128)(2,1)S(1)}, bf16[64,2048]{1,0:T(8,128)(2,1)}, u32[]{:S(2)}) copy-start(bf16[64,2048]{1,0:T(8,128)(2,1)} %sig_ref.1) | copy-start | bytes 786436
  53.3 16.2 %all-to-all-start.1 = ((f32[16,3,512]{2,1,0:T(4,128)}), f32[16,3,512]{2,1,0:T(4,128)S(1)}, u32[]{:S(2)}, u32[]{:S(2)}) async-start(f32[16,3,512]{2,1,0:T(4,128)} %broadcast_in_dim.8), calls=%async_computation.1 | async-start | bytes 262144 | tf_op jit(solution)/shard_map/all_to_all | solution.py:15
  69.5 7.1 %copy-start.4 = (f32[16,3,512]{2,1,0:T(4,128)}, f32[16,3,512]{2,1,0:T(4,128)S(1)}, u32[]{:S(2)}) copy-start(f32[16,3,512]{2,1,0:T(4,128)S(1)} %all-to-all-done.1) | copy-start | bytes 294916
  70.2 24.1 %all-to-all-start.2 = ((f32[64,3,128]{2,1,0:T(4,128)}), f32[64,3,128]{2,1,0:T(4,128)S(1)}, u32[]{:S(2)}, u32[]{:S(2)}) async-start(f32[64,3,128]{2,1,0:T(4,128)} %broadcast_in_dim.7), calls=%async_computation.2 | async-start | bytes 262144 | tf_op jit(solution)/shard_map/all_to_all | solution.py:128
  78.6 11.4 %collective-permute-start = (bf16[128,512]{1,0:T(8,128)(2,1)S(1)}, bf16[128,512]{1,0:T(8,128)(2,1)S(1)}, u32[]{:S(2)}, u32[]{:S(2)}) collective-permute-start(bf16[128,512]{1,0:T(8,128)(2,1)S(1)} %get-tuple-element.23), channel_id=1, source_target_pairs={{0,1},{1,0},{2,3},{3,2},{4,5},{5,4},{6,7},{7,6},{8,9},{9,8},{10,11... | collective-permute-start | bytes 393224 | tf_op jit(solution)/shard_map/ppermute | solution.py:88
  80.8 9.2 %collective-permute-start.1 = (bf16[128,512]{1,0:T(8,128)(2,1)S(1)}, bf16[128,512]{1,0:T(8,128)(2,1)S(1)}, u32[]{:S(2)}, u32[]{:S(2)}) collective-permute-start(bf16[128,512]{1,0:T(8,128)(2,1)S(1)} %get-tuple-element.24), channel_id=1, source_target_pairs={{0,2},{1,3},{2,0},{3,1},{4,6},{5,7},{6,4},{7,5},{8,10},{9,11},{10,... | collective-permute-start | bytes 393224 | tf_op jit(solution)/shard_map/ppermute | solution.py:88
  82.8 8.3 %collective-permute-start.2 = (bf16[128,512]{1,0:T(8,128)(2,1)S(1)}, bf16[128,512]{1,0:T(8,128)(2,1)S(1)}, u32[]{:S(2)}, u32[]{:S(2)}) collective-permute-start(bf16[128,512]{1,0:T(8,128)(2,1)S(1)} %get-tuple-element.25), channel_id=1, source_target_pairs={{0,3},{1,2},{2,1},{3,0},{4,7},{5,6},{6,5},{7,4},{8,11},{9,10},{10,... | collective-permute-start | bytes 393224 | tf_op jit(solution)/shard_map/ppermute | solution.py:88
  94.5 3.3 %copy-start.3 = (bf16[512,2048]{1,0:T(8,128)(2,1)S(1)}, bf16[512,2048]{1,0:T(8,128)(2,1)}, u32[]{:S(2)}) copy-start(bf16[512,2048]{1,0:T(8,128)(2,1)} %param.9) | copy-start | bytes 6291460
  99.3 46.8 %all-to-all-start.3 = ((bf16[64,32,128]{2,1,0:T(8,128)(2,1)}), bf16[64,32,128]{2,1,0:T(8,128)(2,1)S(1)}, u32[]{:S(2)}, u32[]{:S(2)}) async-start(bf16[64,32,128]{2,1,0:T(8,128)(2,1)} %bitcast.82), calls=%async_computation.3 | async-start | bytes 1048576 | tf_op jit(solution)/shard_map/all_to_all | solution.py:151
  112.1 8.4 %collective-permute-start.3 = (bf16[512,128]{1,0:T(8,128)(2,1)S(1)}, bf16[512,128]{1,0:T(8,128)(2,1)S(1)}, u32[]{:S(2)}, u32[]{:S(2)}) collective-permute-start(bf16[512,128]{1,0:T(8,128)(2,1)S(1)} %pad_maximum_fusion.2.refs_0_), channel_id=1, source_target_pairs={{0,1},{1,0},{2,3},{3,2},{4,5},{5,4},{6,7},{7,6},{8,9},{9,8},{10,11... | collective-permute-start | bytes 393224 | tf_op jit(solution)/shard_map/ppermute | solution.py:88
  114.3 6.2 %collective-permute-start.4 = (bf16[512,128]{1,0:T(8,128)(2,1)S(1)}, bf16[512,128]{1,0:T(8,128)(2,1)S(1)}, u32[]{:S(2)}, u32[]{:S(2)}) collective-permute-start(bf16[512,128]{1,0:T(8,128)(2,1)S(1)} %pad_maximum_fusion.2.refs_0_), channel_id=1, source_target_pairs={{0,2},{1,3},{2,0},{3,1},{4,6},{5,7},{6,4},{7,5},{8,10},{9,11},{10,... | collective-permute-start | bytes 393224 | tf_op jit(solution)/shard_map/ppermute | solution.py:88
  117.1 7.0 %collective-permute-start.5 = (bf16[512,128]{1,0:T(8,128)(2,1)S(1)}, bf16[512,128]{1,0:T(8,128)(2,1)S(1)}, u32[]{:S(2)}, u32[]{:S(2)}) collective-permute-start(bf16[512,128]{1,0:T(8,128)(2,1)S(1)} %pad_maximum_fusion.2.refs_0_), channel_id=1, source_target_pairs={{0,3},{1,2},{2,1},{3,0},{4,7},{5,6},{6,5},{7,4},{8,11},{9,10},{10,... | collective-permute-start | bytes 393224 | tf_op jit(solution)/shard_map/ppermute | solution.py:88
  124.8 11.4 %collective-permute-start.6 = (bf16[512,128]{1,0:T(8,128)(2,1)S(1)}, bf16[512,128]{1,0:T(8,128)(2,1)S(1)}, u32[]{:S(2)}, u32[]{:S(2)}) collective-permute-start(bf16[512,128]{1,0:T(8,128)(2,1)S(1)} %get-tuple-element.34), channel_id=1, source_target_pairs={{0,8},{1,9},{2,10},{3,11},{4,12},{5,13},{6,14},{7,15},{8,0},{9,1},... | collective-permute-start | bytes 393224 | tf_op jit(solution)/shard_map/ppermute | solution.py:157
  128.8 12.5 %collective-permute-start.7 = (bf16[512,128]{1,0:T(8,128)(2,1)S(1)}, bf16[512,128]{1,0:T(8,128)(2,1)S(1)}, u32[]{:S(2)}, u32[]{:S(2)}) collective-permute-start(bf16[512,128]{1,0:T(8,128)(2,1)S(1)} %get-tuple-element.35), channel_id=1, source_target_pairs={{0,4},{1,5},{2,6},{3,7},{4,8},{5,9},{6,10},{7,11},{8,12},{9,13},{1... | collective-permute-start | bytes 393224 | tf_op jit(solution)/shard_map/ppermute | solution.py:157
  131.5 10.7 %collective-permute-start.8 = (bf16[512,128]{1,0:T(8,128)(2,1)S(1)}, bf16[512,128]{1,0:T(8,128)(2,1)S(1)}, u32[]{:S(2)}, u32[]{:S(2)}) collective-permute-start(bf16[512,128]{1,0:T(8,128)(2,1)S(1)} %get-tuple-element.36), channel_id=1, source_target_pairs={{0,12},{1,13},{2,14},{3,15},{4,0},{5,1},{6,2},{7,3},{8,4},{9,5},{1... | collective-permute-start | bytes 393224 | tf_op jit(solution)/shard_map/ppermute | solution.py:157
  146.2 0.7 copy-start.6

commit v6 on v5

--- a/solution.py
+++ b/solution.py
@@ -3,10 +3,12 @@
 from jax import lax
 from jax.experimental import pallas as pl
 from jax.experimental.pallas import tpu as pltpu
+from jax.sharding import Mesh
 from jax.sharding import PartitionSpec as P
 
 BF = jnp.bfloat16
 F32 = jnp.float32
+SEQ = ("chip", "core")
 GROUP = 4
 
 
@@ -93,7 +95,7 @@
         wide = width // n_exp
         half = phi.shape[0] // 2
         packed = jnp.concatenate([phi[:half], phi[half:]], axis=1)
-        got_phi = gather_blocks(packed, "seq", n_seq)
+        got_phi = gather_blocks(packed, SEQ, n_seq)
         phi_full = jnp.concatenate([got_phi[:, :, :slots], got_phi[:, :, slots:]], axis=1)
         phi_full = phi_full.reshape(width, slots)
 
@@ -125,7 +127,7 @@
         col_stats = jnp.pad(col_stats, ((0, 0), (0, -slots % 128)))
         spread = jnp.broadcast_to(col_stats[None], (n_seq,) + col_stats.shape)
         spread, row_got = lax.optimization_barrier((spread, row_got))
-        col_got = lax.all_to_all(spread, "seq", 0, 0, tiled=True)
+        col_got = lax.all_to_all(spread, SEQ, 0, 0, tiled=True)
         col_got, weights = lax.optimization_barrier((col_got, weights))
         row_peak, row_total, row_dot = merge_stats(row_got)
         col_peak, col_total, col_dot = merge_stats(col_got[:, :, :slots])
@@ -148,7 +150,14 @@
             tokens, logit_grad, (((0,), (0,)), ((), ())), preferred_element_type=F32
         ).astype(BF)
         both = jnp.concatenate([phi_term, slot_term], axis=1)
-        got = lax.all_to_all(both.reshape(n_seq, -1, 2 * slots), "seq", 0, 0, tiled=True)
+        pairs = both.reshape(n_seq // 2, 2, -1, 2 * slots)
+        first = lax.axis_index("core") == 0
+        kept = jnp.where(first, pairs[:, 0], pairs[:, 1])
+        lent = jnp.where(first, pairs[:, 1], pairs[:, 0])
+        lent = lax.ppermute(lent, "core", [(0, 1), (1, 0)])
+        pair_sum = (kept.astype(F32) + lent.astype(F32)).astype(BF)
+        pair_sum, factors = lax.optimization_barrier((pair_sum, factors))
+        got = lax.all_to_all(pair_sum, "chip", 0, 0, tiled=True)
 
         blocks = column_blocks(factors, weights, groups, wide)
         token_sum = blocks[0].astype(F32)
@@ -166,10 +175,12 @@
 
 
 def solution(mesh):
+    n_seq, n_exp = mesh.devices.shape
+    fine = Mesh(mesh.devices.reshape(n_seq // 2, 2, n_exp), ("chip", "core", "exp"))
     return jax.shard_map(
-        make_per_device(mesh.shape["seq"], mesh.shape["exp"]),
-        mesh=mesh,
-        in_specs=(P("seq", None), P("seq", "exp"), P("exp", None), P("exp", None), P("seq", None)),
-        out_specs=(P("seq", "exp"), P("seq", "exp"), P("exp", "seq")),
+        make_per_device(n_seq, n_exp),
+        mesh=fine,
+        in_specs=(P(SEQ, None), P(SEQ, "exp"), P("exp", None), P("exp", None), P(SEQ, None)),
+        out_specs=(P(SEQ, "exp"), P(SEQ, "exp"), P("exp", SEQ)),
         check_vma=False,
     )

time: 148 us -> 151 us (1.020)
  other arithmetic: 4.2 us -> 6.83 us
    ppermute x3, waiting for transfers between devices: 6.02 us -> 9.27 us  [per_device(): token_sum = token_sum + lax.ppermute(blocks[i], 'exp', turn).astype(F32)]
    all_to_all x2, waiting for transfers between devices: 6.46 us -> 3.34 us  [the longest x1 3.33 us: per_device(): col_got = lax.all_to_all(spread, SEQ, 0, 0, tiled=True)]
    ppermute x0 -> x1, starting transfers between devices: none -> 2.29 us  [per_device(): lent = lax.ppermute(lent, 'core', [(0, 1), (1, 0)])]
    convert_element_type x0 -> x1, other arithmetic: none -> 1.85 us  [per_device(): pair_sum = (kept.astype(F32) + lent.astype(F32)).astype(BF)]
  transfers between devices with their start and end apart: 13 -> 14, of which waited for: 8 -> 8; matrix products, arithmetic and copies ran while one was open for 5% -> 6% of each run, Pallas kernels for 1% -> 1%
where the time goes in v6:
time: 151 us; the launch traced here: 150 us
  starting transfers between devices  77.1 us (51%)
  waiting for transfers between devices  47.2 us (31%)
  local copies, waits for them, and re-layouts  10.9 us (7%)
  other arithmetic  6.83 us (5%)
  matrix products  5.09 us (3%)
  Pallas kernels  1.82 us (1%)
    all_to_all x2, waiting for transfers between devices, gather_blocks(): return lax.all_to_all(spread, axis, 0, 0, tiled=True)  31.3 us
    all_to_all x2, starting transfers between devices, gather_blocks(): return lax.all_to_all(spread, axis, 0, 0, tiled=True)  30.2 us
    ppermute x6, starting transfers between devices, swap(): return lax.ppermute(x, 'exp', [(j, j ^ k) for j in range(n_exp)])  16.8 us
    all_to_all x1, starting transfers between devices, per_device(): got = lax.all_to_all(pair_sum, 'chip', 0, 0, tiled=True)  12.2 us
    ppermute x3, starting transfers between devices, per_device(): token_sum = token_sum + lax.ppermute(blocks[i], 'exp', turn).astype(F32)  10.1 us
    ppermute x3, waiting for transfers between devices, per_device(): token_sum = token_sum + lax.ppermute(blocks[i], 'exp', turn).astype(F32)  9.27 us
    all_to_all x1, starting transfers between devices, per_device(): col_got = lax.all_to_all(spread, SEQ, 0, 0, tiled=True)  5.43 us
    all_to_all x1, waiting for transfers between devices, per_device(): col_got = lax.all_to_all(spread, SEQ, 0, 0, tiled=True)  3.33 us
  transfers between devices with their start and end apart: 14, of which 8 were waited for; matrix products, arithmetic and copies ran while one was open for 6% of the time, Pallas kernels for 1%

profile of v6, /device:TPU:1, one launch (start us, length us, event | category | flops | bytes accessed | tf_op | source)
XLA Modules:
  0.0 149.9 jit_solution(13127190078657262762)
XLA Ops:
  0.6 0.0 copy-start
  0.6 0.9 fusion.19
  1.5 0.1 pad_maximum_fusion.4
  1.6 0.7 broadcast_in_dim.6
  2.3 23.3 %all-to-all-start = ((bf16[64,16,128]{2,1,0:T(8,128)(2,1)}), bf16[64,16,128]{2,1,0:T(8,128)(2,1)S(1)}, u32[]{:S(2)}, u32[]{:S(2)}) async-start(bf16[64,16,128]{2,1,0:T(8,128)(2,1)} %broadcast_in_dim.6), calls=%async_computation | async-start | bytes 524288 | tf_op jit(solution)/shard_map/all_to_all | solution.py:17
  25.6 0.0 copy-done
  25.6 1.7 %fusion.20 = f32[512,64]{0,1:T(8,128)S(1)} fusion(bf16[512,2048]{1,0:T(8,128)(2,1)S(1)} %copy-done, bf16[64,2048]{1,0:T(8,128)(2,1)} %sig_ref.1), kind=kOutput, calls=%fused_computation.54 | convolution fusion | flops 134217728 | bytes 2490368 | tf_op jit(solution)/shard_map/dot_general | solution.py:103
  27.3 22.1 %all-to-all-done = bf16[64,16,128]{2,1,0:T(8,128)(2,1)S(1)} async-done(((bf16[64,16,128]{2,1,0:T(8,128)(2,1)}), bf16[64,16,128]{2,1,0:T(8,128)(2,1)S(1)}, u32[]{:S(2)}, u32[]{:S(2)}) %all-to-all-start) | async-done | bytes 262176 | tf_op jit(solution)/shard_map/all_to_all | solution.py:17
  49.4 0.1 fusion.18
  49.5 0.0 copy-start.2
  49.6 0.0 copy-start.6
  49.6 0.1 pad_maximum_fusion
  49.7 0.9 fusion.17
  50.5 0.2 fusion.8
  50.7 0.4 copy-done.2
  51.1 1.5 %fusion.5 = (f32[512]{0:T(512)S(1)}, f32[64]{0:T(128)S(1)}, f32[512,64]{0,1:T(8,128)}) fusion(f32[64,512]{1,0:T(8,128)S(1)} %get-tuple-element.65, f32[512]{0:T(512)S(1)} %get-tuple-element.53, f32[512,64]{0,1:T(8,128)S(1)} %fusion.20, f32[64]{0:T(128)S(1)} %get-tuple-element.54, bf16[512,2048]{1,0:T(8,128)(2,1)S(1)} %copy-done.2, ...), kind=kOutput, calls=%fused_computation.21 | convolution fusion | flops 134413760 | bytes 2757120 | tf_op jit(solution)/shard_map/dot_general | solution.py:106
  52.7 0.7 broadcast_in_dim.8
  53.3 7.0 %all-to-all-start.1 = ((f32[16,3,512]{2,1,0:T(4,128)}), f32[16,3,512]{2,1,0:T(4,128)S(1)}, u32[]{:S(2)}, u32[]{:S(2)}) async-start(f32[16,3,512]{2,1,0:T(4,128)} %broadcast_in_dim.8), calls=%async_computation.1 | async-start | bytes 262144 | tf_op jit(solution)/shard_map/all_to_all | solution.py:17
  60.3 9.2 %all-to-all-done.1 = f32[16,3,512]{2,1,0:T(4,128)S(1)} async-done(((f32[16,3,512]{2,1,0:T(4,128)}), f32[16,3,512]{2,1,0:T(4,128)S(1)}, u32[]{:S(2)}, u32[]{:S(2)}) %all-to-all-start.1) | async-done | bytes 98336 | tf_op jit(solution)/shard_map/all_to_all | solution.py:17
  69.5 0.7 broadcast_in_dim.7
  70.2 5.4 %all-to-all-start.2 = ((f32[64,3,128]{2,1,0:T(4,128)}), f32[64,3,128]{2,1,0:T(4,128)S(1)}, u32[]{:S(2)}, u32[]{:S(2)}) async-start(f32[64,3,128]{2,1,0:T(4,128)} %broadcast_in_dim.7), calls=%async_computation.2 | async-start | bytes 262144 | tf_op jit(solution)/shard_map/all_to_all | solution.py:130
  75.7 0.8 copy.52
  76.5 0.1 pad_add_fusion.place_ref
  76.6 0.8 copy.44
  77.4 1.1 shard_map.76
  78.6 2.2 %collective-permute-start = (bf16[128,512]{1,0:T(8,128)(2,1)S(1)}, bf16[128,512]{1,0:T(8,128)(2,1)S(1)}, u32[]{:S(2)}, u32[]{:S(2)}) collective-permute-start(bf16[128,512]{1,0:T(8,128)(2,1)S(1)} %get-tuple-element.28), channel_id=1, source_target_pairs={{0,1},{1,0},{2,3},{3,2},{4,5},{5,4},{6,7},{7,6},{8,9},{9,8},{10,11... | collective-permute-start | bytes 393224 | tf_op jit(solution)/shard_map/ppermute | solution.py:90
  80.8 2.0 %collective-permute-start.1 = (bf16[128,512]{1,0:T(8,128)(2,1)S(1)}, bf16[128,512]{1,0:T(8,128)(2,1)S(1)}, u32[]{:S(2)}, u32[]{:S(2)}) collective-permute-start(bf16[128,512]{1,0:T(8,128)(2,1)S(1)} %get-tuple-element.29), channel_id=1, source_target_pairs={{0,2},{1,3},{2,0},{3,1},{4,6},{5,7},{6,4},{7,5},{8,10},{9,11},{10,... | collective-permute-start | bytes 393224 | tf_op jit(solution)/shard_map/ppermute | solution.py:90
  82.8 4.2 %collective-permute-start.2 = (bf16[128,512]{1,0:T(8,128)(2,1)S(1)}, bf16[128,512]{1,0:T(8,128)(2,1)S(1)}, u32[]{:S(2)}, u32[]{:S(2)}) collective-permute-start(bf16[128,512]{1,0:T(8,128)(2,1)S(1)} %get-tuple-element.30), channel_id=1, source_target_pairs={{0,3},{1,2},{2,1},{3,0},{4,7},{5,6},{6,5},{7,4},{8,11},{9,10},{10,... | collective-permute-start | bytes 393224 | tf_op jit(solution)/shard_map/ppermute | solution.py:90
  87.0 1.0 copy.51
  88.0 0.9 copy.47
  89.0 0.9 slice.57
  90.0 0.0 collective-permute-done.refs_5_
  90.0 0.0 collective-permute-done.1.refs_6_
  90.0 1.1 collective-permute-done.2.refs_7_
  91.0 3.3 %all-to-all-done.2 = f32[64,3,128]{2,1,0:T(4,128)S(1)} async-done(((f32[64,3,128]{2,1,0:T(4,128)}), f32[64,3,128]{2,1,0:T(4,128)S(1)}, u32[]{:S(2)}, u32[]{:S(2)}) %all-to-all-start.2) | async-done | bytes 98336 | tf_op jit(solution)/shard_map/all_to_all | solution.py:130
  94.5 1.3 bitcast_convert_fusion
  95.8 1.3 fusion.4
  97.1 0.1 pad_maximum_fusion.2.refs_0_
  97.3 0.5 fusion
  97.8 0.5 fusion.1
  98.3 0.8 pad_maximum_fusion.1
  99.1 1.3 copy.53
  100.5 0.7 copy-done.4
  101.2 2.3 %collective-permute-start.3 = (bf16[32,32,128]{2,1,0:T(8,128)(2,1)S(1)}, bf16[32,32,128]{2,1,0:T(8,128)(2,1)S(1)}, u32[]{:S(2)}, u32[]{:S(2)}) collective-permute-start(bf16[32,32,128]{2,1,0:T(8,128)(2,1)S(1)} %select_bitcast_fusion), channel_id=1, source_target_pairs={{0,16},{16,0},{1,17},{17,1},{2,18},{18,2},{3,19},{19,3},{4,20},{20... | collective-permute-start | bytes 786440 | tf_op jit(solution)/shard_map/ppermute | solution.py:157
  103.5 2.2 %collective-permute-start.4 = (bf16[512,128]{1,0:T(8,128)(2,1)S(1)}, bf16[512,128]{1,0:T(8,128)(2,1)S(1)}, u32[]{:S(2)}, u32[]{:S(2)}) collective-permute-start(bf16[512,128]{1,0:T(8,128)(2,1)S(1)} %pad_maximum_fusion.2.refs_0_), channel_id=1, source_target_pairs={{0,1},{1,0},{2,3},{3,2},{4,5},{5,4},{6,7},{7,6},{8,9},{9,8},{10,11... | collective-permute-start | bytes 393224 | tf_op jit(solution)/shard_map/ppermute | solution.py:90
  105.8 2.0 %collective-permute-start.5 = (bf16[512,128]{1,0:T(8,128)(2,1)S(1)}, bf16[512,128]{1,0:T(8,128)(2,1)S(1)}, u32[]{:S(2)}, u32[]{:S(2)}) collective-permute-start(bf16[512,128]{1,0:T(8,128)(2,1)S(1)} %pad_maximum_fusion.2.refs_0_), channel_id=1, source_target_pairs={{0,2},{1,3},{2,0},{3,1},{4,6},{5,7},{6,4},{7,5},{8,10},{9,11},{10,... | collective-permute-start | bytes 393224 | tf_op jit(solution)/shard_map/ppermute | solution.py:90
  107.8 4.2 %collective-permute-start.6 = (bf16[512,128]{1,0:T(8,128)(2,1)S(1)}, bf16[512,128]{1,0:T(8,128)(2,1)S(1)}, u32[]{:S(2)}, u32[]{:S(2)}) collective-permute-start(bf16[512,128]{1,0:T(8,128)(2,1)S(1)} %pad_maximum_fusion.2.refs_0_), channel_id=1, source_target_pairs={{0,3},{1,2},{2,1},{3,0},{4,7},{5,6},{6,5},{7,4},{8,11},{9,10},{10,... | collective-permute-start | bytes 393224 | tf_op jit(solution)/shard_map/ppermute | solution.py:90
  112.0 0.0 collective-permute-done.3
  112.0 1.8 %fusion.2 = bf16[32,32,128]{2,1,0:T(8,128)(2,1)} fusion(bf16[32,32,128]{2,1,0:T(8,128)(2,1)S(1)} %collective-permute-done.3, pred[]{:T(512)S(6)} %eq.3, bf16[32,2,32,128]{3,2,1,0:T(8,128)(2,1)} %bitcast.88), kind=kLoop, calls=%fused_computation.7 | loop fusion | flops 655360 | bytes 1048577 | tf_op jit(solution)/shard_map/convert_element_type | solution.py:158
  113.8 0.0 collective-permute-done.4.refs_1_
  113.8 0.0 collective-permute-done.5.refs_2_
  113.8 2.3 %collective-permute-done.6.refs_3_ = bf16[512,128]{1,0:T(8,128)(2,1)S(1)} collective-permute-done((bf16[512,128]{1,0:T(8,128)(2,1)S(1)}, bf16[512,128]{1,0:T(8,128)(2,1)S(1)}, u32[]{:S(2)}, u32[]{:S(2)}) %collective-permute-start.6) | collective-permute-done | bytes 131104 | tf_op jit(solution)/shard_map/ppermute | solution.py:90
  116.1 12.2 %all-to-all-start.3 = ((bf16[32,32,128]{2,1,0:T(8,128)(2,1)}), bf16[32,32,128]{2,1,0:T(8,128)(2,1)S(1)}, u32[]{:S(2)}, u32[]{:S(2)}) async-start(bf16[32,32,128]{2,1,0:T(8,128)(2,1)} %fusion.2), calls=%async_computation.3 | async-start | bytes 524288 | tf_op jit(solution)/shard_map/all_to_all | solution.py:160
  128.3 0.7 shard_map.77
  129.0 2.7 %collective-permute-start.7 = (bf16[512,128]{1,0:T(8,128)(2,1)S(1)}, bf16[512,128]{1,0:T(8,128)(2,1)S(1)}, u32[]{:S(2)}, u32[]{:S(2)}) collective-permute-start(bf16[512,128]{1,0:T(8,128)(2,1)S(1)} %get-tuple-element.45), channel_id=1, source_target_pairs={{0,8},{1,9},{2,10},{3,11},{4,12},{5,13},{6,14},{7,15},{8,0},{9,1},... | collective-permute-start | bytes 393224 | tf_op jit(solution)/shard_map/ppermute | solution.py:166
  131.7 3.6 %collective-permute-start.8 = (bf16[512,128]{1,0:T(8,128)(2,1)S(1)}, bf16[512,128]{1,0:T(8,128)(2,1)S(1)}, u32[]{:S(2)}, u32[]{:S(2)}) collective-permute-start(bf16[512,128]{1,0:T(8,128)(2,1)S(1)} %get-tuple-element.46), channel_id=1, source_target_pairs={{0,4},{1,5},{2,6},{3,7},{4,8},{5,9},{6,10},{7,11},{8,12},{9,13},{1... | collective-permute-start | bytes 393224 | tf_op jit(solution)/shard_map/ppermute | solution.py:166
  135.3 3.8 %collective-permute-start.9 = (bf16[512,128]{1,0:T(8,128)(2,1)S(1)}, bf16[512,128]{1,0:T(8,128)(2,1)S(1)}, u32[]{:S(2)}, u32[]{:S(2)}) collective-permute-start(bf16[512,128]{1,0:T(8,128)(2,1)S(1)} %get-tuple-element.47), channel_id=1, source_target_pairs={{0,12},{1,13},{2,14},{3,15},{4,0},{5,1},{6,2},{7,3},{8,4},{9,5},{1... | collective-permute-start | bytes 393224 | tf_op jit(solution)/shard_map/ppermute | solution.py:166
  139.1 0.3 collective-permute-done.7
  139.4 3.7 %collective-permute-done.8 = bf16[512,128]{1,0:T(8,128)(2,1)S(1)} collective-permute-done((bf16[512,128]{1,0:T(8,128)(2,1)S(1)}, bf16[512,128]{1,0:T(8,128)(2,1)S(1)}, u32[]{:S(2)}, u32[]{:S(2)}) %collective-permute-start.8) | collective-permute-done | bytes 131104 | tf_op jit(solution)/shard_map/ppermute | solution.py:166
  143.1 5.3 %collective-permute-done.9 = bf16[512,128]{1,0:T(8,128)(2,1)S(1)} collective-permute-done((bf16[512,128]{1,0:T(8,128)(2,1)S(1)}, bf16[512,128]{1,0:T(8,128)(2,1)S(1)}, u32[]{:S(2)}, u32[]{:S(2)}) %collective-permute-start.9) | collective-permute-done | bytes 131104 | tf_op jit(solution)/shard_map/ppermute | solution.py:166
  148.4 0.7 add_convert_fusion
  149.2 0.0 all-to-all-done.3
  149.2 0.0 copy-start.7
  149.2 0.7 fusion.16
  (21 shorter events, 0.3 us)
Async XLA Ops:
  0.6 25.0 %copy-start = (bf16[512,2048]{1,0:T(8,128)(2,1)S(1)}, bf16[512,2048]{1,0:T(8,128)(2,1)}, u32[]{:S(2)}) copy-start(bf16[512,2048]{1,0:T(8,128)(2,1)} %param.5) | copy-start | bytes 6291460
  2.3 47.1 %all-to-all-start = ((bf16[64,16,128]{2,1,0:T(8,128)(2,1)}), bf16[64,16,128]{2,1,0:T(8,128)(2,1)S(1)}, u32[]{:S(2)}, u32[]{:S(2)}) async-start(bf16[64,16,128]{2,1,0:T(8,128)(2,1)} %broadcast_in_dim.6), calls=%async_computation | async-start | bytes 524288 | tf_op jit(solution)/shard_map/all_to_all | solution.py:17
  49.5 1.6 %copy-start.2 = (bf16[512,2048]{1,0:T(8,128)(2,1)S(1)}, bf16[512,2048]{1,0:T(8,128)(2,1)}, u32[]{:S(2)}) copy-start(bf16[512,2048]{1,0:T(8,128)(2,1)} %param.9) | copy-start | bytes 6291460
  49.6 1.6 %copy-start.6 = (bf16[64,2048]{1,0:T(8,128)(2,1)S(1)}, bf16[64,2048]{1,0:T(8,128)(2,1)}, u32[]{:S(2)}) copy-start(bf16[64,2048]{1,0:T(8,128)(2,1)} %param.7) | copy-start | bytes 786436
  51.1 26.3 %copy-start.1 = (bf16[64,2048]{1,0:T(8,128)(2,1)S(1)}, bf16[64,2048]{1,0:T(8,128)(2,1)}, u32[]{:S(2)}) copy-start(bf16[64,2048]{1,0:T(8,128)(2,1)} %sig_ref.1) | copy-start | bytes 786436
  53.3 16.2 %all-to-all-start.1 = ((f32[16,3,512]{2,1,0:T(4,128)}), f32[16,3,512]{2,1,0:T(4,128)S(1)}, u32[]{:S(2)}, u32[]{:S(2)}) async-start(f32[16,3,512]{2,1,0:T(4,128)} %broadcast_in_dim.8), calls=%async_computation.1 | async-start | bytes 262144 | tf_op jit(solution)/shard_map/all_to_all | solution.py:17
  69.5 7.1 %copy-start.5 = (f32[16,3,512]{2,1,0:T(4,128)}, f32[16,3,512]{2,1,0:T(4,128)S(1)}, u32[]{:S(2)}) copy-start(f32[16,3,512]{2,1,0:T(4,128)S(1)} %all-to-all-done.1) | copy-start | bytes 294916
  70.2 24.1 %all-to-all-start.2 = ((f32[64,3,128]{2,1,0:T(4,128)}), f32[64,3,128]{2,1,0:T(4,128)S(1)}, u32[]{:S(2)}, u32[]{:S(2)}) async-start(f32[64,3,128]{2,1,0:T(4,128)} %broadcast_in_dim.7), calls=%async_computation.2 | async-start | bytes 262144 | tf_op jit(solution)/shard_map/all_to_all | solution.py:130
  78.6 11.4 %collective-permute-start = (bf16[128,512]{1,0:T(8,128)(2,1)S(1)}, bf16[128,512]{1,0:T(8,128)(2,1)S(1)}, u32[]{:S(2)}, u32[]{:S(2)}) collective-permute-start(bf16[128,512]{1,0:T(8,128)(2,1)S(1)} %get-tuple-element.28), channel_id=1, source_target_pairs={{0,1},{1,0},{2,3},{3,2},{4,5},{5,4},{6,7},{7,6},{8,9},{9,8},{10,11... | collective-permute-start | bytes 393224 | tf_op jit(solution)/shard_map/ppermute | solution.py:90
  80.8 9.2 %collective-permute-start.1 = (bf16[128,512]{1,0:T(8,128)(2,1)S(1)}, bf16[128,512]{1,0:T(8,128)(2,1)S(1)}, u32[]{:S(2)}, u32[]{:S(2)}) collective-permute-start(bf16[128,512]{1,0:T(8,128)(2,1)S(1)} %get-tuple-element.29), channel_id=1, source_target_pairs={{0,2},{1,3},{2,0},{3,1},{4,6},{5,7},{6,4},{7,5},{8,10},{9,11},{10,... | collective-permute-start | bytes 393224 | tf_op jit(solution)/shard_map/ppermute | solution.py:90
  82.8 8.3 %collective-permute-start.2 = (bf16[128,512]{1,0:T(8,128)(2,1)S(1)}, bf16[128,512]{1,0:T(8,128)(2,1)S(1)}, u32[]{:S(2)}, u32[]{:S(2)}) collective-permute-start(bf16[128,512]{1,0:T(8,128)(2,1)S(1)} %get-tuple-element.30), channel_id=1, source_target_pairs={{0,3},{1,2},{2,1},{3,0},{4,7},{5,6},{6,5},{7,4},{8,11},{9,10},{10,... | collective-permute-start | bytes 393224 | tf_op jit(solution)/shard_map/ppermute | solution.py:90
  94.5 3.3 %copy-start.3 = (bf16[512,2048]{1,0:T(8,128)(2,1)S(1)}, bf16[512,2048]{1,0:T(8,128)(2,1)}, u32[]{:S(2)}) copy-start(bf16[512,2048]{1,0:T(8,128)(2,1)} %param.9) | copy-start | bytes 6291460
  100.4 0.8 copy-start.4
  101.2 10.7 %collective-permute-start.3 = (bf16[32,32,128]{2,1,0:T(8,128)(2,1)S(1)}, bf16[32,32,128]{2,1,0:T(8,128)(2,1)S(1)}, u32[]{:S(2)}, u32[]{:S(2)}) collective-permute-start(bf16[32,32,128]{2,1,0:T(8,128)(2,1)S(1)} %select_bitcast_fusion), channel_id=1, source_target_pairs={{0,16},{16,0},{1,17},{17,1},{2,18},{18,2},{3,19},{19,3},{4,20},{20... | collective-permute-start | bytes 786440 | tf_op jit(solution)/shard_map/ppermute | solution.py:157
  103.5 10.3 %collective-permute-start.4 = (bf16[512,128]{1,0:T(8,128)(2,1)S(1)}, bf16[512,128]{1,0:T(8,128)(2,1)S(1)}, u32[]{:S(2)}, u32[]{:S(2)}) collective-permute-start(bf16[512,128]{1,0:T(8,128)(2,1)S(1)} %pad_maximum_fusion.2.refs_0_), channel_id=1, source_target_pairs={{0,1},{1,0},{2,3},{3,2},{4,5},{5,4},{6,7},{7,6},{8,9},{9,8},{10,11... | collective-permute-start | bytes 393224 | tf_op jit(solution)/shard_map/ppermute | solution.py:90
  105.8 8.0 %collective-permute-start.5 = (bf16[512,128]{1,0:T(8,128)(2,1)S(1)}, bf16[512,128]{1,0:T(8,128)(2,1)S(1)}, u32[]{:S(2)}, u32[]{:S(2)}) collective-permute-start(bf16[512,128]{1,0:T(8,128)(2,1)S(1)} %pad_maximum_fusion.2.refs_0_), channel_id=1, source_target_pairs={{0,2},{1,3},{2,0},{3,1},{4,6},{5,7},{6,4},{7,5},{8,10},{9,11},{10,... | collective-permute-start | bytes 393224 | tf_op jit(solution)/shard_map/ppermute | solution.py:90
  107.8 8.3 %collective-permute-start.6 = (bf16[512,128]{1,0:T(8,128)(2,1)S(1)}, bf16[512,128]{1,0:T(8,128)(2,1)S(1)}, u32[]{:S(2)}, u32[]{:S(2)}) collective-permute-start(bf16[512,128]{1,0:T(8,128)(2,1)S(1)} %pad_maximum_fusion.2.refs_0_), channel_id=1, source_target_pairs={{0,3},{1,2},{2,1},{3,0},{4,7},{5,6},{6,5},{7,4},{8,11},{9,10},{10,... | collective-permute-start | bytes 393224 | tf_op jit(solution)/shard_map/ppermute | solution.py:90
  116.1 33.1 %all-to-all-start.3 = ((bf16[32,32,128]{2,1,0:T(8,128)(2,1)}), bf16[32,32,128]{2,1,0:T(8,128)(2,1)S(1)}, u32[]{:S(2)}, u32[]{:S(2)}) async-start(bf16[32,32,128]{2,1,0:T(8,128)(2,1)} %fusion.2), calls=%async_computation.3 | async-start | bytes 524288 | tf_op jit(solution)/shard_map/all_to_all | solution.py:160
  129.0 10.4 %collective-permute-start.7 = (bf16[512,128]{1,0:T(8,128)(2,1)S(1)}, bf16[512,128]{1,0:T(8,128)(2,1)S(1)}, u32[]{:S(2)}, u32[]{:S(2)}) collective-permute-start(bf16[512,128]{1,0:T(8,128)(2,1)S(1)} %get-tuple-element.45), channel_id=1, source_target_pairs={{0,8},{1,9},{2,10},{3,11},{4,12},{5,13},{6,14},{7,15},{8,0},{9,1},... | collective-permute-start | bytes 393224 | tf_op jit(solution)/shard_map/ppermute | solution.py:166
  131.7 11.4 %collective-permute-start.8 = (bf16[512,128]{1,0:T(8,128)(2,1)S(1)}, bf16[512,128]{1,0:T(8,128)(2,1)S(1)}, u32[]{:S(2)}, u32[]{:S(2)}) collective-permute-start(bf16[512,128]{1,0:T(8,128)(2,1)S(1)} %get-tuple-element.46), channel_id=1, source_target_pairs={{0,4},{1,5},{2,6},{3,7},{4,8},{5,9},{6,10},{7,11},{8,12},{9,13},{1... | collective-permute-start | bytes 393224 | tf_op jit(solution)/shard_map/ppermute | solution.py:166
  135.3 13.1 %collective-permute-start.9 = (bf16[512,128]{1,0:T(8,128)(2,1)S(1)}, bf16[512,128]{1,0:T(8,128)(2,1)S(1)}, u32[]{:S(2)}, u32[]{:S(2)}) collective-permute-start(bf16[512,128]{1,0:T(8,128)(2,1)S(1)} %get-tuple-element.47), channel_id=1, source_target_pairs={{0,12},{1,13},{2,14},{3,15},{4,0},{5,1},{6,2},{7,3},{8,4},{9,5},{1... | collective-permute-start | bytes 393224 | tf_op jit(solution)/shard_map/ppermute | solution.py:166
  149.2 0.7 copy-start.7

commit v7 on v5

--- a/solution.py
+++ b/solution.py
@@ -22,6 +22,23 @@
     total = jnp.sum(total * scale, axis=0)
     dot = jnp.sum(dot * scale, axis=0)
     return top, total, dot / total
+
+
+def copies_kernel(block_ref, out_ref):
+    half = block_ref.shape[0] // 2
+    packed = jnp.concatenate([block_ref[:half], block_ref[half:]], axis=1)
+    out_ref[...] = jnp.broadcast_to(packed[None], out_ref.shape)
+
+
+def packed_copies(block, n):
+    rows, width = block.shape
+    return pl.pallas_call(
+        copies_kernel,
+        out_shape=jax.ShapeDtypeStruct((n, rows // 2, 2 * width), block.dtype),
+        cost_estimate=pl.CostEstimate(
+            flops=0, bytes_accessed=2 * (n + 1) * rows * width, transcendentals=0
+        ),
+    )(block)
 
 
 def weights_kernel(place_ref, sig_ref, phi_ref, *out_refs):
@@ -91,9 +108,7 @@
         rows, width = tokens.shape
         slots = expert_out.shape[0]
         wide = width // n_exp
-        half = phi.shape[0] // 2
-        packed = jnp.concatenate([phi[:half], phi[half:]], axis=1)
-        got_phi = gather_blocks(packed, "seq", n_seq)
+        got_phi = lax.all_to_all(packed_copies(phi, n_seq), "seq", 0, 0, tiled=True)
         phi_full = jnp.concatenate([got_phi[:, :, :slots], got_phi[:, :, slots:]], axis=1)
         phi_full = phi_full.reshape(width, slots)
 
@@ -124,9 +139,8 @@
         row_got = gather_blocks(row_stats, "exp", n_exp)
         col_stats = jnp.pad(col_stats, ((0, 0), (0, -slots % 128)))
         spread = jnp.broadcast_to(col_stats[None], (n_seq,) + col_stats.shape)
-        spread, row_got = lax.optimization_barrier((spread, row_got))
+        spread, row_got, weights = lax.optimization_barrier((spread, row_got, weights))
         col_got = lax.all_to_all(spread, "seq", 0, 0, tiled=True)
-        col_got, weights = lax.optimization_barrier((col_got, weights))
         row_peak, row_total, row_dot = merge_stats(row_got)
         col_peak, col_total, col_dot = merge_stats(col_got[:, :, :slots])
 

time: 148 us -> 146 us (0.986)
  waiting for transfers between devices: 48.5 us -> 54.6 us
  starting transfers between devices: 76.5 us -> 71.6 us
  local copies, waits for them, and re-layouts: 9.81 us -> 6.77 us
  Pallas kernels: 1.82 us -> 3.46 us
    all_to_all x2 -> x1, waiting for transfers between devices: 31.3 us -> 0.01 us  [gather_blocks(): return lax.all_to_all(spread, axis, 0, 0, tiled=True)]
    all_to_all x2 -> x1, starting transfers between devices: 30.2 us -> 6.95 us  [gather_blocks(): return lax.all_to_all(spread, axis, 0, 0, tiled=True)]
    all_to_all x0 -> x1, starting transfers between devices: none -> 23.3 us  [per_device(): got_phi = lax.all_to_all(packed_copies(phi, n_seq), 'seq', 0, 0, tiled=True)]
    all_to_all x0 -> x1, waiting for transfers between devices: none -> 22.1 us  [per_device(): got_phi = lax.all_to_all(packed_copies(phi, n_seq), 'seq', 0, 0, tiled=True)]
    all_to_all x1, waiting for transfers between devices: 3.33 us -> 16.4 us  [per_device(): col_got = lax.all_to_all(spread, 'seq', 0, 0, tiled=True)]
    all_to_all x1, starting transfers between devices: 12.8 us -> 4.46 us  [per_device(): lax.all_to_all(both.reshape(n_seq, -1, 2 * slots), 'seq', 0, 0, tiled=True)]
    ppermute x6, waiting for transfers between devices: 4.69 us -> 8.69 us  [swap(): return lax.ppermute(x, 'exp', [(j, j ^ k) for j in range(n_exp)])]
    ppermute x3, starting transfers between devices: 11.4 us -> 13.7 us  [per_device(): token_sum = token_sum + lax.ppermute(blocks[i], 'exp', turn).astype(F32)]
  transfers between devices with their start and end apart: 13 -> 13, of which waited for: 8 -> 8; matrix products, arithmetic and copies ran while one was open for 5% -> 3% of each run, Pallas kernels for 1% -> 1%
where the time goes in v7:
time: 146 us
  starting transfers between devices  71.6 us (49%)
  waiting for transfers between devices  54.6 us (37%)
  local copies, waits for them, and re-layouts  6.77 us (5%)
  matrix products  5.09 us (3%)
  Pallas kernels  3.46 us (2%)
  other arithmetic  3.07 us (2%)
    all_to_all x1, starting transfers between devices, per_device(): got_phi = lax.all_to_all(packed_copies(phi, n_seq), 'seq', 0, 0, tiled=True)  23.3 us
    all_to_all x1, waiting for transfers between devices, per_device(): got_phi = lax.all_to_all(packed_copies(phi, n_seq), 'seq', 0, 0, tiled=True)  22.1 us
    ppermute x6, starting transfers between devices, swap(): return lax.ppermute(x, 'exp', [(j, j ^ k) for j in range(n_exp)])  16.8 us
    all_to_all x1, waiting for transfers between devices, per_device(): col_got = lax.all_to_all(spread, 'seq', 0, 0, tiled=True)  16.4 us
    ppermute x3, starting transfers between devices, per_device(): token_sum = token_sum + lax.ppermute(blocks[i], 'exp', turn).astype(F32)  13.7 us
    ppermute x6, waiting for transfers between devices, swap(): return lax.ppermute(x, 'exp', [(j, j ^ k) for j in range(n_exp)])  8.69 us
    all_to_all x1, starting transfers between devices, gather_blocks(): return lax.all_to_all(spread, axis, 0, 0, tiled=True)  6.95 us
    all_to_all x1, starting transfers between devices, per_device(): col_got = lax.all_to_all(spread, 'seq', 0, 0, tiled=True)  6.41 us
  transfers between devices with their start and end apart: 13, of which 8 were waited for; matrix products, arithmetic and copies ran while one was open for 3% of the time, Pallas kernels for 1%

profile of v7, /device:TPU:1, one launch (start us, length us, event | category | flops | bytes accessed | tf_op | source)
XLA Modules:
  0.0 145.6 jit_solution(6562427774495928461)
XLA Ops:
  0.6 0.0 copy-start
  0.6 1.6 %shard_map.76 = bf16[64,16,128]{2,1,0:T(8,128)(2,1)} custom-call(bf16[32,64]{1,0:T(8,128)(2,1)} %block_ref.1), custom_call_target="tpu_custom_call" | custom-call | bytes 266240 | tf_op jit(solution)/shard_map/pallas_call | solution.py:35
  2.3 23.3 %all-to-all-start = ((bf16[64,16,128]{2,1,0:T(8,128)(2,1)}), bf16[64,16,128]{2,1,0:T(8,128)(2,1)S(1)}, u32[]{:S(2)}, u32[]{:S(2)}) async-start(bf16[64,16,128]{2,1,0:T(8,128)(2,1)} %shard_map.76), calls=%async_computation | async-start | bytes 524288 | tf_op jit(solution)/shard_map/all_to_all | solution.py:111
  25.6 0.0 copy-done
  25.6 1.7 %fusion.16 = f32[512,64]{0,1:T(8,128)S(1)} fusion(bf16[512,2048]{1,0:T(8,128)(2,1)S(1)} %copy-done, bf16[64,2048]{1,0:T(8,128)(2,1)} %sig_ref.1), kind=kOutput, calls=%fused_computation.46 | convolution fusion | flops 134217728 | bytes 2490368 | tf_op jit(solution)/shard_map/dot_general | solution.py:116
  27.3 22.1 %all-to-all-done = bf16[64,16,128]{2,1,0:T(8,128)(2,1)S(1)} async-done(((bf16[64,16,128]{2,1,0:T(8,128)(2,1)}), bf16[64,16,128]{2,1,0:T(8,128)(2,1)S(1)}, u32[]{:S(2)}, u32[]{:S(2)}) %all-to-all-start) | async-done | bytes 262176 | tf_op jit(solution)/shard_map/all_to_all | solution.py:111
  49.4 0.1 fusion.14
  49.5 0.0 copy-start.2
  49.5 0.0 copy-start.4
  49.5 0.1 pad_maximum_fusion
  49.7 0.9 fusion.13
  50.5 0.0 copy-start.1
  50.5 0.2 fusion.7
  50.7 0.4 copy-done.2
  51.1 0.0 copy-done.4
  51.1 1.5 %fusion.4 = (f32[512]{0:T(512)S(1)}, f32[64]{0:T(128)S(1)}, f32[512,64]{0,1:T(8,128)}) fusion(f32[64,512]{1,0:T(8,128)S(1)} %get-tuple-element.54, f32[512]{0:T(512)S(1)} %get-tuple-element.41, f32[512,64]{0,1:T(8,128)S(1)} %fusion.16, f32[64]{0:T(128)S(1)} %get-tuple-element.42, bf16[512,2048]{1,0:T(8,128)(2,1)S(1)} %copy-done.2, ...), kind=kOutput, calls=%fused_computation.18 | convolution fusion | flops 134413760 | bytes 2757120 | tf_op jit(solution)/shard_map/dot_general | solution.py:119
  52.7 0.7 broadcast_in_dim.5
  53.3 7.0 %all-to-all-start.1 = ((f32[16,3,512]{2,1,0:T(4,128)}), f32[16,3,512]{2,1,0:T(4,128)S(1)}, u32[]{:S(2)}, u32[]{:S(2)}) async-start(f32[16,3,512]{2,1,0:T(4,128)} %broadcast_in_dim.5), calls=%async_computation.1 | async-start | bytes 262144 | tf_op jit(solution)/shard_map/all_to_all | solution.py:15
  60.3 0.1 pad_add_fusion.place_ref
  60.4 0.0 copy-done.1
  60.4 1.1 shard_map.77
  61.5 3.3 %collective-permute-start = (bf16[128,512]{1,0:T(8,128)(2,1)S(1)}, bf16[128,512]{1,0:T(8,128)(2,1)S(1)}, u32[]{:S(2)}, u32[]{:S(2)}) collective-permute-start(bf16[128,512]{1,0:T(8,128)(2,1)S(1)} %get-tuple-element.21), channel_id=1, source_target_pairs={{0,1},{1,0},{2,3},{3,2},{4,5},{5,4},{6,7},{7,6},{8,9},{9,8},{10,11... | collective-permute-start | bytes 393224 | tf_op jit(solution)/shard_map/ppermute | solution.py:105
  64.8 3.1 %collective-permute-start.1 = (bf16[128,512]{1,0:T(8,128)(2,1)S(1)}, bf16[128,512]{1,0:T(8,128)(2,1)S(1)}, u32[]{:S(2)}, u32[]{:S(2)}) collective-permute-start(bf16[128,512]{1,0:T(8,128)(2,1)S(1)} %get-tuple-element.22), channel_id=1, source_target_pairs={{0,2},{1,3},{2,0},{3,1},{4,6},{5,7},{6,4},{7,5},{8,10},{9,11},{10,... | collective-permute-start | bytes 393224 | tf_op jit(solution)/shard_map/ppermute | solution.py:105
  67.9 2.0 %collective-permute-start.2 = (bf16[128,512]{1,0:T(8,128)(2,1)S(1)}, bf16[128,512]{1,0:T(8,128)(2,1)S(1)}, u32[]{:S(2)}, u32[]{:S(2)}) collective-permute-start(bf16[128,512]{1,0:T(8,128)(2,1)S(1)} %get-tuple-element.23), channel_id=1, source_target_pairs={{0,3},{1,2},{2,1},{3,0},{4,7},{5,6},{6,5},{7,4},{8,11},{9,10},{10,... | collective-permute-start | bytes 393224 | tf_op jit(solution)/shard_map/ppermute | solution.py:105
  69.9 0.0 collective-permute-done.refs_5_
  70.0 1.5 %collective-permute-done.1.refs_6_ = bf16[128,512]{1,0:T(8,128)(2,1)S(1)} collective-permute-done((bf16[128,512]{1,0:T(8,128)(2,1)S(1)}, bf16[128,512]{1,0:T(8,128)(2,1)S(1)}, u32[]{:S(2)}, u32[]{:S(2)}) %collective-permute-start.1) | collective-permute-done | bytes 131104 | tf_op jit(solution)/shard_map/ppermute | solution.py:105
  71.4 3.7 %collective-permute-done.2.refs_7_ = bf16[128,512]{1,0:T(8,128)(2,1)S(1)} collective-permute-done((bf16[128,512]{1,0:T(8,128)(2,1)S(1)}, bf16[128,512]{1,0:T(8,128)(2,1)S(1)}, u32[]{:S(2)}, u32[]{:S(2)}) %collective-permute-start.2) | collective-permute-done | bytes 131104 | tf_op jit(solution)/shard_map/ppermute | solution.py:105
  75.1 0.0 all-to-all-done.1
  75.1 0.7 broadcast_in_dim.4
  75.8 6.4 %all-to-all-start.2 = ((f32[64,3,128]{2,1,0:T(4,128)}), f32[64,3,128]{2,1,0:T(4,128)}, u32[]{:S(2)}, u32[]{:S(2)}) async-start(f32[64,3,128]{2,1,0:T(4,128)} %broadcast_in_dim.4), calls=%async_computation.2 | async-start | bytes 262144 | tf_op jit(solution)/shard_map/all_to_all | solution.py:143
  82.2 0.1 copy.48
  82.3 0.1 copy.40
  82.5 1.7 %copy.47 = f32[512,64]{1,0:T(8,128)} copy(f32[512,64]{0,1:T(8,128)} %get-tuple-element.55) | data formatting | bytes 262144 | tf_op jit(solution)/shard_map/dot_general | solution.py:119
  84.3 16.4 %all-to-all-done.2 = f32[64,3,128]{2,1,0:T(4,128)} async-done(((f32[64,3,128]{2,1,0:T(4,128)}), f32[64,3,128]{2,1,0:T(4,128)}, u32[]{:S(2)}, u32[]{:S(2)}) %all-to-all-start.2) | async-done | bytes 98336 | tf_op jit(solution)/shard_map/all_to_all | solution.py:143
  100.7 1.2 fusion.15
  101.9 0.0 copy-start.3
  101.9 0.2 bitcast_convert_fusion
  102.2 1.3 fusion.3
  103.5 0.1 pad_maximum_fusion.2.refs_0_
  103.6 0.5 fusion
  104.2 0.0 copy-done.3
  104.2 0.5 fusion.1
  104.7 1.0 copy.49
  105.7 4.5 %all-to-all-start.3 = ((bf16[64,32,128]{2,1,0:T(8,128)(2,1)}), bf16[64,32,128]{2,1,0:T(8,128)(2,1)S(1)}, u32[]{:S(2)}, u32[]{:S(2)}) async-start(bf16[64,32,128]{2,1,0:T(8,128)(2,1)} %bitcast.74), calls=%async_computation.3 | async-start | bytes 1048576 | tf_op jit(solution)/shard_map/all_to_all | solution.py:165
  110.2 2.2 %collective-permute-start.3 = (bf16[512,128]{1,0:T(8,128)(2,1)S(1)}, bf16[512,128]{1,0:T(8,128)(2,1)S(1)}, u32[]{:S(2)}, u32[]{:S(2)}) collective-permute-start(bf16[512,128]{1,0:T(8,128)(2,1)S(1)} %pad_maximum_fusion.2.refs_0_), channel_id=1, source_target_pairs={{0,1},{1,0},{2,3},{3,2},{4,5},{5,4},{6,7},{7,6},{8,9},{9,8},{10,11... | collective-permute-start | bytes 393224 | tf_op jit(solution)/shard_map/ppermute | solution.py:105
  112.4 2.8 %collective-permute-start.4 = (bf16[512,128]{1,0:T(8,128)(2,1)S(1)}, bf16[512,128]{1,0:T(8,128)(2,1)S(1)}, u32[]{:S(2)}, u32[]{:S(2)}) collective-permute-start(bf16[512,128]{1,0:T(8,128)(2,1)S(1)} %pad_maximum_fusion.2.refs_0_), channel_id=1, source_target_pairs={{0,2},{1,3},{2,0},{3,1},{4,6},{5,7},{6,4},{7,5},{8,10},{9,11},{10,... | collective-permute-start | bytes 393224 | tf_op jit(solution)/shard_map/ppermute | solution.py:105
  115.2 3.4 %collective-permute-start.5 = (bf16[512,128]{1,0:T(8,128)(2,1)S(1)}, bf16[512,128]{1,0:T(8,128)(2,1)S(1)}, u32[]{:S(2)}, u32[]{:S(2)}) collective-permute-start(bf16[512,128]{1,0:T(8,128)(2,1)S(1)} %pad_maximum_fusion.2.refs_0_), channel_id=1, source_target_pairs={{0,3},{1,2},{2,1},{3,0},{4,7},{5,6},{6,5},{7,4},{8,11},{9,10},{10,... | collective-permute-start | bytes 393224 | tf_op jit(solution)/shard_map/ppermute | solution.py:105
  118.6 0.0 collective-permute-done.3.refs_1_
  118.6 0.0 collective-permute-done.4.refs_2_
  118.6 3.5 %collective-permute-done.5.refs_3_ = bf16[512,128]{1,0:T(8,128)(2,1)S(1)} collective-permute-done((bf16[512,128]{1,0:T(8,128)(2,1)S(1)}, bf16[512,128]{1,0:T(8,128)(2,1)S(1)}, u32[]{:S(2)}, u32[]{:S(2)}) %collective-permute-start.5) | collective-permute-done | bytes 131104 | tf_op jit(solution)/shard_map/ppermute | solution.py:105
  122.1 0.7 shard_map.78
  122.8 6.3 %collective-permute-start.6 = (bf16[512,128]{1,0:T(8,128)(2,1)S(1)}, bf16[512,128]{1,0:T(8,128)(2,1)S(1)}, u32[]{:S(2)}, u32[]{:S(2)}) collective-permute-start(bf16[512,128]{1,0:T(8,128)(2,1)S(1)} %get-tuple-element.32), channel_id=1, source_target_pairs={{0,8},{1,9},{2,10},{3,11},{4,12},{5,13},{6,14},{7,15},{8,0},{9,1},... | collective-permute-start | bytes 393224 | tf_op jit(solution)/shard_map/ppermute | solution.py:171
  129.2 2.2 %collective-permute-start.7 = (bf16[512,128]{1,0:T(8,128)(2,1)S(1)}, bf16[512,128]{1,0:T(8,128)(2,1)S(1)}, u32[]{:S(2)}, u32[]{:S(2)}) collective-permute-start(bf16[512,128]{1,0:T(8,128)(2,1)S(1)} %get-tuple-element.33), channel_id=1, source_target_pairs={{0,4},{1,5},{2,6},{3,7},{4,8},{5,9},{6,10},{7,11},{8,12},{9,13},{1... | collective-permute-start | bytes 393224 | tf_op jit(solution)/shard_map/ppermute | solution.py:171
  131.4 5.2 %collective-permute-start.8 = (bf16[512,128]{1,0:T(8,128)(2,1)S(1)}, bf16[512,128]{1,0:T(8,128)(2,1)S(1)}, u32[]{:S(2)}, u32[]{:S(2)}) collective-permute-start(bf16[512,128]{1,0:T(8,128)(2,1)S(1)} %get-tuple-element.34), channel_id=1, source_target_pairs={{0,12},{1,13},{2,14},{3,15},{4,0},{5,1},{6,2},{7,3},{8,4},{9,5},{1... | collective-permute-start | bytes 393224 | tf_op jit(solution)/shard_map/ppermute | solution.py:171
  136.6 0.0 collective-permute-done.6
  136.6 2.6 %collective-permute-done.7 = bf16[512,128]{1,0:T(8,128)(2,1)S(1)} collective-permute-done((bf16[512,128]{1,0:T(8,128)(2,1)S(1)}, bf16[512,128]{1,0:T(8,128)(2,1)S(1)}, u32[]{:S(2)}, u32[]{:S(2)}) %collective-permute-start.7) | collective-permute-done | bytes 131104 | tf_op jit(solution)/shard_map/ppermute | solution.py:171
  139.2 1.1 collective-permute-done.8
  140.3 0.7 add_convert_fusion
  141.0 3.7 %all-to-all-done.3 = bf16[64,32,128]{2,1,0:T(8,128)(2,1)S(1)} async-done(((bf16[64,32,128]{2,1,0:T(8,128)(2,1)}), bf16[64,32,128]{2,1,0:T(8,128)(2,1)S(1)}, u32[]{:S(2)}, u32[]{:S(2)}) %all-to-all-start.3) | async-done | bytes 524320 | tf_op jit(solution)/shard_map/all_to_all | solution.py:165
  144.8 0.1 convert_reduce_fusion
  144.9 0.0 copy-start.5
  144.9 0.7 fusion.12
  145.5 0.0 copy-done.5
  (11 shorter events, 0.3 us)
Async XLA Ops:
  0.6 24.9 %copy-start = (bf16[512,2048]{1,0:T(8,128)(2,1)S(1)}, bf16[512,2048]{1,0:T(8,128)(2,1)}, u32[]{:S(2)}) copy-start(bf16[512,2048]{1,0:T(8,128)(2,1)} %param.5) | copy-start | bytes 6291460
  2.3 47.1 %all-to-all-start = ((bf16[64,16,128]{2,1,0:T(8,128)(2,1)}), bf16[64,16,128]{2,1,0:T(8,128)(2,1)S(1)}, u32[]{:S(2)}, u32[]{:S(2)}) async-start(bf16[64,16,128]{2,1,0:T(8,128)(2,1)} %shard_map.76), calls=%async_computation | async-start | bytes 524288 | tf_op jit(solution)/shard_map/all_to_all | solution.py:111
  49.5 1.6 %copy-start.2 = (bf16[512,2048]{1,0:T(8,128)(2,1)S(1)}, bf16[512,2048]{1,0:T(8,128)(2,1)}, u32[]{:S(2)}) copy-start(bf16[512,2048]{1,0:T(8,128)(2,1)} %param.9) | copy-start | bytes 6291460
  49.5 1.6 %copy-start.4 = (bf16[64,2048]{1,0:T(8,128)(2,1)S(1)}, bf16[64,2048]{1,0:T(8,128)(2,1)}, u32[]{:S(2)}) copy-start(bf16[64,2048]{1,0:T(8,128)(2,1)} %param.7) | copy-start | bytes 786436
  50.5 9.8 %copy-start.1 = (bf16[64,2048]{1,0:T(8,128)(2,1)S(1)}, bf16[64,2048]{1,0:T(8,128)(2,1)}, u32[]{:S(2)}) copy-start(bf16[64,2048]{1,0:T(8,128)(2,1)} %sig_ref.1) | copy-start | bytes 786436
  53.3 21.8 %all-to-all-start.1 = ((f32[16,3,512]{2,1,0:T(4,128)}), f32[16,3,512]{2,1,0:T(4,128)S(1)}, u32[]{:S(2)}, u32[]{:S(2)}) async-start(f32[16,3,512]{2,1,0:T(4,128)} %broadcast_in_dim.5), calls=%async_computation.1 | async-start | bytes 262144 | tf_op jit(solution)/shard_map/all_to_all | solution.py:15
  61.5 8.4 %collective-permute-start = (bf16[128,512]{1,0:T(8,128)(2,1)S(1)}, bf16[128,512]{1,0:T(8,128)(2,1)S(1)}, u32[]{:S(2)}, u32[]{:S(2)}) collective-permute-start(bf16[128,512]{1,0:T(8,128)(2,1)S(1)} %get-tuple-element.21), channel_id=1, source_target_pairs={{0,1},{1,0},{2,3},{3,2},{4,5},{5,4},{6,7},{7,6},{8,9},{9,8},{10,11... | collective-permute-start | bytes 393224 | tf_op jit(solution)/shard_map/ppermute | solution.py:105
  64.8 6.6 %collective-permute-start.1 = (bf16[128,512]{1,0:T(8,128)(2,1)S(1)}, bf16[128,512]{1,0:T(8,128)(2,1)S(1)}, u32[]{:S(2)}, u32[]{:S(2)}) collective-permute-start(bf16[128,512]{1,0:T(8,128)(2,1)S(1)} %get-tuple-element.22), channel_id=1, source_target_pairs={{0,2},{1,3},{2,0},{3,1},{4,6},{5,7},{6,4},{7,5},{8,10},{9,11},{10,... | collective-permute-start | bytes 393224 | tf_op jit(solution)/shard_map/ppermute | solution.py:105
  67.9 7.2 %collective-permute-start.2 = (bf16[128,512]{1,0:T(8,128)(2,1)S(1)}, bf16[128,512]{1,0:T(8,128)(2,1)S(1)}, u32[]{:S(2)}, u32[]{:S(2)}) collective-permute-start(bf16[128,512]{1,0:T(8,128)(2,1)S(1)} %get-tuple-element.23), channel_id=1, source_target_pairs={{0,3},{1,2},{2,1},{3,0},{4,7},{5,6},{6,5},{7,4},{8,11},{9,10},{10,... | collective-permute-start | bytes 393224 | tf_op jit(solution)/shard_map/ppermute | solution.py:105
  75.8 24.9 %all-to-all-start.2 = ((f32[64,3,128]{2,1,0:T(4,128)}), f32[64,3,128]{2,1,0:T(4,128)}, u32[]{:S(2)}, u32[]{:S(2)}) async-start(f32[64,3,128]{2,1,0:T(4,128)} %broadcast_in_dim.4), calls=%async_computation.2 | async-start | bytes 262144 | tf_op jit(solution)/shard_map/all_to_all | solution.py:143
  101.9 2.2 %copy-start.3 = (bf16[512,2048]{1,0:T(8,128)(2,1)S(1)}, bf16[512,2048]{1,0:T(8,128)(2,1)}, u32[]{:S(2)}) copy-start(bf16[512,2048]{1,0:T(8,128)(2,1)} %param.9) | copy-start | bytes 6291460
  105.7 39.1 %all-to-all-start.3 = ((bf16[64,32,128]{2,1,0:T(8,128)(2,1)}), bf16[64,32,128]{2,1,0:T(8,128)(2,1)S(1)}, u32[]{:S(2)}, u32[]{:S(2)}) async-start(bf16[64,32,128]{2,1,0:T(8,128)(2,1)} %bitcast.74), calls=%async_computation.3 | async-start | bytes 1048576 | tf_op jit(solution)/shard_map/all_to_all | solution.py:165
  110.2 8.4 %collective-permute-start.3 = (bf16[512,128]{1,0:T(8,128)(2,1)S(1)}, bf16[512,128]{1,0:T(8,128)(2,1)S(1)}, u32[]{:S(2)}, u32[]{:S(2)}) collective-permute-start(bf16[512,128]{1,0:T(8,128)(2,1)S(1)} %pad_maximum_fusion.2.refs_0_), channel_id=1, source_target_pairs={{0,1},{1,0},{2,3},{3,2},{4,5},{5,4},{6,7},{7,6},{8,9},{9,8},{10,11... | collective-permute-start | bytes 393224 | tf_op jit(solution)/shard_map/ppermute | solution.py:105
  112.4 6.2 %collective-permute-start.4 = (bf16[512,128]{1,0:T(8,128)(2,1)S(1)}, bf16[512,128]{1,0:T(8,128)(2,1)S(1)}, u32[]{:S(2)}, u32[]{:S(2)}) collective-permute-start(bf16[512,128]{1,0:T(8,128)(2,1)S(1)} %pad_maximum_fusion.2.refs_0_), channel_id=1, source_target_pairs={{0,2},{1,3},{2,0},{3,1},{4,6},{5,7},{6,4},{7,5},{8,10},{9,11},{10,... | collective-permute-start | bytes 393224 | tf_op jit(solution)/shard_map/ppermute | solution.py:105
  115.2 7.0 %collective-permute-start.5 = (bf16[512,128]{1,0:T(8,128)(2,1)S(1)}, bf16[512,128]{1,0:T(8,128)(2,1)S(1)}, u32[]{:S(2)}, u32[]{:S(2)}) collective-permute-start(bf16[512,128]{1,0:T(8,128)(2,1)S(1)} %pad_maximum_fusion.2.refs_0_), channel_id=1, source_target_pairs={{0,3},{1,2},{2,1},{3,0},{4,7},{5,6},{6,5},{7,4},{8,11},{9,10},{10,... | collective-permute-start | bytes 393224 | tf_op jit(solution)/shard_map/ppermute | solution.py:105
  122.8 13.8 %collective-permute-start.6 = (bf16[512,128]{1,0:T(8,128)(2,1)S(1)}, bf16[512,128]{1,0:T(8,128)(2,1)S(1)}, u32[]{:S(2)}, u32[]{:S(2)}) collective-permute-start(bf16[512,128]{1,0:T(8,128)(2,1)S(1)} %get-tuple-element.32), channel_id=1, source_target_pairs={{0,8},{1,9},{2,10},{3,11},{4,12},{5,13},{6,14},{7,15},{8,0},{9,1},... | collective-permute-start | bytes 393224 | tf_op jit(solution)/shard_map/ppermute | solution.py:171
  129.2 10.1 %collective-permute-start.7 = (bf16[512,128]{1,0:T(8,128)(2,1)S(1)}, bf16[512,128]{1,0:T(8,128)(2,1)S(1)}, u32[]{:S(2)}, u32[]{:S(2)}) collective-permute-start(bf16[512,128]{1,0:T(8,128)(2,1)S(1)} %get-tuple-element.33), channel_id=1, source_target_pairs={{0,4},{1,5},{2,6},{3,7},{4,8},{5,9},{6,10},{7,11},{8,12},{9,13},{1... | collective-permute-start | bytes 393224 | tf_op jit(solution)/shard_map/ppermute | solution.py:171
  131.4 8.9 %collective-permute-start.8 = (bf16[512,128]{1,0:T(8,128)(2,1)S(1)}, bf16[512,128]{1,0:T(8,128)(2,1)S(1)}, u32[]{:S(2)}, u32[]{:S(2)}) collective-permute-start(bf16[512,128]{1,0:T(8,128)(2,1)S(1)} %get-tuple-element.34), channel_id=1, source_target_pairs={{0,12},{1,13},{2,14},{3,15},{4,0},{5,1},{6,2},{7,3},{8,4},{9,5},{1... | collective-permute-start | bytes 393224 | tf_op jit(solution)/shard_map/ppermute | solution.py:171
  144.9 0.7 copy-start.5

commit v8 on v7

--- a/solution.py
+++ b/solution.py
@@ -123,7 +123,9 @@
         rank = lax.axis_index("exp")
         place = jnp.stack([lax.rem(rank, GROUP), lax.div(rank, GROUP)]).astype(jnp.int32)
         weights = split_weights(place, slot_in_grad, phi_full, groups, wide)
-        weights = [weights[0]] + [swap(weights[k], k) for k in range(1, GROUP)]
+        weights = list(weights)
+        lent = weights[1:]
+        weights[1] = swap(lent[0], 1)
 
         row_top = jnp.max(logits, axis=1)
         row_exp = jnp.exp(logits - row_top[:, None])
@@ -139,8 +141,13 @@
         row_got = gather_blocks(row_stats, "exp", n_exp)
         col_stats = jnp.pad(col_stats, ((0, 0), (0, -slots % 128)))
         spread = jnp.broadcast_to(col_stats[None], (n_seq,) + col_stats.shape)
-        spread, row_got, weights = lax.optimization_barrier((spread, row_got, weights))
+        spread, row_got, lent, weights[1] = lax.optimization_barrier(
+            (spread, row_got, lent, weights[1])
+        )
         col_got = lax.all_to_all(spread, "seq", 0, 0, tiled=True)
+        for k in range(2, GROUP):
+            weights[k] = swap(lent[k - 1], k)
+        col_got, weights = lax.optimization_barrier((col_got, weights))
         row_peak, row_total, row_dot = merge_stats(row_got)
         col_peak, col_total, col_dot = merge_stats(col_got[:, :, :slots])
 

time: 146 us -> 148 us (1.014)
  waiting for transfers between devices: 54.6 us -> 45.4 us
  starting transfers between devices: 71.6 us -> 78.7 us
  local copies, waits for them, and re-layouts: 6.77 us -> 10.2 us
    all_to_all x1, waiting for transfers between devices: 16.4 us -> 5.56 us  [per_device(): col_got = lax.all_to_all(spread, 'seq', 0, 0, tiled=True)]
    all_to_all x1, starting transfers between devices: 4.46 us -> 11.3 us  [per_device(): lax.all_to_all(both.reshape(n_seq, -1, 2 * slots), 'seq', 0, 0, tiled=True)]
    ppermute x6, waiting for transfers between devices: 8.69 us -> 11 us  [swap(): return lax.ppermute(x, 'exp', [(j, j ^ k) for j in range(n_exp)])]
    optimization_barrier x1 -> x2, local copies, waits for them, and re-layouts: 0.03 us -> 1.85 us  [the longest x1 0.94 us: per_device(): lax.optimization_barrier((spread, row_got, lent, weights[1]))]
  transfers between devices with their start and end apart: 13 -> 13, of which waited for: 8 -> 11; matrix products, arithmetic and copies ran while one was open for 3% -> 5% of each run, Pallas kernels for 1% -> 1%
where the time goes in v8:
time: 148 us; the launch traced here: 147 us
  starting transfers between devices  78.7 us (53%)
  waiting for transfers between devices  45.4 us (31%)
  local copies, waits for them, and re-layouts  10.2 us (7%)
  matrix products  5.1 us (3%)
  Pallas kernels  3.47 us (2%)
  other arithmetic  3.06 us (2%)
    all_to_all x1, starting transfers between devices, per_device(): got_phi = lax.all_to_all(packed_copies(phi, n_seq), 'seq', 0, 0, tiled=True)  23.3 us
    all_to_all x1, waiting for transfers between devices, per_device(): got_phi = lax.all_to_all(packed_copies(phi, n_seq), 'seq', 0, 0, tiled=True)  22.1 us
    ppermute x6, starting transfers between devices, swap(): return lax.ppermute(x, 'exp', [(j, j ^ k) for j in range(n_exp)])  16.9 us
    ppermute x3, starting transfers between devices, per_device(): token_sum = token_sum + lax.ppermute(blocks[i], 'exp', turn).astype(F32)  14 us
    all_to_all x1, starting transfers between devices, per_device(): lax.all_to_all(both.reshape(n_seq, -1, 2 * slots), 'seq', 0, 0, tiled=True)  11.3 us
    ppermute x6, waiting for transfers between devices, swap(): return lax.ppermute(x, 'exp', [(j, j ^ k) for j in range(n_exp)])  11 us
    all_to_all x1, starting transfers between devices, gather_blocks(): return lax.all_to_all(spread, axis, 0, 0, tiled=True)  7 us
    all_to_all x1, starting transfers between devices, per_device(): col_got = lax.all_to_all(spread, 'seq', 0, 0, tiled=True)  6.15 us
  transfers between devices with their start and end apart: 13, of which 11 were waited for; matrix products, arithmetic and copies ran while one was open for 5% of the time, Pallas kernels for 1%

profile of v8, /device:TPU:1, one launch (start us, length us, event | category | flops | bytes accessed | tf_op | source)
XLA Modules:
  0.0 146.9 jit_solution(10693958250811494103)
XLA Ops:
  0.6 0.0 copy-start
  0.6 1.6 %shard_map.76 = bf16[64,16,128]{2,1,0:T(8,128)(2,1)} custom-call(bf16[32,64]{1,0:T(8,128)(2,1)} %block_ref.1), custom_call_target="tpu_custom_call" | custom-call | bytes 266240 | tf_op jit(solution)/shard_map/pallas_call | solution.py:35
  2.3 23.3 %all-to-all-start = ((bf16[64,16,128]{2,1,0:T(8,128)(2,1)}), bf16[64,16,128]{2,1,0:T(8,128)(2,1)S(1)}, u32[]{:S(2)}, u32[]{:S(2)}) async-start(bf16[64,16,128]{2,1,0:T(8,128)(2,1)} %shard_map.76), calls=%async_computation | async-start | bytes 524288 | tf_op jit(solution)/shard_map/all_to_all | solution.py:111
  25.6 0.0 copy-done
  25.6 1.7 %fusion.18 = f32[512,64]{0,1:T(8,128)S(1)} fusion(bf16[512,2048]{1,0:T(8,128)(2,1)S(1)} %copy-done, bf16[64,2048]{1,0:T(8,128)(2,1)} %sig_ref.1), kind=kOutput, calls=%fused_computation.49 | convolution fusion | flops 134217728 | bytes 2490368 | tf_op jit(solution)/shard_map/dot_general | solution.py:116
  27.3 22.1 %all-to-all-done = bf16[64,16,128]{2,1,0:T(8,128)(2,1)S(1)} async-done(((bf16[64,16,128]{2,1,0:T(8,128)(2,1)}), bf16[64,16,128]{2,1,0:T(8,128)(2,1)S(1)}, u32[]{:S(2)}, u32[]{:S(2)}) %all-to-all-start) | async-done | bytes 262176 | tf_op jit(solution)/shard_map/all_to_all | solution.py:111
  49.4 0.1 fusion.17
  49.5 0.0 copy-start.2
  49.5 0.0 copy-start.5
  49.5 0.1 pad_maximum_fusion
  49.7 0.9 fusion.16
  50.5 0.0 copy-start.1
  50.5 0.2 fusion.7
  50.7 0.4 copy-done.2
  51.1 0.0 copy-done.5
  51.1 1.5 %fusion.4 = (f32[512]{0:T(512)S(1)}, f32[64]{0:T(128)S(1)}, f32[512,64]{0,1:T(8,128)}) fusion(f32[64,512]{1,0:T(8,128)S(1)} %get-tuple-element.59, f32[512]{0:T(512)S(1)} %get-tuple-element.49, f32[512,64]{0,1:T(8,128)S(1)} %fusion.18, f32[64]{0:T(128)S(1)} %get-tuple-element.50, bf16[512,2048]{1,0:T(8,128)(2,1)S(1)} %copy-done.2, ...), kind=kOutput, calls=%fused_computation.18 | convolution fusion | flops 134413760 | bytes 2757120 | tf_op jit(solution)/shard_map/dot_general | solution.py:119
  52.7 0.7 broadcast_in_dim.5
  53.3 7.0 %all-to-all-start.1 = ((f32[16,3,512]{2,1,0:T(4,128)}), f32[16,3,512]{2,1,0:T(4,128)}, u32[]{:S(2)}, u32[]{:S(2)}) async-start(f32[16,3,512]{2,1,0:T(4,128)} %broadcast_in_dim.5), calls=%async_computation.1 | async-start | bytes 262144 | tf_op jit(solution)/shard_map/all_to_all | solution.py:15
  60.3 0.0 copy-done.4
  60.3 0.1 pad_add_fusion.place_ref
  60.4 0.0 copy-done.1
  60.4 1.1 shard_map.77
  61.6 3.2 %collective-permute-start = (bf16[128,512]{1,0:T(8,128)(2,1)S(1)}, bf16[128,512]{1,0:T(8,128)(2,1)S(1)}, u32[]{:S(2)}, u32[]{:S(2)}) collective-permute-start(bf16[128,512]{1,0:T(8,128)(2,1)S(1)} %get-tuple-element.24), channel_id=1, source_target_pairs={{0,1},{1,0},{2,3},{3,2},{4,5},{5,4},{6,7},{7,6},{8,9},{9,8},{10,11... | collective-permute-start | bytes 393224 | tf_op jit(solution)/shard_map/ppermute | solution.py:105
  64.8 4.6 %collective-permute-done.refs_5_ = bf16[128,512]{1,0:T(8,128)(2,1)S(1)} collective-permute-done((bf16[128,512]{1,0:T(8,128)(2,1)S(1)}, bf16[128,512]{1,0:T(8,128)(2,1)S(1)}, u32[]{:S(2)}, u32[]{:S(2)}) %collective-permute-start) | collective-permute-done | bytes 131104 | tf_op jit(solution)/shard_map/ppermute | solution.py:105
  69.4 0.2 all-to-all-done.1
  69.6 0.7 broadcast_in_dim.4
  70.3 6.2 %all-to-all-start.2 = ((f32[64,3,128]{2,1,0:T(4,128)}), f32[64,3,128]{2,1,0:T(4,128)}, u32[]{:S(2)}, u32[]{:S(2)}) async-start(f32[64,3,128]{2,1,0:T(4,128)} %broadcast_in_dim.4), calls=%async_computation.2 | async-start | bytes 262144 | tf_op jit(solution)/shard_map/all_to_all | solution.py:147
  76.4 1.0 copy.48
  77.5 0.1 copy.40
  77.6 1.7 %copy.47 = f32[512,64]{1,0:T(8,128)} copy(f32[512,64]{0,1:T(8,128)} %get-tuple-element.60) | data formatting | bytes 262144 | tf_op jit(solution)/shard_map/dot_general | solution.py:119
  79.3 0.9 copy.43
  80.3 2.2 %collective-permute-start.1 = (bf16[128,512]{1,0:T(8,128)(2,1)S(1)}, bf16[128,512]{1,0:T(8,128)(2,1)S(1)}, u32[]{:S(2)}, u32[]{:S(2)}) collective-permute-start(bf16[128,512]{1,0:T(8,128)(2,1)S(1)} %get-tuple-element.30), channel_id=1, source_target_pairs={{0,2},{1,3},{2,0},{3,1},{4,6},{5,7},{6,4},{7,5},{8,10},{9,11},{10,... | collective-permute-start | bytes 393224 | tf_op jit(solution)/shard_map/ppermute | solution.py:105
  82.4 3.2 %collective-permute-start.2 = (bf16[128,512]{1,0:T(8,128)(2,1)S(1)}, bf16[128,512]{1,0:T(8,128)(2,1)S(1)}, u32[]{:S(2)}, u32[]{:S(2)}) collective-permute-start(bf16[128,512]{1,0:T(8,128)(2,1)S(1)} %get-tuple-element.31), channel_id=1, source_target_pairs={{0,3},{1,2},{2,1},{3,0},{4,7},{5,6},{6,5},{7,4},{8,11},{9,10},{10,... | collective-permute-start | bytes 393224 | tf_op jit(solution)/shard_map/ppermute | solution.py:105
  85.6 0.9 slice.41
  86.6 0.1 collective-permute-done.1.refs_6_
  86.7 2.8 %collective-permute-done.2.refs_7_ = bf16[128,512]{1,0:T(8,128)(2,1)S(1)} collective-permute-done((bf16[128,512]{1,0:T(8,128)(2,1)S(1)}, bf16[128,512]{1,0:T(8,128)(2,1)S(1)}, u32[]{:S(2)}, u32[]{:S(2)}) %collective-permute-start.2) | collective-permute-done | bytes 131104 | tf_op jit(solution)/shard_map/ppermute | solution.py:105
  89.5 5.6 %all-to-all-done.2 = f32[64,3,128]{2,1,0:T(4,128)} async-done(((f32[64,3,128]{2,1,0:T(4,128)}), f32[64,3,128]{2,1,0:T(4,128)}, u32[]{:S(2)}, u32[]{:S(2)}) %all-to-all-start.2) | async-done | bytes 98336 | tf_op jit(solution)/shard_map/all_to_all | solution.py:147
  95.0 0.9 copy.39
  96.0 0.9 slice.42
  97.0 0.2 bitcast_convert_fusion
  97.2 1.3 fusion.3
  98.5 0.1 pad_maximum_fusion.2.refs_0_
  98.7 0.5 fusion
  99.2 0.0 copy-done.3
  99.2 0.5 fusion.1
  99.7 1.0 copy.49
  100.7 11.3 %all-to-all-start.3 = ((bf16[64,32,128]{2,1,0:T(8,128)(2,1)}), bf16[64,32,128]{2,1,0:T(8,128)(2,1)S(1)}, u32[]{:S(2)}, u32[]{:S(2)}) async-start(bf16[64,32,128]{2,1,0:T(8,128)(2,1)} %bitcast.82), calls=%async_computation.3 | async-start | bytes 1048576 | tf_op jit(solution)/shard_map/all_to_all | solution.py:172
  112.1 2.6 %collective-permute-start.3 = (bf16[512,128]{1,0:T(8,128)(2,1)S(1)}, bf16[512,128]{1,0:T(8,128)(2,1)S(1)}, u32[]{:S(2)}, u32[]{:S(2)}) collective-permute-start(bf16[512,128]{1,0:T(8,128)(2,1)S(1)} %pad_maximum_fusion.2.refs_0_), channel_id=1, source_target_pairs={{0,1},{1,0},{2,3},{3,2},{4,5},{5,4},{6,7},{7,6},{8,9},{9,8},{10,11... | collective-permute-start | bytes 393224 | tf_op jit(solution)/shard_map/ppermute | solution.py:105
  114.7 2.3 %collective-permute-start.4 = (bf16[512,128]{1,0:T(8,128)(2,1)S(1)}, bf16[512,128]{1,0:T(8,128)(2,1)S(1)}, u32[]{:S(2)}, u32[]{:S(2)}) collective-permute-start(bf16[512,128]{1,0:T(8,128)(2,1)S(1)} %pad_maximum_fusion.2.refs_0_), channel_id=1, source_target_pairs={{0,2},{1,3},{2,0},{3,1},{4,6},{5,7},{6,4},{7,5},{8,10},{9,11},{10,... | collective-permute-start | bytes 393224 | tf_op jit(solution)/shard_map/ppermute | solution.py:105
  117.1 3.4 %collective-permute-start.5 = (bf16[512,128]{1,0:T(8,128)(2,1)S(1)}, bf16[512,128]{1,0:T(8,128)(2,1)S(1)}, u32[]{:S(2)}, u32[]{:S(2)}) collective-permute-start(bf16[512,128]{1,0:T(8,128)(2,1)S(1)} %pad_maximum_fusion.2.refs_0_), channel_id=1, source_target_pairs={{0,3},{1,2},{2,1},{3,0},{4,7},{5,6},{6,5},{7,4},{8,11},{9,10},{10,... | collective-permute-start | bytes 393224 | tf_op jit(solution)/shard_map/ppermute | solution.py:105
  120.5 0.0 collective-permute-done.3.refs_1_
  120.5 0.4 collective-permute-done.4.refs_2_
  120.9 3.1 %collective-permute-done.5.refs_3_ = bf16[512,128]{1,0:T(8,128)(2,1)S(1)} collective-permute-done((bf16[512,128]{1,0:T(8,128)(2,1)S(1)}, bf16[512,128]{1,0:T(8,128)(2,1)S(1)}, u32[]{:S(2)}, u32[]{:S(2)}) %collective-permute-start.5) | collective-permute-done | bytes 131104 | tf_op jit(solution)/shard_map/ppermute | solution.py:105
  124.0 0.7 shard_map.78
  124.7 6.6 %collective-permute-start.6 = (bf16[512,128]{1,0:T(8,128)(2,1)S(1)}, bf16[512,128]{1,0:T(8,128)(2,1)S(1)}, u32[]{:S(2)}, u32[]{:S(2)}) collective-permute-start(bf16[512,128]{1,0:T(8,128)(2,1)S(1)} %get-tuple-element.40), channel_id=1, source_target_pairs={{0,8},{1,9},{2,10},{3,11},{4,12},{5,13},{6,14},{7,15},{8,0},{9,1},... | collective-permute-start | bytes 393224 | tf_op jit(solution)/shard_map/ppermute | solution.py:178
  131.3 2.5 %collective-permute-start.7 = (bf16[512,128]{1,0:T(8,128)(2,1)S(1)}, bf16[512,128]{1,0:T(8,128)(2,1)S(1)}, u32[]{:S(2)}, u32[]{:S(2)}) collective-permute-start(bf16[512,128]{1,0:T(8,128)(2,1)S(1)} %get-tuple-element.41), channel_id=1, source_target_pairs={{0,4},{1,5},{2,6},{3,7},{4,8},{5,9},{6,10},{7,11},{8,12},{9,13},{1... | collective-permute-start | bytes 393224 | tf_op jit(solution)/shard_map/ppermute | solution.py:178
  133.8 4.9 %collective-permute-start.8 = (bf16[512,128]{1,0:T(8,128)(2,1)S(1)}, bf16[512,128]{1,0:T(8,128)(2,1)S(1)}, u32[]{:S(2)}, u32[]{:S(2)}) collective-permute-start(bf16[512,128]{1,0:T(8,128)(2,1)S(1)} %get-tuple-element.42), channel_id=1, source_target_pairs={{0,12},{1,13},{2,14},{3,15},{4,0},{5,1},{6,2},{7,3},{8,4},{9,5},{1... | collective-permute-start | bytes 393224 | tf_op jit(solution)/shard_map/ppermute | solution.py:178
  138.7 0.0 collective-permute-done.6
  138.8 1.8 %collective-permute-done.7 = bf16[512,128]{1,0:T(8,128)(2,1)S(1)} collective-permute-done((bf16[512,128]{1,0:T(8,128)(2,1)S(1)}, bf16[512,128]{1,0:T(8,128)(2,1)S(1)}, u32[]{:S(2)}, u32[]{:S(2)}) %collective-permute-start.7) | collective-permute-done | bytes 131104 | tf_op jit(solution)/shard_map/ppermute | solution.py:178
  140.5 1.4 collective-permute-done.8
  142.0 0.7 add_convert_fusion
  142.7 3.4 %all-to-all-done.3 = bf16[64,32,128]{2,1,0:T(8,128)(2,1)S(1)} async-done(((bf16[64,32,128]{2,1,0:T(8,128)(2,1)}), bf16[64,32,128]{2,1,0:T(8,128)(2,1)S(1)}, u32[]{:S(2)}, u32[]{:S(2)}) %all-to-all-start.3) | async-done | bytes 524320 | tf_op jit(solution)/shard_map/all_to_all | solution.py:172
  146.1 0.1 convert_reduce_fusion
  146.2 0.7 fusion.15
  (13 shorter events, 0.2 us)
Async XLA Ops:
  0.6 24.9 %copy-start = (bf16[512,2048]{1,0:T(8,128)(2,1)S(1)}, bf16[512,2048]{1,0:T(8,128)(2,1)}, u32[]{:S(2)}) copy-start(bf16[512,2048]{1,0:T(8,128)(2,1)} %param.5) | copy-start | bytes 6291460
  2.3 47.1 %all-to-all-start = ((bf16[64,16,128]{2,1,0:T(8,128)(2,1)}), bf16[64,16,128]{2,1,0:T(8,128)(2,1)S(1)}, u32[]{:S(2)}, u32[]{:S(2)}) async-start(bf16[64,16,128]{2,1,0:T(8,128)(2,1)} %shard_map.76), calls=%async_computation | async-start | bytes 524288 | tf_op jit(solution)/shard_map/all_to_all | solution.py:111
  27.3 33.0 %copy-start.4 = (f32[512,64]{0,1:T(8,128)}, f32[512,64]{0,1:T(8,128)S(1)}, u32[]{:S(2)}) copy-start(f32[512,64]{0,1:T(8,128)S(1)} %fusion.18) | copy-start | bytes 393220
  49.5 1.6 %copy-start.2 = (bf16[512,2048]{1,0:T(8,128)(2,1)S(1)}, bf16[512,2048]{1,0:T(8,128)(2,1)}, u32[]{:S(2)}) copy-start(bf16[512,2048]{1,0:T(8,128)(2,1)} %param.9) | copy-start | bytes 6291460
  49.5 1.6 %copy-start.5 = (bf16[64,2048]{1,0:T(8,128)(2,1)S(1)}, bf16[64,2048]{1,0:T(8,128)(2,1)}, u32[]{:S(2)}) copy-start(bf16[64,2048]{1,0:T(8,128)(2,1)} %param.7) | copy-start | bytes 786436
  50.5 9.9 %copy-start.1 = (bf16[64,2048]{1,0:T(8,128)(2,1)S(1)}, bf16[64,2048]{1,0:T(8,128)(2,1)}, u32[]{:S(2)}) copy-start(bf16[64,2048]{1,0:T(8,128)(2,1)} %sig_ref.1) | copy-start | bytes 786436
  53.3 16.3 %all-to-all-start.1 = ((f32[16,3,512]{2,1,0:T(4,128)}), f32[16,3,512]{2,1,0:T(4,128)}, u32[]{:S(2)}, u32[]{:S(2)}) async-start(f32[16,3,512]{2,1,0:T(4,128)} %broadcast_in_dim.5), calls=%async_computation.1 | async-start | bytes 262144 | tf_op jit(solution)/shard_map/all_to_all | solution.py:15
  61.6 7.9 %collective-permute-start = (bf16[128,512]{1,0:T(8,128)(2,1)S(1)}, bf16[128,512]{1,0:T(8,128)(2,1)S(1)}, u32[]{:S(2)}, u32[]{:S(2)}) collective-permute-start(bf16[128,512]{1,0:T(8,128)(2,1)S(1)} %get-tuple-element.24), channel_id=1, source_target_pairs={{0,1},{1,0},{2,3},{3,2},{4,5},{5,4},{6,7},{7,6},{8,9},{9,8},{10,11... | collective-permute-start | bytes 393224 | tf_op jit(solution)/shard_map/ppermute | solution.py:105
  70.3 24.8 %all-to-all-start.2 = ((f32[64,3,128]{2,1,0:T(4,128)}), f32[64,3,128]{2,1,0:T(4,128)}, u32[]{:S(2)}, u32[]{:S(2)}) async-start(f32[64,3,128]{2,1,0:T(4,128)} %broadcast_in_dim.4), calls=%async_computation.2 | async-start | bytes 262144 | tf_op jit(solution)/shard_map/all_to_all | solution.py:147
  80.3 6.4 %collective-permute-start.1 = (bf16[128,512]{1,0:T(8,128)(2,1)S(1)}, bf16[128,512]{1,0:T(8,128)(2,1)S(1)}, u32[]{:S(2)}, u32[]{:S(2)}) collective-permute-start(bf16[128,512]{1,0:T(8,128)(2,1)S(1)} %get-tuple-element.30), channel_id=1, source_target_pairs={{0,2},{1,3},{2,0},{3,1},{4,6},{5,7},{6,4},{7,5},{8,10},{9,11},{10,... | collective-permute-start | bytes 393224 | tf_op jit(solution)/shard_map/ppermute | solution.py:105
  82.4 7.0 %collective-permute-start.2 = (bf16[128,512]{1,0:T(8,128)(2,1)S(1)}, bf16[128,512]{1,0:T(8,128)(2,1)S(1)}, u32[]{:S(2)}, u32[]{:S(2)}) collective-permute-start(bf16[128,512]{1,0:T(8,128)(2,1)S(1)} %get-tuple-element.31), channel_id=1, source_target_pairs={{0,3},{1,2},{2,1},{3,0},{4,7},{5,6},{6,5},{7,4},{8,11},{9,10},{10,... | collective-permute-start | bytes 393224 | tf_op jit(solution)/shard_map/ppermute | solution.py:105
  97.0 2.2 %copy-start.3 = (bf16[512,2048]{1,0:T(8,128)(2,1)S(1)}, bf16[512,2048]{1,0:T(8,128)(2,1)}, u32[]{:S(2)}) copy-start(bf16[512,2048]{1,0:T(8,128)(2,1)} %param.9) | copy-start | bytes 6291460
  100.7 45.3 %all-to-all-start.3 = ((bf16[64,32,128]{2,1,0:T(8,128)(2,1)}), bf16[64,32,128]{2,1,0:T(8,128)(2,1)S(1)}, u32[]{:S(2)}, u32[]{:S(2)}) async-start(bf16[64,32,128]{2,1,0:T(8,128)(2,1)} %bitcast.82), calls=%async_computation.3 | async-start | bytes 1048576 | tf_op jit(solution)/shard_map/all_to_all | solution.py:172
  112.1 8.4 %collective-permute-start.3 = (bf16[512,128]{1,0:T(8,128)(2,1)S(1)}, bf16[512,128]{1,0:T(8,128)(2,1)S(1)}, u32[]{:S(2)}, u32[]{:S(2)}) collective-permute-start(bf16[512,128]{1,0:T(8,128)(2,1)S(1)} %pad_maximum_fusion.2.refs_0_), channel_id=1, source_target_pairs={{0,1},{1,0},{2,3},{3,2},{4,5},{5,4},{6,7},{7,6},{8,9},{9,8},{10,11... | collective-permute-start | bytes 393224 | tf_op jit(solution)/shard_map/ppermute | solution.py:105
  114.7 6.2 %collective-permute-start.4 = (bf16[512,128]{1,0:T(8,128)(2,1)S(1)}, bf16[512,128]{1,0:T(8,128)(2,1)S(1)}, u32[]{:S(2)}, u32[]{:S(2)}) collective-permute-start(bf16[512,128]{1,0:T(8,128)(2,1)S(1)} %pad_maximum_fusion.2.refs_0_), channel_id=1, source_target_pairs={{0,2},{1,3},{2,0},{3,1},{4,6},{5,7},{6,4},{7,5},{8,10},{9,11},{10,... | collective-permute-start | bytes 393224 | tf_op jit(solution)/shard_map/ppermute | solution.py:105
  117.1 6.9 %collective-permute-start.5 = (bf16[512,128]{1,0:T(8,128)(2,1)S(1)}, bf16[512,128]{1,0:T(8,128)(2,1)S(1)}, u32[]{:S(2)}, u32[]{:S(2)}) collective-permute-start(bf16[512,128]{1,0:T(8,128)(2,1)S(1)} %pad_maximum_fusion.2.refs_0_), channel_id=1, source_target_pairs={{0,3},{1,2},{2,1},{3,0},{4,7},{5,6},{6,5},{7,4},{8,11},{9,10},{10,... | collective-permute-start | bytes 393224 | tf_op jit(solution)/shard_map/ppermute | solution.py:105
  124.7 14.1 %collective-permute-start.6 = (bf16[512,128]{1,0:T(8,128)(2,1)S(1)}, bf16[512,128]{1,0:T(8,128)(2,1)S(1)}, u32[]{:S(2)}, u32[]{:S(2)}) collective-permute-start(bf16[512,128]{1,0:T(8,128)(2,1)S(1)} %get-tuple-element.40), channel_id=1, source_target_pairs={{0,8},{1,9},{2,10},{3,11},{4,12},{5,13},{6,14},{7,15},{8,0},{9,1},... | collective-permute-start | bytes 393224 | tf_op jit(solution)/shard_map/ppermute | solution.py:178
  131.3 9.2 %collective-permute-start.7 = (bf16[512,128]{1,0:T(8,128)(2,1)S(1)}, bf16[512,128]{1,0:T(8,128)(2,1)S(1)}, u32[]{:S(2)}, u32[]{:S(2)}) collective-permute-start(bf16[512,128]{1,0:T(8,128)(2,1)S(1)} %get-tuple-element.41), channel_id=1, source_target_pairs={{0,4},{1,5},{2,6},{3,7},{4,8},{5,9},{6,10},{7,11},{8,12},{9,13},{1... | collective-permute-start | bytes 393224 | tf_op jit(solution)/shard_map/ppermute | solution.py:178
  133.8 8.1 %collective-permute-start.8 = (bf16[512,128]{1,0:T(8,128)(2,1)S(1)}, bf16[512,128]{1,0:T(8,128)(2,1)S(1)}, u32[]{:S(2)}, u32[]{:S(2)}) collective-permute-start(bf16[512,128]{1,0:T(8,128)(2,1)S(1)} %get-tuple-element.42), channel_id=1, source_target_pairs={{0,12},{1,13},{2,14},{3,15},{4,0},{5,1},{6,2},{7,3},{8,4},{9,5},{1... | collective-permute-start | bytes 393224 | tf_op jit(solution)/shard_map/ppermute | solution.py:178
  146.2 0.7 copy-start.6

commit v9 on v7

--- a/solution.py
+++ b/solution.py
@@ -123,7 +123,6 @@
         rank = lax.axis_index("exp")
         place = jnp.stack([lax.rem(rank, GROUP), lax.div(rank, GROUP)]).astype(jnp.int32)
         weights = split_weights(place, slot_in_grad, phi_full, groups, wide)
-        weights = [weights[0]] + [swap(weights[k], k) for k in range(1, GROUP)]
 
         row_top = jnp.max(logits, axis=1)
         row_exp = jnp.exp(logits - row_top[:, None])
@@ -141,6 +140,8 @@
         spread = jnp.broadcast_to(col_stats[None], (n_seq,) + col_stats.shape)
         spread, row_got, weights = lax.optimization_barrier((spread, row_got, weights))
         col_got = lax.all_to_all(spread, "seq", 0, 0, tiled=True)
+        weights = [weights[0]] + [swap(weights[k], k) for k in range(GROUP - 1, 0, -1)][::-1]
+        col_got, weights = lax.optimization_barrier((col_got, weights))
         row_peak, row_total, row_dot = merge_stats(row_got)
         col_peak, col_total, col_dot = merge_stats(col_got[:, :, :slots])
 

time: 146 us -> 151 us (1.034)
  starting transfers between devices: 71.6 us -> 79.2 us
  waiting for transfers between devices: 54.6 us -> 47.3 us
  local copies, waits for them, and re-layouts: 6.77 us -> 11.1 us
    all_to_all x1, waiting for transfers between devices: 16.4 us -> 1.37 us  [per_device(): col_got = lax.all_to_all(spread, 'seq', 0, 0, tiled=True)]
    all_to_all x1, starting transfers between devices: 4.46 us -> 14.7 us  [per_device(): lax.all_to_all(both.reshape(n_seq, -1, 2 * slots), 'seq', 0, 0, tiled=True)]
    all_to_all x1, waiting for transfers between devices: 0.01 us -> 8.03 us  [gather_blocks(): return lax.all_to_all(spread, axis, 0, 0, tiled=True)]
    ppermute x3, starting transfers between devices: 13.7 us -> 11.4 us  [per_device(): token_sum = token_sum + lax.ppermute(blocks[i], 'exp', turn).astype(F32)]
    ppermute x3, waiting for transfers between devices: 3.72 us -> 6.01 us  [per_device(): token_sum = token_sum + lax.ppermute(blocks[i], 'exp', turn).astype(F32)]
    ppermute x6, waiting for transfers between devices: 8.69 us -> 6.72 us  [swap(): return lax.ppermute(x, 'exp', [(j, j ^ k) for j in range(n_exp)])]
  transfers between devices with their start and end apart: 13 -> 13, of which waited for: 8 -> 8; matrix products, arithmetic and copies ran while one was open for 3% -> 5% of each run, Pallas kernels for 1% -> 1%
where the time goes in v9:
time: 151 us; the launch traced here: 150 us
  starting transfers between devices  79.2 us (52%)
  waiting for transfers between devices  47.3 us (31%)
  local copies, waits for them, and re-layouts  11.1 us (7%)
  matrix products  5.1 us (3%)
  Pallas kernels  3.46 us (2%)
  other arithmetic  3.06 us (2%)
    all_to_all x1, starting transfers between devices, per_device(): got_phi = lax.all_to_all(packed_copies(phi, n_seq), 'seq', 0, 0, tiled=True)  23.3 us
    all_to_all x1, waiting for transfers between devices, per_device(): got_phi = lax.all_to_all(packed_copies(phi, n_seq), 'seq', 0, 0, tiled=True)  22.1 us
    ppermute x6, starting transfers between devices, swap(): return lax.ppermute(x, 'exp', [(j, j ^ k) for j in range(n_exp)])  16.7 us
    all_to_all x1, starting transfers between devices, per_device(): lax.all_to_all(both.reshape(n_seq, -1, 2 * slots), 'seq', 0, 0, tiled=True)  14.7 us
    ppermute x3, starting transfers between devices, per_device(): token_sum = token_sum + lax.ppermute(blocks[i], 'exp', turn).astype(F32)  11.4 us
    all_to_all x1, waiting for transfers between devices, gather_blocks(): return lax.all_to_all(spread, axis, 0, 0, tiled=True)  8.03 us
    all_to_all x1, starting transfers between devices, gather_blocks(): return lax.all_to_all(spread, axis, 0, 0, tiled=True)  7 us
    ppermute x6, waiting for transfers between devices, swap(): return lax.ppermute(x, 'exp', [(j, j ^ k) for j in range(n_exp)])  6.72 us
  transfers between devices with their start and end apart: 13, of which 8 were waited for; matrix products, arithmetic and copies ran while one was open for 5% of the time, Pallas kernels for 1%

profile of v9, /device:TPU:1, one launch (start us, length us, event | category | flops | bytes accessed | tf_op | source)
XLA Modules:
  0.0 150.2 jit_solution(3713444963543087394)
XLA Ops:
  0.6 0.0 copy-start
  0.6 1.6 %shard_map.76 = bf16[64,16,128]{2,1,0:T(8,128)(2,1)} custom-call(bf16[32,64]{1,0:T(8,128)(2,1)} %block_ref.1), custom_call_target="tpu_custom_call" | custom-call | bytes 266240 | tf_op jit(solution)/shard_map/pallas_call | solution.py:35
  2.3 23.3 %all-to-all-start = ((bf16[64,16,128]{2,1,0:T(8,128)(2,1)}), bf16[64,16,128]{2,1,0:T(8,128)(2,1)S(1)}, u32[]{:S(2)}, u32[]{:S(2)}) async-start(bf16[64,16,128]{2,1,0:T(8,128)(2,1)} %shard_map.76), calls=%async_computation | async-start | bytes 524288 | tf_op jit(solution)/shard_map/all_to_all | solution.py:111
  25.6 0.0 copy-done
  25.6 1.7 %fusion.18 = f32[512,64]{0,1:T(8,128)S(1)} fusion(bf16[512,2048]{1,0:T(8,128)(2,1)S(1)} %copy-done, bf16[64,2048]{1,0:T(8,128)(2,1)} %sig_ref.1), kind=kOutput, calls=%fused_computation.49 | convolution fusion | flops 134217728 | bytes 2490368 | tf_op jit(solution)/shard_map/dot_general | solution.py:116
  27.3 22.1 %all-to-all-done = bf16[64,16,128]{2,1,0:T(8,128)(2,1)S(1)} async-done(((bf16[64,16,128]{2,1,0:T(8,128)(2,1)}), bf16[64,16,128]{2,1,0:T(8,128)(2,1)S(1)}, u32[]{:S(2)}, u32[]{:S(2)}) %all-to-all-start) | async-done | bytes 262176 | tf_op jit(solution)/shard_map/all_to_all | solution.py:111
  49.4 0.1 fusion.17
  49.5 0.0 copy-start.2
  49.5 0.0 copy-start.6
  49.5 0.1 pad_maximum_fusion
  49.7 0.9 fusion.16
  50.5 0.0 copy-start.1
  50.5 0.2 fusion.7
  50.7 0.0 copy-done.5
  50.7 0.4 copy-done.2
  51.1 0.0 copy-done.6
  51.1 1.5 %fusion.4 = (f32[512]{0:T(512)S(1)}, f32[64]{0:T(128)S(1)}, f32[512,64]{0,1:T(8,128)}) fusion(f32[64,512]{1,0:T(8,128)S(1)} %get-tuple-element.61, f32[512]{0:T(512)S(1)} %get-tuple-element.51, f32[512,64]{0,1:T(8,128)S(1)} %fusion.18, f32[64]{0:T(128)S(1)} %get-tuple-element.52, bf16[512,2048]{1,0:T(8,128)(2,1)S(1)} %copy-done.2, ...), kind=kOutput, calls=%fused_computation.18 | convolution fusion | flops 134413760 | bytes 2757120 | tf_op jit(solution)/shard_map/dot_general | solution.py:119
  52.7 0.7 broadcast_in_dim.5
  53.3 7.0 %all-to-all-start.1 = ((f32[16,3,512]{2,1,0:T(4,128)}), f32[16,3,512]{2,1,0:T(4,128)}, u32[]{:S(2)}, u32[]{:S(2)}) async-start(f32[16,3,512]{2,1,0:T(4,128)} %broadcast_in_dim.5), calls=%async_computation.1 | async-start | bytes 262144 | tf_op jit(solution)/shard_map/all_to_all | solution.py:15
  60.3 0.0 copy-done.4
  60.4 0.1 pad_add_fusion.place_ref
  60.4 1.1 shard_map.77
  61.6 8.0 %all-to-all-done.1 = f32[16,3,512]{2,1,0:T(4,128)} async-done(((f32[16,3,512]{2,1,0:T(4,128)}), f32[16,3,512]{2,1,0:T(4,128)}, u32[]{:S(2)}, u32[]{:S(2)}) %all-to-all-start.1) | async-done | bytes 98336 | tf_op jit(solution)/shard_map/all_to_all | solution.py:15
  69.6 0.7 broadcast_in_dim.4
  70.3 6.2 %all-to-all-start.2 = ((f32[64,3,128]{2,1,0:T(4,128)}), f32[64,3,128]{2,1,0:T(4,128)}, u32[]{:S(2)}, u32[]{:S(2)}) async-start(f32[64,3,128]{2,1,0:T(4,128)} %broadcast_in_dim.4), calls=%async_computation.2 | async-start | bytes 262144 | tf_op jit(solution)/shard_map/all_to_all | solution.py:142
  76.5 1.0 copy.48
  77.5 1.0 copy.40
  78.5 1.7 %copy.47 = f32[512,64]{1,0:T(8,128)} copy(f32[512,64]{0,1:T(8,128)} %get-tuple-element.62) | data formatting | bytes 262144 | tf_op jit(solution)/shard_map/dot_general | solution.py:119
  80.3 0.9 copy.43
  81.2 2.2 %collective-permute-start = (bf16[128,512]{1,0:T(8,128)(2,1)S(1)}, bf16[128,512]{1,0:T(8,128)(2,1)S(1)}, u32[]{:S(2)}, u32[]{:S(2)}) collective-permute-start(bf16[128,512]{1,0:T(8,128)(2,1)S(1)} %get-tuple-element.31), channel_id=1, source_target_pairs={{0,1},{1,0},{2,3},{3,2},{4,5},{5,4},{6,7},{7,6},{8,9},{9,8},{10,11... | collective-permute-start | bytes 393224 | tf_op jit(solution)/shard_map/ppermute | solution.py:105
  83.4 2.0 %collective-permute-start.1 = (bf16[128,512]{1,0:T(8,128)(2,1)S(1)}, bf16[128,512]{1,0:T(8,128)(2,1)S(1)}, u32[]{:S(2)}, u32[]{:S(2)}) collective-permute-start(bf16[128,512]{1,0:T(8,128)(2,1)S(1)} %get-tuple-element.32), channel_id=1, source_target_pairs={{0,2},{1,3},{2,0},{3,1},{4,6},{5,7},{6,4},{7,5},{8,10},{9,11},{10,... | collective-permute-start | bytes 393224 | tf_op jit(solution)/shard_map/ppermute | solution.py:105
  85.4 4.2 %collective-permute-start.2 = (bf16[128,512]{1,0:T(8,128)(2,1)S(1)}, bf16[128,512]{1,0:T(8,128)(2,1)S(1)}, u32[]{:S(2)}, u32[]{:S(2)}) collective-permute-start(bf16[128,512]{1,0:T(8,128)(2,1)S(1)} %get-tuple-element.33), channel_id=1, source_target_pairs={{0,3},{1,2},{2,1},{3,0},{4,7},{5,6},{6,5},{7,4},{8,11},{9,10},{10,... | collective-permute-start | bytes 393224 | tf_op jit(solution)/shard_map/ppermute | solution.py:105
  89.6 0.9 slice.41
  90.6 0.0 collective-permute-done.refs_5_
  90.6 0.0 collective-permute-done.1.refs_6_
  90.6 3.1 %collective-permute-done.2.refs_7_ = bf16[128,512]{1,0:T(8,128)(2,1)S(1)} collective-permute-done((bf16[128,512]{1,0:T(8,128)(2,1)S(1)}, bf16[128,512]{1,0:T(8,128)(2,1)S(1)}, u32[]{:S(2)}, u32[]{:S(2)}) %collective-permute-start.2) | collective-permute-done | bytes 131104 | tf_op jit(solution)/shard_map/ppermute | solution.py:105
  93.7 1.4 all-to-all-done.2
  95.1 0.9 copy.39
  96.0 0.9 slice.42
  97.0 0.2 bitcast_convert_fusion
  97.2 1.3 fusion.3
  98.6 0.1 pad_maximum_fusion.2.refs_0_
  98.7 0.5 fusion
  99.2 0.0 copy-done.3
  99.2 0.5 fusion.1
  99.8 1.0 copy.49
  100.8 14.7 %all-to-all-start.3 = ((bf16[64,32,128]{2,1,0:T(8,128)(2,1)}), bf16[64,32,128]{2,1,0:T(8,128)(2,1)S(1)}, u32[]{:S(2)}, u32[]{:S(2)}) async-start(bf16[64,32,128]{2,1,0:T(8,128)(2,1)} %bitcast.82), calls=%async_computation.3 | async-start | bytes 1048576 | tf_op jit(solution)/shard_map/all_to_all | solution.py:166
  115.5 2.2 %collective-permute-start.3 = (bf16[512,128]{1,0:T(8,128)(2,1)S(1)}, bf16[512,128]{1,0:T(8,128)(2,1)S(1)}, u32[]{:S(2)}, u32[]{:S(2)}) collective-permute-start(bf16[512,128]{1,0:T(8,128)(2,1)S(1)} %pad_maximum_fusion.2.refs_0_), channel_id=1, source_target_pairs={{0,1},{1,0},{2,3},{3,2},{4,5},{5,4},{6,7},{7,6},{8,9},{9,8},{10,11... | collective-permute-start | bytes 393224 | tf_op jit(solution)/shard_map/ppermute | solution.py:105
  117.7 2.8 %collective-permute-start.4 = (bf16[512,128]{1,0:T(8,128)(2,1)S(1)}, bf16[512,128]{1,0:T(8,128)(2,1)S(1)}, u32[]{:S(2)}, u32[]{:S(2)}) collective-permute-start(bf16[512,128]{1,0:T(8,128)(2,1)S(1)} %pad_maximum_fusion.2.refs_0_), channel_id=1, source_target_pairs={{0,2},{1,3},{2,0},{3,1},{4,6},{5,7},{6,4},{7,5},{8,10},{9,11},{10,... | collective-permute-start | bytes 393224 | tf_op jit(solution)/shard_map/ppermute | solution.py:105
  120.5 3.3 %collective-permute-start.5 = (bf16[512,128]{1,0:T(8,128)(2,1)S(1)}, bf16[512,128]{1,0:T(8,128)(2,1)S(1)}, u32[]{:S(2)}, u32[]{:S(2)}) collective-permute-start(bf16[512,128]{1,0:T(8,128)(2,1)S(1)} %pad_maximum_fusion.2.refs_0_), channel_id=1, source_target_pairs={{0,3},{1,2},{2,1},{3,0},{4,7},{5,6},{6,5},{7,4},{8,11},{9,10},{10,... | collective-permute-start | bytes 393224 | tf_op jit(solution)/shard_map/ppermute | solution.py:105
  123.8 0.0 collective-permute-done.3.refs_1_
  123.9 0.0 collective-permute-done.4.refs_2_
  123.9 3.6 %collective-permute-done.5.refs_3_ = bf16[512,128]{1,0:T(8,128)(2,1)S(1)} collective-permute-done((bf16[512,128]{1,0:T(8,128)(2,1)S(1)}, bf16[512,128]{1,0:T(8,128)(2,1)S(1)}, u32[]{:S(2)}, u32[]{:S(2)}) %collective-permute-start.5) | collective-permute-done | bytes 131104 | tf_op jit(solution)/shard_map/ppermute | solution.py:105
  127.5 0.7 shard_map.78
  128.2 4.0 %collective-permute-start.6 = (bf16[512,128]{1,0:T(8,128)(2,1)S(1)}, bf16[512,128]{1,0:T(8,128)(2,1)S(1)}, u32[]{:S(2)}, u32[]{:S(2)}) collective-permute-start(bf16[512,128]{1,0:T(8,128)(2,1)S(1)} %get-tuple-element.42), channel_id=1, source_target_pairs={{0,8},{1,9},{2,10},{3,11},{4,12},{5,13},{6,14},{7,15},{8,0},{9,1},... | collective-permute-start | bytes 393224 | tf_op jit(solution)/shard_map/ppermute | solution.py:172
  132.2 2.7 %collective-permute-start.7 = (bf16[512,128]{1,0:T(8,128)(2,1)S(1)}, bf16[512,128]{1,0:T(8,128)(2,1)S(1)}, u32[]{:S(2)}, u32[]{:S(2)}) collective-permute-start(bf16[512,128]{1,0:T(8,128)(2,1)S(1)} %get-tuple-element.43), channel_id=1, source_target_pairs={{0,4},{1,5},{2,6},{3,7},{4,8},{5,9},{6,10},{7,11},{8,12},{9,13},{1... | collective-permute-start | bytes 393224 | tf_op jit(solution)/shard_map/ppermute | solution.py:172
  134.9 4.6 %collective-permute-start.8 = (bf16[512,128]{1,0:T(8,128)(2,1)S(1)}, bf16[512,128]{1,0:T(8,128)(2,1)S(1)}, u32[]{:S(2)}, u32[]{:S(2)}) collective-permute-start(bf16[512,128]{1,0:T(8,128)(2,1)S(1)} %get-tuple-element.44), channel_id=1, source_target_pairs={{0,12},{1,13},{2,14},{3,15},{4,0},{5,1},{6,2},{7,3},{8,4},{9,5},{1... | collective-permute-start | bytes 393224 | tf_op jit(solution)/shard_map/ppermute | solution.py:172
  139.6 0.0 collective-permute-done.6
  139.6 4.4 %collective-permute-done.7 = bf16[512,128]{1,0:T(8,128)(2,1)S(1)} collective-permute-done((bf16[512,128]{1,0:T(8,128)(2,1)S(1)}, bf16[512,128]{1,0:T(8,128)(2,1)S(1)}, u32[]{:S(2)}, u32[]{:S(2)}) %collective-permute-start.7) | collective-permute-done | bytes 131104 | tf_op jit(solution)/shard_map/ppermute | solution.py:172
  144.0 1.6 %collective-permute-done.8 = bf16[512,128]{1,0:T(8,128)(2,1)S(1)} collective-permute-done((bf16[512,128]{1,0:T(8,128)(2,1)S(1)}, bf16[512,128]{1,0:T(8,128)(2,1)S(1)}, u32[]{:S(2)}, u32[]{:S(2)}) %collective-permute-start.8) | collective-permute-done | bytes 131104 | tf_op jit(solution)/shard_map/ppermute | solution.py:172
  145.6 0.7 add_convert_fusion
  146.3 3.1 %all-to-all-done.3 = bf16[64,32,128]{2,1,0:T(8,128)(2,1)S(1)} async-done(((bf16[64,32,128]{2,1,0:T(8,128)(2,1)}), bf16[64,32,128]{2,1,0:T(8,128)(2,1)S(1)}, u32[]{:S(2)}, u32[]{:S(2)}) %all-to-all-start.3) | async-done | bytes 524320 | tf_op jit(solution)/shard_map/all_to_all | solution.py:166
  149.4 0.1 convert_reduce_fusion
  149.6 0.7 fusion.15
  (15 shorter events, 0.2 us)
Async XLA Ops:
  0.6 24.9 %copy-start = (bf16[512,2048]{1,0:T(8,128)(2,1)S(1)}, bf16[512,2048]{1,0:T(8,128)(2,1)}, u32[]{:S(2)}) copy-start(bf16[512,2048]{1,0:T(8,128)(2,1)} %param.5) | copy-start | bytes 6291460
  2.3 47.1 %all-to-all-start = ((bf16[64,16,128]{2,1,0:T(8,128)(2,1)}), bf16[64,16,128]{2,1,0:T(8,128)(2,1)S(1)}, u32[]{:S(2)}, u32[]{:S(2)}) async-start(bf16[64,16,128]{2,1,0:T(8,128)(2,1)} %shard_map.76), calls=%async_computation | async-start | bytes 524288 | tf_op jit(solution)/shard_map/all_to_all | solution.py:111
  27.3 23.4 %copy-start.5 = (f32[512,64]{0,1:T(8,128)}, f32[512,64]{0,1:T(8,128)S(1)}, u32[]{:S(2)}) copy-start(f32[512,64]{0,1:T(8,128)S(1)} %fusion.18) | copy-start | bytes 393220
  49.5 1.6 %copy-start.2 = (bf16[512,2048]{1,0:T(8,128)(2,1)S(1)}, bf16[512,2048]{1,0:T(8,128)(2,1)}, u32[]{:S(2)}) copy-start(bf16[512,2048]{1,0:T(8,128)(2,1)} %param.9) | copy-start | bytes 6291460
  49.5 1.6 %copy-start.6 = (bf16[64,2048]{1,0:T(8,128)(2,1)S(1)}, bf16[64,2048]{1,0:T(8,128)(2,1)}, u32[]{:S(2)}) copy-start(bf16[64,2048]{1,0:T(8,128)(2,1)} %param.7) | copy-start | bytes 786436
  50.5 9.8 %copy-start.4 = (f32[64,512]{1,0:T(8,128)}, f32[64,512]{1,0:T(8,128)S(1)}, u32[]{:S(2)}) copy-start(f32[64,512]{1,0:T(8,128)S(1)} %get-tuple-element.61) | copy-start | bytes 393220
  50.5 9.9 %copy-start.1 = (bf16[64,2048]{1,0:T(8,128)(2,1)S(1)}, bf16[64,2048]{1,0:T(8,128)(2,1)}, u32[]{:S(2)}) copy-start(bf16[64,2048]{1,0:T(8,128)(2,1)} %sig_ref.1) | copy-start | bytes 786436
  53.3 16.3 %all-to-all-start.1 = ((f32[16,3,512]{2,1,0:T(4,128)}), f32[16,3,512]{2,1,0:T(4,128)}, u32[]{:S(2)}, u32[]{:S(2)}) async-start(f32[16,3,512]{2,1,0:T(4,128)} %broadcast_in_dim.5), calls=%async_computation.1 | async-start | bytes 262144 | tf_op jit(solution)/shard_map/all_to_all | solution.py:15
  70.3 24.8 %all-to-all-start.2 = ((f32[64,3,128]{2,1,0:T(4,128)}), f32[64,3,128]{2,1,0:T(4,128)}, u32[]{:S(2)}, u32[]{:S(2)}) async-start(f32[64,3,128]{2,1,0:T(4,128)} %broadcast_in_dim.4), calls=%async_computation.2 | async-start | bytes 262144 | tf_op jit(solution)/shard_map/all_to_all | solution.py:142
  81.2 9.4 %collective-permute-start = (bf16[128,512]{1,0:T(8,128)(2,1)S(1)}, bf16[128,512]{1,0:T(8,128)(2,1)S(1)}, u32[]{:S(2)}, u32[]{:S(2)}) collective-permute-start(bf16[128,512]{1,0:T(8,128)(2,1)S(1)} %get-tuple-element.31), channel_id=1, source_target_pairs={{0,1},{1,0},{2,3},{3,2},{4,5},{5,4},{6,7},{7,6},{8,9},{9,8},{10,11... | collective-permute-start | bytes 393224 | tf_op jit(solution)/shard_map/ppermute | solution.py:105
  83.4 7.2 %collective-permute-start.1 = (bf16[128,512]{1,0:T(8,128)(2,1)S(1)}, bf16[128,512]{1,0:T(8,128)(2,1)S(1)}, u32[]{:S(2)}, u32[]{:S(2)}) collective-permute-start(bf16[128,512]{1,0:T(8,128)(2,1)S(1)} %get-tuple-element.32), channel_id=1, source_target_pairs={{0,2},{1,3},{2,0},{3,1},{4,6},{5,7},{6,4},{7,5},{8,10},{9,11},{10,... | collective-permute-start | bytes 393224 | tf_op jit(solution)/shard_map/ppermute | solution.py:105
  85.4 8.3 %collective-permute-start.2 = (bf16[128,512]{1,0:T(8,128)(2,1)S(1)}, bf16[128,512]{1,0:T(8,128)(2,1)S(1)}, u32[]{:S(2)}, u32[]{:S(2)}) collective-permute-start(bf16[128,512]{1,0:T(8,128)(2,1)S(1)} %get-tuple-element.33), channel_id=1, source_target_pairs={{0,3},{1,2},{2,1},{3,0},{4,7},{5,6},{6,5},{7,4},{8,11},{9,10},{10,... | collective-permute-start | bytes 393224 | tf_op jit(solution)/shard_map/ppermute | solution.py:105
  97.0 2.2 %copy-start.3 = (bf16[512,2048]{1,0:T(8,128)(2,1)S(1)}, bf16[512,2048]{1,0:T(8,128)(2,1)}, u32[]{:S(2)}) copy-start(bf16[512,2048]{1,0:T(8,128)(2,1)} %param.9) | copy-start | bytes 6291460
  100.8 48.7 %all-to-all-start.3 = ((bf16[64,32,128]{2,1,0:T(8,128)(2,1)}), bf16[64,32,128]{2,1,0:T(8,128)(2,1)S(1)}, u32[]{:S(2)}, u32[]{:S(2)}) async-start(bf16[64,32,128]{2,1,0:T(8,128)(2,1)} %bitcast.82), calls=%async_computation.3 | async-start | bytes 1048576 | tf_op jit(solution)/shard_map/all_to_all | solution.py:166
  115.5 8.4 %collective-permute-start.3 = (bf16[512,128]{1,0:T(8,128)(2,1)S(1)}, bf16[512,128]{1,0:T(8,128)(2,1)S(1)}, u32[]{:S(2)}, u32[]{:S(2)}) collective-permute-start(bf16[512,128]{1,0:T(8,128)(2,1)S(1)} %pad_maximum_fusion.2.refs_0_), channel_id=1, source_target_pairs={{0,1},{1,0},{2,3},{3,2},{4,5},{5,4},{6,7},{7,6},{8,9},{9,8},{10,11... | collective-permute-start | bytes 393224 | tf_op jit(solution)/shard_map/ppermute | solution.py:105
  117.7 6.2 %collective-permute-start.4 = (bf16[512,128]{1,0:T(8,128)(2,1)S(1)}, bf16[512,128]{1,0:T(8,128)(2,1)S(1)}, u32[]{:S(2)}, u32[]{:S(2)}) collective-permute-start(bf16[512,128]{1,0:T(8,128)(2,1)S(1)} %pad_maximum_fusion.2.refs_0_), channel_id=1, source_target_pairs={{0,2},{1,3},{2,0},{3,1},{4,6},{5,7},{6,4},{7,5},{8,10},{9,11},{10,... | collective-permute-start | bytes 393224 | tf_op jit(solution)/shard_map/ppermute | solution.py:105
  120.5 7.0 %collective-permute-start.5 = (bf16[512,128]{1,0:T(8,128)(2,1)S(1)}, bf16[512,128]{1,0:T(8,128)(2,1)S(1)}, u32[]{:S(2)}, u32[]{:S(2)}) collective-permute-start(bf16[512,128]{1,0:T(8,128)(2,1)S(1)} %pad_maximum_fusion.2.refs_0_), channel_id=1, source_target_pairs={{0,3},{1,2},{2,1},{3,0},{4,7},{5,6},{6,5},{7,4},{8,11},{9,10},{10,... | collective-permute-start | bytes 393224 | tf_op jit(solution)/shard_map/ppermute | solution.py:105
  128.2 11.4 %collective-permute-start.6 = (bf16[512,128]{1,0:T(8,128)(2,1)S(1)}, bf16[512,128]{1,0:T(8,128)(2,1)S(1)}, u32[]{:S(2)}, u32[]{:S(2)}) collective-permute-start(bf16[512,128]{1,0:T(8,128)(2,1)S(1)} %get-tuple-element.42), channel_id=1, source_target_pairs={{0,8},{1,9},{2,10},{3,11},{4,12},{5,13},{6,14},{7,15},{8,0},{9,1},... | collective-permute-start | bytes 393224 | tf_op jit(solution)/shard_map/ppermute | solution.py:172
  132.2 11.8 %collective-permute-start.7 = (bf16[512,128]{1,0:T(8,128)(2,1)S(1)}, bf16[512,128]{1,0:T(8,128)(2,1)S(1)}, u32[]{:S(2)}, u32[]{:S(2)}) collective-permute-start(bf16[512,128]{1,0:T(8,128)(2,1)S(1)} %get-tuple-element.43), channel_id=1, source_target_pairs={{0,4},{1,5},{2,6},{3,7},{4,8},{5,9},{6,10},{7,11},{8,12},{9,13},{1... | collective-permute-start | bytes 393224 | tf_op jit(solution)/shard_map/ppermute | solution.py:172
  134.9 10.7 %collective-permute-start.8 = (bf16[512,128]{1,0:T(8,128)(2,1)S(1)}, bf16[512,128]{1,0:T(8,128)(2,1)S(1)}, u32[]{:S(2)}, u32[]{:S(2)}) collective-permute-start(bf16[512,128]{1,0:T(8,128)(2,1)S(1)} %get-tuple-element.44), channel_id=1, source_target_pairs={{0,12},{1,13},{2,14},{3,15},{4,0},{5,1},{6,2},{7,3},{8,4},{9,5},{1... | collective-permute-start | bytes 393224 | tf_op jit(solution)/shard_map/ppermute | solution.py:172
  149.6 0.7 copy-start.7
